TPU v7x, 32 devices: a whole 2x2x4 slice. The times are simulated.
32 devices in a mesh: row: 4 (over y, core), col: 8 (over z, x).
Axes of the slice: x: 2, y: 2, z: 4, core: 2. Of those that a mesh axis runs over, the one named last changes fastest.
Arguments:
- params: float32 [64, 8192], replicated, may hold values from -6 to 6
- momentum: float32 [4, 8, 64, 8192], P('row', 'col'), may hold values from -6 to 6
- gradient: float32 [4, 8, 64, 8192], P('row', 'col'), may hold values from -6 to 6
- chosen_rows: int32 [4, 8, 128, 4], P('row', 'col'), may hold values from 0 to 63, as said below
- live_counts: int32 [4, 8, 128], P('row', 'col'), may hold values from 1 to 4, as said below
- common_rows: int32 [8, 128, 8], P('col'), may hold values from 0 to 63, as said below
Outputs:
- new_params: float32 [64, 8192], replicated
- new_momentum: float32 [4, 8, 64, 8192], P('row', 'col')
Inputs may be any that keep to these rules, and one draw needn't show every extreme that they name: `chosen_rows`: within one replica's block the 4 entries are distinct; entries at positions at or past the block's live count are ignored. `live_counts`: every replica has 4 live rows in some block. `common_rows`: within one group's block the 8 entries are distinct.
All inputs are finite; a program needn't handle non-finite values.
Results may differ from a plain program's by a relative error of at most 0.0003.
Values sent between devices are 32-bit elements; how exact they have to be, the bound alone decides.
No kernel may reach another device: no remote copies, remote signals or barrier semaphores. Data moves between devices by JAX's collectives and lax.ppermute only.
A program may use at most 128 MiB of HBM per device.

v0:
```python
import functools
import math

import jax
import jax.numpy as jnp
import ml_dtypes
import numpy as np
from jax import lax
from jax.experimental import pallas as pl
from jax.experimental.pallas import tpu as pltpu
from jax.sharding import PartitionSpec as P

decay_rate = 0.9
step_size = 0.1
LANES = 128
SUB = 8
CORES = 2
EVERY = ("row", "col")
VMEM_BYTES = 48 * 1024 * 1024


def dct_table(order):
    freq = np.arange(order, dtype=np.float64)[:, None]
    place = np.arange(order, dtype=np.float64)[None, :]
    matrix = math.sqrt(2.0 / order) * np.cos(math.pi * (2.0 * place + 1.0) * freq / (2.0 * order))
    return np.where(freq == 0.0, matrix * math.sqrt(0.5), matrix)


def split_table(matrix):
    high = matrix.astype(ml_dtypes.bfloat16)
    low = (matrix - high.astype(np.float64)).astype(ml_dtypes.bfloat16)
    return np.concatenate([high, low, high], axis=1)


def product(table, field):
    high = field.astype(jnp.bfloat16)
    low = (field - high.astype(jnp.float32)).astype(jnp.bfloat16)
    stacked = jnp.concatenate([high, high, low], axis=0)
    return jnp.dot(table, stacked, preferred_element_type=jnp.float32)


def lane_blocks(order, first):
    return first + lax.broadcasted_iota(jnp.int32, (SUB, LANES), 1) // order


def pick_kernel(width, table_ref, chosen_ref, counts_ref, common_ref, m_ref, g_ref, out_ref):
    order = m_ref.shape[-2]
    chosen = chosen_ref[...]
    common = common_ref[...]
    slot = lax.broadcasted_iota(jnp.int32, chosen.shape, 0)
    inside = chosen == common[0:1]
    for q in range(1, common.shape[0]):
        inside = inside | (chosen == common[q : q + 1])
    rows = jnp.where(inside & (slot < counts_ref[...]), chosen, -1)
    rows = jnp.concatenate([rows, rows], axis=0)
    slots = chosen.shape[0]
    spectrum = product(table_ref[...], decay_rate * m_ref[0, 0] + g_ref[0, 0])
    step_blocks = m_ref.shape[-1] // order
    first = lax.rem(pl.program_id(0) * step_blocks, LANES)
    values_part = lax.broadcasted_iota(jnp.int32, (SUB, LANES), 0) < slots
    for t in range(m_ref.shape[-1] // LANES):
        lanes = lane_blocks(order, first + t * (LANES // order))
        row = jnp.take_along_axis(rows, lanes, axis=1)
        tile, within = row >> 3, row & 7
        picked = jnp.zeros((SUB, LANES), jnp.float32)
        for r in range(order // SUB):
            here = spectrum[r * SUB : (r + 1) * SUB, t * LANES : (t + 1) * LANES]
            picked = jnp.where(tile == r, jnp.take_along_axis(here, within, axis=0), picked)
        column = t * LANES
        out_ref[column // width, :, column % width : column % width + LANES] = jnp.where(
            values_part, picked, row.astype(jnp.float32)
        )


def rest_kernel(table_ref, back_ref, chosen_ref, counts_ref, m_ref, g_ref, out_ref):
    order, columns = m_ref.shape[-2:]
    chosen = chosen_ref[...]
    slot = lax.broadcasted_iota(jnp.int32, chosen.shape, 0)
    bits = jnp.where(slot < counts_ref[...], jnp.int32(1) << (chosen & 31), 0)
    words = []
    for half in range(order // 32):
        mine = jnp.where((chosen >> 5) == half, bits, 0)
        word = mine[0:1]
        for s in range(1, chosen.shape[0]):
            word = word | mine[s : s + 1]
        words.append(jnp.broadcast_to(word, (SUB, LANES)))
    decayed = decay_rate * m_ref[0, 0] + g_ref[0, 0]
    spectrum = product(table_ref[...], decayed)
    first = lax.rem(pl.program_id(0) * (columns // order), LANES)
    sub = lax.broadcasted_iota(jnp.int32, (SUB, LANES), 0)
    parts = []
    for t in range(columns // LANES):
        lanes = lane_blocks(order, first + t * (LANES // order))
        wide = [jnp.take_along_axis(word, lanes, axis=1) for word in words]
        tiles = []
        for r in range(order // SUB):
            here = spectrum[r * SUB : (r + 1) * SUB, t * LANES : (t + 1) * LANES]
            bit = jnp.int32(1) << (sub + (r * SUB) % 32)
            tiles.append(jnp.where((wide[r * SUB // 32] & bit) != 0, here, 0.0))
        parts.append(jnp.concatenate(tiles, axis=0))
    sent = jnp.concatenate(parts, axis=1)
    out_ref[0, 0] = decayed - product(back_ref[...], sent)


def sum_kernel(back_ref, got_ref, params_ref, out_ref, held, arrived):
    order, width = out_ref.shape
    me = lax.axis_index("row") * lax.axis_size("col") + lax.axis_index("col")
    copy = pltpu.make_async_copy(
        params_ref.at[:, pl.ds(pl.multiple_of(me * width, LANES), width)], held, arrived
    )
    copy.start()
    slots = got_ref.shape[1] // 2
    tiles = order // SUB
    sub = lax.broadcasted_iota(jnp.int32, (SUB, LANES), 0).astype(jnp.float32)

    def add(n, totals):
        totals = list(totals)
        for t in range(width // LANES):
            got = got_ref[n, :, t * LANES : (t + 1) * LANES]
            for s in range(slots):
                value = jnp.broadcast_to(got[s : s + 1], (SUB, LANES))
                row = jnp.broadcast_to(got[slots + s : slots + s + 1], (SUB, LANES)) - sub
                for r in range(tiles):
                    k = t * tiles + r
                    totals[k] = totals[k] + jnp.where(row == r * SUB, value, 0.0)
        return tuple(totals)

    zero = jnp.zeros((SUB, LANES), jnp.float32)
    totals = lax.fori_loop(0, got_ref.shape[0], add, (zero,) * (tiles * (width // LANES)))
    total = jnp.concatenate(
        [
            jnp.concatenate(totals[t * tiles : (t + 1) * tiles], axis=0)
            for t in range(width // LANES)
        ],
        axis=1,
    )
    update = product(back_ref[...], total)
    copy.wait()
    out_ref[...] = held[...] - step_size * update


def place_kernel(places, sizes, *refs):
    *pieces, out_ref, sems = refs
    y_size, z_size, x_size = sizes
    row, col = lax.axis_index("row"), lax.axis_index("col")
    y, core, z, x = row // CORES, row % CORES, col // x_size, col % x_size
    copies = []
    for piece, (other, first, second) in zip(pieces, places, strict=True):
        owner = 1 - core if other else core
        dy = jnp.where(owner == 0, first, second)
        dx = jnp.where(owner == 0, second, first)
        width = piece.shape[-1]
        for j in range(z_size):
            place = ((y ^ dy) * CORES + owner) * (z_size * x_size) + (z ^ j) * x_size + (x ^ dx)
            copy = pltpu.make_async_copy(
                piece.at[j],
                out_ref.at[:, pl.ds(pl.multiple_of(place * width, LANES), width)],
                sems.at[len(copies)],
            )
            copy.start()
            copies.append(copy)
    for copy in copies:
        copy.wait()


def vmem():
    return pl.BlockSpec(memory_space=pltpu.VMEM)


def limits():
    return pltpu.CompilerParams(vmem_limit_bytes=VMEM_BYTES)


def list_spec(rows, step):
    return pl.BlockSpec((rows, LANES), lambda i: (0, i * step // LANES))


def pick(forward, momentum, gradient, chosen, counts, common, parts):
    order, columns = momentum.shape[-2:]
    width = columns // parts
    step = max(width, columns // 8)
    lists = functools.partial(list_spec, step=step // order)
    field = pl.BlockSpec((1, 1, order, step), lambda i: (0, 0, 0, i))
    slots = chosen.shape[0]
    return pl.pallas_call(
        functools.partial(pick_kernel, width),
        grid=(columns // step,),
        in_specs=[vmem(), lists(slots), lists(1), lists(common.shape[0]), field, field],
        out_specs=pl.BlockSpec((step // width, 2 * slots, width), lambda i: (i, 0, 0)),
        out_shape=jax.ShapeDtypeStruct((parts, 2 * slots, width), jnp.float32),
        compiler_params=limits(),
        name="pick_rows",
    )(forward, chosen, counts, common, momentum, gradient)


def rest(forward, back, momentum, gradient, chosen, counts):
    order, columns = momentum.shape[-2:]
    step = columns // 8
    lists = functools.partial(list_spec, step=step // order)
    field = pl.BlockSpec((1, 1, order, step), lambda i: (0, 0, 0, i))
    return pl.pallas_call(
        rest_kernel,
        grid=(columns // step,),
        in_specs=[vmem(), vmem(), lists(chosen.shape[0]), lists(1), field, field],
        out_specs=field,
        out_shape=jax.ShapeDtypeStruct(momentum.shape, jnp.float32),
        compiler_params=limits(),
        name="residual",
        cost_estimate=pl.CostEstimate(
            flops=12 * order * order * columns,
            bytes_accessed=3 * momentum.size * 4,
            transcendentals=0,
        ),
    )(forward, back, chosen, counts, momentum, gradient)


def add_up(back, got, params):
    width = got.shape[-1]
    order = params.shape[0]
    return pl.pallas_call(
        sum_kernel,
        in_specs=[vmem(), vmem(), pl.BlockSpec(memory_space=pl.ANY)],
        out_specs=vmem(),
        out_shape=jax.ShapeDtypeStruct((order, width), jnp.float32),
        scratch_shapes=[pltpu.VMEM((order, width), jnp.float32), pltpu.SemaphoreType.DMA],
        compiler_params=limits(),
        name="sum_and_update",
    )(back, got, params)


def spread(mine, sizes):
    y_size, z_size, x_size = sizes

    def swap(array, zero, one):
        pairs = []
        for y in range(y_size):
            for core in range(CORES):
                for z in range(z_size):
                    for x in range(x_size):
                        dy, dk, dz, dx = (zero, one)[core]
                        here = ((y * CORES + core) * z_size + z) * x_size + x
                        there = (((y ^ dy) * CORES + (core ^ dk)) * z_size + (z ^ dz)) * x_size + (
                            x ^ dx
                        )
                        pairs.append((here, there))
        return lax.ppermute(array, EVERY, pairs)

    line = [mine] + [swap(mine, (0, 0, j, 0), (0, 0, j, 0)) for j in range(1, z_size)]
    own = jnp.stack(line)
    pieces = [(own, 0, 0)]
    first = []
    for i in range(1, x_size):
        got = swap(own, (0, 0, 0, i), (i, 0, 0, 0))
        first.append((got, 0, i))
    pieces += first
    for j in range(1, y_size):
        pieces.append((swap(own, (j, 0, 0, 0), (0, 0, 0, j)), j, 0))
        for array, _, i in first:
            pieces.append((swap(array, (j, 0, 0, 0), (0, 0, 0, j)), j, i))
    other = [(swap(array, (0, 1, 0, 0), (0, 1, 0, 0)), dy, dx) for array, dy, dx in pieces]
    return [(array, 0, dy, dx) for array, dy, dx in pieces] + [
        (array, 1, dy, dx) for array, dy, dx in other
    ]


def place(pieces, sizes, params):
    arrays = [piece[0] for piece in pieces]
    places = [piece[1:] for piece in pieces]
    anywhere = pl.BlockSpec(memory_space=pl.ANY)
    return pl.pallas_call(
        functools.partial(place_kernel, places, sizes),
        in_specs=[anywhere] * len(arrays),
        out_specs=anywhere,
        out_shape=jax.ShapeDtypeStruct(params.shape, jnp.float32),
        scratch_shapes=[pltpu.SemaphoreType.DMA((len(arrays) * sizes[1],))],
        compiler_params=limits(),
        name="place_columns",
    )(*arrays)


def body(sizes, parts, params, momentum, gradient, chosen_rows, live_counts, common_rows):
    matrix = dct_table(params.shape[0])
    forward, back = jnp.asarray(split_table(matrix)), jnp.asarray(split_table(matrix.T))
    chosen = jnp.transpose(chosen_rows[0, 0])
    counts = live_counts[0]
    common = jnp.transpose(common_rows[0])
    sent = pick(forward, momentum, gradient, chosen, counts, common, parts)
    residual = rest(forward, back, momentum, gradient, chosen, counts)
    if sizes is not None:
        got = lax.all_to_all(sent, EVERY, 0, 0, tiled=True)
        mine = add_up(back, got, params)
        new_params = place(spread(mine, sizes), sizes, params)
    else:
        new_params = plain_update(back, sent, params)
    return new_params, residual


def plain_update(back, sent, params):
    order, columns = params.shape
    got = lax.all_to_all(sent, "col", 0, 0, tiled=True)
    got = lax.all_gather(got, "row", axis=0, tiled=True)
    slots = sent.shape[1] // 2
    row = got[:, slots:].astype(jnp.int32)
    table = row[:, :, None, :] == jnp.arange(order, dtype=jnp.int32)[:, None]
    total = jnp.sum(jnp.where(table, got[:, :slots, None, :], 0.0), axis=(0, 1))
    total = lax.all_gather(total, "col", axis=1, tiled=True)
    return params - step_size * product(back, total)


def solution(mesh):
    rows, cols = mesh.shape["row"], mesh.shape["col"]
    placed = (
        P(),
        P("row", "col", None, None),
        P("row", "col", None, None),
        P("row", "col", None, None),
        P("row", "col", None),
        P("col", None, None),
    )

    def step(params, *rest_of):
        columns = params.shape[1]
        side = rows // CORES
        depth = cols // max(side, 1)
        whole = rows == side * CORES and cols == side * depth
        powers = all(n > 0 and n & (n - 1) == 0 for n in (side, depth))
        shared = columns % (rows * cols * LANES) == 0
        sizes = (side, depth, side) if whole and powers and shared else None
        parts = cols if sizes is None else rows * cols
        return jax.shard_map(
            functools.partial(body, sizes, parts),
            mesh=mesh,
            in_specs=placed,
            out_specs=(P(), P("row", "col", None, None)),
            check_vma=False,
        )(params, *rest_of)

    return step
```

profile of v0, /device:TPU:0, one launch (start us, length us, event | category | flops | bytes accessed | tf_op | source)
XLA Modules:
  0.0 58.5 jit_solution(1137354855995114650)
XLA Ops:
  0.6 1.6 %copy-done = f32[1,1,64,8192]{3,2,1,0:T(8,128)S(1)} copy-done((f32[1,1,64,8192]{3,2,1,0:T(8,128)S(1)}, f32[1,1,64,8192]{3,2,1,0:T(8,128)}, u32[]{:S(2)}) %copy-start) | copy-done | bytes 2097176
  2.2 1.6 %copy-done.2 = f32[1,1,64,8192]{3,2,1,0:T(8,128)S(1)} copy-done((f32[1,1,64,8192]{3,2,1,0:T(8,128)S(1)}, f32[1,1,64,8192]{3,2,1,0:T(8,128)}, u32[]{:S(2)}) %copy-start.2) | copy-done | bytes 2097176
  3.8 0.8 %copy-done.5 = bf16[64,192]{1,0:T(8,128)(2,1)S(1)} copy-done((bf16[64,192]{1,0:T(8,128)(2,1)S(1)}, bf16[64,192]{1,0:T(8,128)(2,1)}, u32[]{:S(2)}) %copy-start.5) | copy-done | bytes 24600
  4.6 0.7 %copy-done.8 = s32[1,1,128,4]{2,3,1,0:T(4,128)S(1)} copy-done((s32[1,1,128,4]{2,3,1,0:T(4,128)S(1)}, s32[1,1,128,4]{2,3,1,0:T(4,128)}, u32[]{:S(2)}) %copy-start.8) | copy-done | bytes 2072
  5.3 0.7 %copy-done.9 = s32[1,128,8]{1,2,0:T(8,128)S(1)} copy-done((s32[1,128,8]{1,2,0:T(8,128)S(1)}, s32[1,128,8]{1,2,0:T(8,128)}, u32[]{:S(2)}) %copy-start.9) | copy-done | bytes 4120
  5.9 0.7 %copy-done.10 = s32[1,1,128]{2,1,0:T(1,128)S(1)} copy-done((s32[1,1,128]{2,1,0:T(1,128)S(1)}, s32[1,1,128]{2,1,0:T(1,128)}, u32[]{:S(2)}) %copy-start.10) | copy-done | bytes 536
  6.6 2.0 %pick_rows.1 = f32[32,8,256]{2,1,0:T(8,128)S(1)} custom-call(bf16[64,192]{1,0:T(8,128)(2,1)S(1)} %copy-done.5, s32[4,128]{1,0:T(4,128)S(1)} %bitcast.12, s32[1,128]{1,0:T(1,128)S(1)} %bitcast.15, s32[8,128]{1,0:T(8,128)S(1)} %bitcast.14, f32[1,1,64,8192]{3,2,1,0:T(8,128)S(1)} %copy-done, f32[1,1,64,8192]{3,2,1,0:T(8,128)S(1)} %copy-done.2), custom_call_target="tpu_custom_call" | custom-call | tf_op jit(solution)/shard_map/pick_rows/pallas_call | solution.py:185
  8.6 0.0 copy-start.1
  8.6 0.0 copy-start.6
  8.7 17.8 %all_to_all.5.got_ref = f32[32,8,256]{2,1,0:T(8,128)S(1)} all-to-all(f32[32,8,256]{2,1,0:T(8,128)S(1)} %pick_rows.1), channel_id=1, replica_groups=mesh['row'=4,'col'=8] {'row','col'}, dimensions={0} | all-to-all | bytes 524288 | tf_op jit(solution)/shard_map/all_to_all | solution.py:290
  26.4 1.2 %sum_and_update.1 = f32[64,256]{1,0:T(8,128)S(1)} custom-call(bf16[64,192]{1,0:T(8,128)(2,1)S(1)} %copy-done.7, f32[32,8,256]{2,1,0:T(8,128)S(1)} %all_to_all.5.got_ref, f32[64,8192]{1,0:T(8,128)S(1)} %copy-done.4), custom_call_target="tpu_custom_call" | custom-call | tf_op jit(solution)/shard_map/sum_and_update/pallas_call | solution.py:220
  27.6 1.2 %collective-permute-start.2 = (f32[64,256]{1,0:T(8,128)S(1)}, f32[64,256]{1,0:T(8,128)S(1)}, u32[]{:S(2)}, u32[]{:S(2)}) collective-permute-start(f32[64,256]{1,0:T(8,128)S(1)} %sum_and_update.1), channel_id=1, source_target_pairs={{0,6},{1,7},{2,4},{3,5},{4,2},{5,3},{6,0},{7,1},{8,14},{9,15},{10,... | collective-permute-start | bytes 196616 | tf_op jit(solution)/shard_map/ppermute | solution.py:246
  28.8 1.3 %collective-permute-start.1 = (f32[64,256]{1,0:T(8,128)S(1)}, f32[64,256]{1,0:T(8,128)S(1)}, u32[]{:S(2)}, u32[]{:S(2)}) collective-permute-start(f32[64,256]{1,0:T(8,128)S(1)} %sum_and_update.1), channel_id=1, source_target_pairs={{0,4},{1,5},{2,6},{3,7},{4,0},{5,1},{6,2},{7,3},{8,12},{9,13},{10,... | collective-permute-start | bytes 196616 | tf_op jit(solution)/shard_map/ppermute | solution.py:246
  30.1 2.0 %collective-permute-start = (f32[64,256]{1,0:T(8,128)S(1)}, f32[64,256]{1,0:T(8,128)S(1)}, u32[]{:S(2)}, u32[]{:S(2)}) collective-permute-start(f32[64,256]{1,0:T(8,128)S(1)} %sum_and_update.1), channel_id=1, source_target_pairs={{0,2},{1,3},{2,0},{3,1},{4,6},{5,7},{6,4},{7,5},{8,10},{9,11},{10,... | collective-permute-start | bytes 196616 | tf_op jit(solution)/shard_map/ppermute | solution.py:246
  32.1 2.4 %collective-permute-done.2 = f32[64,256]{1,0:T(8,128)S(1)} collective-permute-done((f32[64,256]{1,0:T(8,128)S(1)}, f32[64,256]{1,0:T(8,128)S(1)}, u32[]{:S(2)}, u32[]{:S(2)}) %collective-permute-start.2) | collective-permute-done | bytes 65568 | tf_op jit(solution)/shard_map/ppermute | solution.py:246
  34.5 2.1 %collective-permute-done.1 = f32[64,256]{1,0:T(8,128)S(1)} collective-permute-done((f32[64,256]{1,0:T(8,128)S(1)}, f32[64,256]{1,0:T(8,128)S(1)}, u32[]{:S(2)}, u32[]{:S(2)}) %collective-permute-start.1) | collective-permute-done | bytes 65568 | tf_op jit(solution)/shard_map/ppermute | solution.py:246
  36.6 0.6 collective-permute-start.3
  37.2 0.9 %collective-permute-start.4 = (f32[4,64,256]{2,1,0:T(8,128)S(1)}, f32[4,64,256]{2,1,0:T(8,128)S(1)}, u32[]{:S(2)}, u32[]{:S(2)}) collective-permute-start(f32[4,64,256]{2,1,0:T(8,128)S(1)} %pad_maximum_fusion.refs_0_), channel_id=1, source_target_pairs={{0,16},{1,17},{2,18},{3,19},{4,20},{5,21},{6,22},{7,23},{8,9},{9,8... | collective-permute-start | bytes 786440 | tf_op jit(solution)/shard_map/ppermute | solution.py:246
  38.1 7.4 %collective-permute-done.3.refs_1_ = f32[4,64,256]{2,1,0:T(8,128)S(1)} collective-permute-done((f32[4,64,256]{2,1,0:T(8,128)S(1)}, f32[4,64,256]{2,1,0:T(8,128)S(1)}, u32[]{:S(2)}, u32[]{:S(2)}) %collective-permute-start.3) | collective-permute-done | bytes 262176 | tf_op jit(solution)/shard_map/ppermute | solution.py:246
  45.5 0.6 collective-permute-start.5
  46.1 0.5 collective-permute-start.7
  46.6 5.3 %collective-permute-done.5.refs_3_ = f32[4,64,256]{2,1,0:T(8,128)S(1)} collective-permute-done((f32[4,64,256]{2,1,0:T(8,128)S(1)}, f32[4,64,256]{2,1,0:T(8,128)S(1)}, u32[]{:S(2)}, u32[]{:S(2)}) %collective-permute-start.5) | collective-permute-done | bytes 262176 | tf_op jit(solution)/shard_map/ppermute | solution.py:246
  51.9 5.0 %residual.1 = f32[1,1,64,8192]{3,2,1,0:T(8,128)} custom-call(bf16[64,192]{1,0:T(8,128)(2,1)S(1)} %copy-done.6, bf16[64,192]{1,0:T(8,128)(2,1)S(1)} %copy-done.7, s32[4,128]{1,0:T(4,128)S(1)} %bitcast.13, s32[1,128]{1,0:T(1,128)S(1)} %bitcast.16, f32[1,1,64,8192]{3,2,1,0:T(8,128)S(1)} %copy-done.1, f32[1,1,64,8192]{3,2,1,0:T(8,128)S(1)} %copy-done.3), custom_call_target="tpu_custom_call" | custom-call | flops 402653184 | bytes 6291456 | tf_op jit(solution)/shard_map/residual/pallas_call | solution.py:201
  56.9 1.6 %place_columns.1 = f32[64,8192]{1,0:T(8,128)} custom-call(f32[4,64,256]{2,1,0:T(8,128)S(1)} %pad_maximum_fusion.refs_0_, f32[4,64,256]{2,1,0:T(8,128)S(1)} %collective-permute-done.3.refs_1_, f32[4,64,256]{2,1,0:T(8,128)S(1)} %collective-permute-done.4.refs_2_, f32[4,64,256]{2,1,0:T(8,128)S(1)} %collective-permute-done.5.refs_3_, ...), custom_call_target="tpu_custom_call" | custom-call | tf_op jit(solution)/shard_map/place_columns/pallas_call | solution.py:270
  (24 shorter events, 0.1 us)
Async XLA Ops:
  0.6 1.6 %copy-start = (f32[1,1,64,8192]{3,2,1,0:T(8,128)S(1)}, f32[1,1,64,8192]{3,2,1,0:T(8,128)}, u32[]{:S(2)}) copy-start(f32[1,1,64,8192]{3,2,1,0:T(8,128)} %m_ref.3) | copy-start | bytes 6291460
  2.2 1.6 %copy-start.2 = (f32[1,1,64,8192]{3,2,1,0:T(8,128)S(1)}, f32[1,1,64,8192]{3,2,1,0:T(8,128)}, u32[]{:S(2)}) copy-start(f32[1,1,64,8192]{3,2,1,0:T(8,128)} %g_ref.3) | copy-start | bytes 6291460
  3.8 0.8 %copy-start.5 = (bf16[64,192]{1,0:T(8,128)(2,1)S(1)}, bf16[64,192]{1,0:T(8,128)(2,1)}, u32[]{:S(2)}) copy-start(bf16[64,192]{1,0:T(8,128)(2,1)} %constant.4.clone.table_ref) | copy-start | bytes 73732
  4.6 0.7 %copy-start.8 = (s32[1,1,128,4]{2,3,1,0:T(4,128)S(1)}, s32[1,1,128,4]{2,3,1,0:T(4,128)}, u32[]{:S(2)}) copy-start(s32[1,1,128,4]{2,3,1,0:T(4,128)} %param.11) | copy-start | bytes 6148
  5.3 0.7 %copy-start.9 = (s32[1,128,8]{1,2,0:T(8,128)S(1)}, s32[1,128,8]{1,2,0:T(8,128)}, u32[]{:S(2)}) copy-start(s32[1,128,8]{1,2,0:T(8,128)} %param.13) | copy-start | bytes 12292
  5.9 0.7 %copy-start.10 = (s32[1,1,128]{2,1,0:T(1,128)S(1)}, s32[1,1,128]{2,1,0:T(1,128)}, u32[]{:S(2)}) copy-start(s32[1,1,128]{2,1,0:T(1,128)} %param.12) | copy-start | bytes 1540
  6.6 19.8 %copy-start.4 = (f32[64,8192]{1,0:T(8,128)S(1)}, f32[64,8192]{1,0:T(8,128)}, u32[]{:S(2)}) copy-start(f32[64,8192]{1,0:T(8,128)} %params_ref.1) | copy-start | bytes 6291460
  6.6 19.8 %copy-start.7 = (bf16[64,192]{1,0:T(8,128)(2,1)S(1)}, bf16[64,192]{1,0:T(8,128)(2,1)}, u32[]{:S(2)}) copy-start(bf16[64,192]{1,0:T(8,128)(2,1)} %constant.5.clone.back_ref) | copy-start | bytes 73732
  6.6 45.3 %copy-start.3 = (f32[1,1,64,8192]{3,2,1,0:T(8,128)S(1)}, f32[1,1,64,8192]{3,2,1,0:T(8,128)}, u32[]{:S(2)}) copy-start(f32[1,1,64,8192]{3,2,1,0:T(8,128)} %g_ref.3) | copy-start | bytes 6291460
  8.6 43.3 %copy-start.1 = (f32[1,1,64,8192]{3,2,1,0:T(8,128)S(1)}, f32[1,1,64,8192]{3,2,1,0:T(8,128)}, u32[]{:S(2)}) copy-start(f32[1,1,64,8192]{3,2,1,0:T(8,128)} %m_ref.3) | copy-start | bytes 6291460
  8.6 43.3 %copy-start.6 = (bf16[64,192]{1,0:T(8,128)(2,1)S(1)}, bf16[64,192]{1,0:T(8,128)(2,1)}, u32[]{:S(2)}) copy-start(bf16[64,192]{1,0:T(8,128)(2,1)} %constant.4.clone.table_ref) | copy-start | bytes 73732
  27.6 6.9 %collective-permute-start.2 = (f32[64,256]{1,0:T(8,128)S(1)}, f32[64,256]{1,0:T(8,128)S(1)}, u32[]{:S(2)}, u32[]{:S(2)}) collective-permute-start(f32[64,256]{1,0:T(8,128)S(1)} %sum_and_update.1), channel_id=1, source_target_pairs={{0,6},{1,7},{2,4},{3,5},{4,2},{5,3},{6,0},{7,1},{8,14},{9,15},{10,... | collective-permute-start | bytes 196616 | tf_op jit(solution)/shard_map/ppermute | solution.py:246
  28.8 7.8 %collective-permute-start.1 = (f32[64,256]{1,0:T(8,128)S(1)}, f32[64,256]{1,0:T(8,128)S(1)}, u32[]{:S(2)}, u32[]{:S(2)}) collective-permute-start(f32[64,256]{1,0:T(8,128)S(1)} %sum_and_update.1), channel_id=1, source_target_pairs={{0,4},{1,5},{2,6},{3,7},{4,0},{5,1},{6,2},{7,3},{8,12},{9,13},{10,... | collective-permute-start | bytes 196616 | tf_op jit(solution)/shard_map/ppermute | solution.py:246
  30.1 6.5 %collective-permute-start = (f32[64,256]{1,0:T(8,128)S(1)}, f32[64,256]{1,0:T(8,128)S(1)}, u32[]{:S(2)}, u32[]{:S(2)}) collective-permute-start(f32[64,256]{1,0:T(8,128)S(1)} %sum_and_update.1), channel_id=1, source_target_pairs={{0,2},{1,3},{2,0},{3,1},{4,6},{5,7},{6,4},{7,5},{8,10},{9,11},{10,... | collective-permute-start | bytes 196616 | tf_op jit(solution)/shard_map/ppermute | solution.py:246
  36.6 8.9 %collective-permute-start.3 = (f32[4,64,256]{2,1,0:T(8,128)S(1)}, f32[4,64,256]{2,1,0:T(8,128)S(1)}, u32[]{:S(2)}, u32[]{:S(2)}) collective-permute-start(f32[4,64,256]{2,1,0:T(8,128)S(1)} %pad_maximum_fusion.refs_0_), channel_id=1, source_target_pairs={{0,1},{1,0},{2,3},{3,2},{4,5},{5,4},{6,7},{7,6},{8,24},{9,25},{10,... | collective-permute-start | bytes 786440 | tf_op jit(solution)/shard_map/ppermute | solution.py:246
  37.2 9.5 %collective-permute-start.4 = (f32[4,64,256]{2,1,0:T(8,128)S(1)}, f32[4,64,256]{2,1,0:T(8,128)S(1)}, u32[]{:S(2)}, u32[]{:S(2)}) collective-permute-start(f32[4,64,256]{2,1,0:T(8,128)S(1)} %pad_maximum_fusion.refs_0_), channel_id=1, source_target_pairs={{0,16},{1,17},{2,18},{3,19},{4,20},{5,21},{6,22},{7,23},{8,9},{9,8... | collective-permute-start | bytes 786440 | tf_op jit(solution)/shard_map/ppermute | solution.py:246
  45.5 6.4 %collective-permute-start.5 = (f32[4,64,256]{2,1,0:T(8,128)S(1)}, f32[4,64,256]{2,1,0:T(8,128)S(1)}, u32[]{:S(2)}, u32[]{:S(2)}) collective-permute-start(f32[4,64,256]{2,1,0:T(8,128)S(1)} %collective-permute-done.3.refs_1_), channel_id=1, source_target_pairs={{0,16},{1,17},{2,18},{3,19},{4,20},{5,21},{6,22},{7,23},{8,9},{9,8... | collective-permute-start | bytes 786440 | tf_op jit(solution)/shard_map/ppermute | solution.py:246
  46.1 10.8 %collective-permute-start.6 = (f32[4,64,256]{2,1,0:T(8,128)S(1)}, f32[4,64,256]{2,1,0:T(8,128)S(1)}, u32[]{:S(2)}, u32[]{:S(2)}) collective-permute-start(f32[4,64,256]{2,1,0:T(8,128)S(1)} %pad_maximum_fusion.refs_0_), channel_id=1, source_target_pairs={{0,8},{1,9},{2,10},{3,11},{4,12},{5,13},{6,14},{7,15},{8,0},{9,1},... | collective-permute-start | bytes 786440 | tf_op jit(solution)/shard_map/ppermute | solution.py:246
  46.1 10.8 %collective-permute-start.7 = (f32[4,64,256]{2,1,0:T(8,128)S(1)}, f32[4,64,256]{2,1,0:T(8,128)S(1)}, u32[]{:S(2)}, u32[]{:S(2)}) collective-permute-start(f32[4,64,256]{2,1,0:T(8,128)S(1)} %collective-permute-done.3.refs_1_), channel_id=1, source_target_pairs={{0,8},{1,9},{2,10},{3,11},{4,12},{5,13},{6,14},{7,15},{8,0},{9,1},... | collective-permute-start | bytes 786440 | tf_op jit(solution)/shard_map/ppermute | solution.py:246
  46.6 10.3 %collective-permute-start.8 = (f32[4,64,256]{2,1,0:T(8,128)S(1)}, f32[4,64,256]{2,1,0:T(8,128)S(1)}, u32[]{:S(2)}, u32[]{:S(2)}) collective-permute-start(f32[4,64,256]{2,1,0:T(8,128)S(1)} %collective-permute-done.4.refs_2_), channel_id=1, source_target_pairs={{0,8},{1,9},{2,10},{3,11},{4,12},{5,13},{6,14},{7,15},{8,0},{9,1},... | collective-permute-start | bytes 786440 | tf_op jit(solution)/shard_map/ppermute | solution.py:246
  51.9 5.0 %collective-permute-start.9 = (f32[4,64,256]{2,1,0:T(8,128)S(1)}, f32[4,64,256]{2,1,0:T(8,128)S(1)}, u32[]{:S(2)}, u32[]{:S(2)}) collective-permute-start(f32[4,64,256]{2,1,0:T(8,128)S(1)} %collective-permute-done.5.refs_3_), channel_id=1, source_target_pairs={{0,8},{1,9},{2,10},{3,11},{4,12},{5,13},{6,14},{7,15},{8,0},{9,1},... | collective-permute-start | bytes 786440 | tf_op jit(solution)/shard_map/ppermute | solution.py:246
where the time goes:
time: 58.9 us; the launch traced here: 58.5 us
  blocking collectives  17.8 us (30%)
  waiting for transfers between devices  17.2 us (29%)
  Pallas kernels  9.81 us (17%)
  starting transfers between devices  7.03 us (12%)
  local copies, waits for them, and re-layouts  5.98 us (10%)
  between operations  0.71 us (1%)
    all_to_all x1, blocking collectives, body(): got = lax.all_to_all(sent, EVERY, 0, 0, tiled=True)  17.8 us
    ppermute x10, waiting for transfers between devices, swap(): return lax.ppermute(array, EVERY, pairs)  17.2 us
    ppermute x10, starting transfers between devices, swap(): return lax.ppermute(array, EVERY, pairs)  7.03 us
    unnamed x22, local copies, waits for them, and re-layouts  5.98 us
    pallas_call x1, Pallas kernels, rest(): pl.pallas_call(rest_kernel, grid=(columns // step,), in_specs=[vmem(), vm...  4.98 us
    pallas_call x1, Pallas kernels, pick(): pl.pallas_call(functools.partial(pick_kernel, width), grid=(columns // st...  2.01 us
    pallas_call x1, Pallas kernels, place(): pl.pallas_call(functools.partial(place_kernel, places, sizes), in_specs=[...  1.59 us
    pallas_call x1, Pallas kernels, add_up(): pl.pallas_call(sum_kernel, in_specs=[vmem(), vmem(), pl.BlockSpec(memory_...  1.22 us
  transfers between devices with their start and end apart: 10, of which 4 were waited for; matrix products, arithmetic and copies ran while one was open for 0% of the time, Pallas kernels for 9%

commit v1 on v0

--- a/solution.py
+++ b/solution.py
@@ -43,33 +43,69 @@
     return first + lax.broadcasted_iota(jnp.int32, (SUB, LANES), 1) // order
 
 
-def pick_kernel(width, table_ref, chosen_ref, counts_ref, common_ref, m_ref, g_ref, out_ref):
-    order = m_ref.shape[-2]
+def pick_kernel(width, steps, *refs):
+    sources, out_ref, held, arrived = refs[:6], refs[6], refs[7:13], refs[13]
+    table_ref, chosen_ref, counts_ref, common_ref, m_ref, g_ref = held
+    order, columns = m_ref.shape
+    step = columns // steps
+    copies = [
+        pltpu.make_async_copy(source, target, arrived.at[n])
+        for n, (source, target) in enumerate(zip(sources[:4], held[:4], strict=True))
+    ]
+    for i in range(steps):
+        cut = pl.ds(i * step, step)
+        for source, target in zip(sources[4:], held[4:], strict=True):
+            copies.append(
+                pltpu.make_async_copy(
+                    source.at[0, 0, :, cut], target.at[:, cut], arrived.at[len(copies)]
+                )
+            )
+    for copy in copies:
+        copy.start()
+    for copy in copies[:4]:
+        copy.wait()
     chosen = chosen_ref[...]
     common = common_ref[...]
+    slots = chosen.shape[0]
     slot = lax.broadcasted_iota(jnp.int32, chosen.shape, 0)
     inside = chosen == common[0:1]
     for q in range(1, common.shape[0]):
         inside = inside | (chosen == common[q : q + 1])
     rows = jnp.where(inside & (slot < counts_ref[...]), chosen, -1)
     rows = jnp.concatenate([rows, rows], axis=0)
-    slots = chosen.shape[0]
-    spectrum = product(table_ref[...], decay_rate * m_ref[0, 0] + g_ref[0, 0])
-    step_blocks = m_ref.shape[-1] // order
-    first = lax.rem(pl.program_id(0) * step_blocks, LANES)
-    values_part = lax.broadcasted_iota(jnp.int32, (SUB, LANES), 0) < slots
-    for t in range(m_ref.shape[-1] // LANES):
-        lanes = lane_blocks(order, first + t * (LANES // order))
-        row = jnp.take_along_axis(rows, lanes, axis=1)
-        tile, within = row >> 3, row & 7
-        picked = jnp.zeros((SUB, LANES), jnp.float32)
-        for r in range(order // SUB):
-            here = spectrum[r * SUB : (r + 1) * SUB, t * LANES : (t + 1) * LANES]
-            picked = jnp.where(tile == r, jnp.take_along_axis(here, within, axis=0), picked)
-        column = t * LANES
-        out_ref[column // width, :, column % width : column % width + LANES] = jnp.where(
-            values_part, picked, row.astype(jnp.float32)
-        )
+    share = width // order
+    for i in range(steps):
+        for copy in copies[4 + 2 * i : 6 + 2 * i]:
+            copy.wait()
+        cut = pl.ds(i * step, step)
+        spectrum = product(table_ref[...], decay_rate * m_ref[:, cut] + g_ref[:, cut])
+        for t in range(step // LANES):
+            column = i * step + t * LANES
+            part, at = divmod(column, width)
+            row = block_lanes(rows, order, column // order)
+            tile, within = row >> 3, row & 7
+            picked = jnp.zeros((SUB, LANES), jnp.float32)
+            for r in range(order // SUB):
+                here = spectrum[r * SUB : (r + 1) * SUB, t * LANES : (t + 1) * LANES]
+                picked = jnp.where(
+                    tile == r, jnp.take_along_axis(here, within, axis=0), picked
+                )
+            out_ref[part, :, at : at + LANES] = picked[:slots]
+            if at == 0:
+                lanes = lax.broadcasted_iota(jnp.int32, (SUB, LANES), 1)
+                lanes = column // order + jnp.minimum(lanes, share - 1)
+                numbers = take_blocks(rows, lanes, column // order)
+                out_ref[part, :, width : width + LANES] = numbers[:slots].astype(jnp.float32)
+
+
+def take_blocks(rows, lanes, first):
+    base = first // LANES * LANES
+    return jnp.take_along_axis(rows[:, base : base + LANES], lanes - base, axis=1)
+
+
+def block_lanes(rows, order, first):
+    lanes = first + lax.broadcasted_iota(jnp.int32, (SUB, LANES), 1) // order
+    return take_blocks(rows, lanes, first)
 
 
 def rest_kernel(table_ref, back_ref, chosen_ref, counts_ref, m_ref, g_ref, out_ref):
@@ -109,24 +145,28 @@
         params_ref.at[:, pl.ds(pl.multiple_of(me * width, LANES), width)], held, arrived
     )
     copy.start()
-    slots = got_ref.shape[1] // 2
+    slots = got_ref.shape[1]
     tiles = order // SUB
     sub = lax.broadcasted_iota(jnp.int32, (SUB, LANES), 0).astype(jnp.float32)
 
     def add(n, totals):
         totals = list(totals)
+        numbers = jnp.concatenate([got_ref[n, :, width:]] * 2, axis=0)
         for t in range(width // LANES):
-            got = got_ref[n, :, t * LANES : (t + 1) * LANES]
+            values = got_ref[n, :, t * LANES : (t + 1) * LANES]
+            rows = block_lanes(numbers, order, t * (LANES // order))
             for s in range(slots):
-                value = jnp.broadcast_to(got[s : s + 1], (SUB, LANES))
-                row = jnp.broadcast_to(got[slots + s : slots + s + 1], (SUB, LANES)) - sub
+                value = jnp.broadcast_to(values[s : s + 1], (SUB, LANES))
+                row = jnp.broadcast_to(rows[s : s + 1], (SUB, LANES)) - sub
                 for r in range(tiles):
                     k = t * tiles + r
                     totals[k] = totals[k] + jnp.where(row == r * SUB, value, 0.0)
         return tuple(totals)
 
     zero = jnp.zeros((SUB, LANES), jnp.float32)
-    totals = lax.fori_loop(0, got_ref.shape[0], add, (zero,) * (tiles * (width // LANES)))
+    totals = lax.fori_loop(
+        0, got_ref.shape[0], add, (zero,) * (tiles * (width // LANES)), unroll=8
+    )
     total = jnp.concatenate(
         [
             jnp.concatenate(totals[t * tiles : (t + 1) * tiles], axis=0)
@@ -145,10 +185,8 @@
     row, col = lax.axis_index("row"), lax.axis_index("col")
     y, core, z, x = row // CORES, row % CORES, col // x_size, col % x_size
     copies = []
-    for piece, (other, first, second) in zip(pieces, places, strict=True):
+    for piece, (other, dy, dx) in zip(pieces, places, strict=True):
         owner = 1 - core if other else core
-        dy = jnp.where(owner == 0, first, second)
-        dx = jnp.where(owner == 0, second, first)
         width = piece.shape[-1]
         for j in range(z_size):
             place = ((y ^ dy) * CORES + owner) * (z_size * x_size) + (z ^ j) * x_size + (x ^ dx)
@@ -163,6 +201,10 @@
         copy.wait()
 
 
+def in_hbm(array):
+    return pltpu.with_memory_space_constraint(array, pltpu.HBM)
+
+
 def vmem():
     return pl.BlockSpec(memory_space=pltpu.VMEM)
 
@@ -178,19 +220,19 @@
 def pick(forward, momentum, gradient, chosen, counts, common, parts):
     order, columns = momentum.shape[-2:]
     width = columns // parts
-    step = max(width, columns // 8)
-    lists = functools.partial(list_spec, step=step // order)
-    field = pl.BlockSpec((1, 1, order, step), lambda i: (0, 0, 0, i))
+    steps = min(8, parts)
     slots = chosen.shape[0]
+    sources = (forward, chosen, counts, common, momentum, gradient)
+    held = [pltpu.VMEM(source.shape[-2:], source.dtype) for source in sources]
     return pl.pallas_call(
-        functools.partial(pick_kernel, width),
-        grid=(columns // step,),
-        in_specs=[vmem(), lists(slots), lists(1), lists(common.shape[0]), field, field],
-        out_specs=pl.BlockSpec((step // width, 2 * slots, width), lambda i: (i, 0, 0)),
-        out_shape=jax.ShapeDtypeStruct((parts, 2 * slots, width), jnp.float32),
+        functools.partial(pick_kernel, width, steps),
+        in_specs=[pl.BlockSpec(memory_space=pltpu.HBM)] * len(sources),
+        out_specs=vmem(),
+        out_shape=jax.ShapeDtypeStruct((parts, slots, width + LANES), jnp.float32),
+        scratch_shapes=held + [pltpu.SemaphoreType.DMA((4 + 2 * steps,))],
         compiler_params=limits(),
         name="pick_rows",
-    )(forward, chosen, counts, common, momentum, gradient)
+    )(*map(in_hbm, sources))
 
 
 def rest(forward, back, momentum, gradient, chosen, counts):
@@ -215,52 +257,45 @@
 
 
 def add_up(back, got, params):
-    width = got.shape[-1]
+    width = got.shape[-1] - LANES
     order = params.shape[0]
     return pl.pallas_call(
         sum_kernel,
-        in_specs=[vmem(), vmem(), pl.BlockSpec(memory_space=pl.ANY)],
+        in_specs=[vmem(), vmem(), pl.BlockSpec(memory_space=pltpu.HBM)],
         out_specs=vmem(),
         out_shape=jax.ShapeDtypeStruct((order, width), jnp.float32),
         scratch_shapes=[pltpu.VMEM((order, width), jnp.float32), pltpu.SemaphoreType.DMA],
         compiler_params=limits(),
         name="sum_and_update",
-    )(back, got, params)
-
-
-def spread(mine, sizes):
+    )(back, got, in_hbm(params))
+
+
+def spread(mine, residual, sizes):
     y_size, z_size, x_size = sizes
 
-    def swap(array, zero, one):
+    def swap(array, by):
         pairs = []
         for y in range(y_size):
             for core in range(CORES):
                 for z in range(z_size):
                     for x in range(x_size):
-                        dy, dk, dz, dx = (zero, one)[core]
                         here = ((y * CORES + core) * z_size + z) * x_size + x
-                        there = (((y ^ dy) * CORES + (core ^ dk)) * z_size + (z ^ dz)) * x_size + (
-                            x ^ dx
-                        )
-                        pairs.append((here, there))
+                        there = ((y ^ by[0]) * CORES + (core ^ by[1])) * z_size + (z ^ by[2])
+                        pairs.append((here, there * x_size + (x ^ by[3])))
         return lax.ppermute(array, EVERY, pairs)
 
-    line = [mine] + [swap(mine, (0, 0, j, 0), (0, 0, j, 0)) for j in range(1, z_size)]
+    line = [mine] + [swap(mine, (0, 0, j, 0)) for j in range(1, z_size)]
     own = jnp.stack(line)
-    pieces = [(own, 0, 0)]
-    first = []
-    for i in range(1, x_size):
-        got = swap(own, (0, 0, 0, i), (i, 0, 0, 0))
-        first.append((got, 0, i))
-    pieces += first
-    for j in range(1, y_size):
-        pieces.append((swap(own, (j, 0, 0, 0), (0, 0, 0, j)), j, 0))
-        for array, _, i in first:
-            pieces.append((swap(array, (j, 0, 0, 0), (0, 0, 0, j)), j, i))
-    other = [(swap(array, (0, 1, 0, 0), (0, 1, 0, 0)), dy, dx) for array, dy, dx in pieces]
-    return [(array, 0, dy, dx) for array, dy, dx in pieces] + [
-        (array, 1, dy, dx) for array, dy, dx in other
-    ]
+    far = [(j, i) for j in range(y_size) for i in range(x_size) if j or i]
+    far.sort(key=lambda at: sum(map(bool, at)))
+    pieces = [(own, 0, 0)] + [(swap(own, (j, 0, 0, i)), j, i) for j, i in far]
+    others = [(swap(array, (0, 1, 0, 0)), j, i) for array, j, i in pieces[:-1]]
+    array, j, i = pieces.pop()
+    array, residual, early = lax.optimization_barrier((array, residual, [o[0] for o in others]))
+    pieces.append((array, j, i))
+    others = [(a, o[1], o[2]) for a, o in zip(early, others, strict=True)]
+    others.append((swap(array, (0, 1, 0, 0)), j, i))
+    return pieces, others, residual
 
 
 def place(pieces, sizes, params):
@@ -289,7 +324,9 @@
     if sizes is not None:
         got = lax.all_to_all(sent, EVERY, 0, 0, tiled=True)
         mine = add_up(back, got, params)
-        new_params = place(spread(mine, sizes), sizes, params)
+        near, others, residual = spread(mine, residual, sizes)
+        pieces = [(a, 0, j, i) for a, j, i in near] + [(a, 1, j, i) for a, j, i in others]
+        new_params = place(pieces, sizes, params)
     else:
         new_params = plain_update(back, sent, params)
     return new_params, residual
@@ -299,10 +336,11 @@
     order, columns = params.shape
     got = lax.all_to_all(sent, "col", 0, 0, tiled=True)
     got = lax.all_gather(got, "row", axis=0, tiled=True)
-    slots = sent.shape[1] // 2
-    row = got[:, slots:].astype(jnp.int32)
+    width = columns // sent.shape[0]
+    row = got[:, :, width : width + width // order].astype(jnp.int32)
+    row = jnp.repeat(row, order, axis=2)
     table = row[:, :, None, :] == jnp.arange(order, dtype=jnp.int32)[:, None]
-    total = jnp.sum(jnp.where(table, got[:, :slots, None, :], 0.0), axis=(0, 1))
+    total = jnp.sum(jnp.where(table, got[:, :, None, :width], 0.0), axis=(0, 1))
     total = lax.all_gather(total, "col", axis=1, tiled=True)
     return params - step_size * product(back, total)
 

time: 58.9 us -> 48.9 us (0.83)
  local copies, waits for them, and re-layouts: 5.98 us -> 0.04 us
  waiting for transfers between devices: 17.2 us -> 12.7 us
  blocking collectives: 17.8 us -> 15.7 us
  starting transfers between devices: 7.03 us -> 8.57 us
  Pallas kernels: 9.81 us -> 10.9 us
    unnamed x22 -> x12, local copies, waits for them, and re-layouts: 5.98 us -> 0.04 us
    ppermute x10, waiting for transfers between devices: 17.2 us -> 12.7 us  [swap(): return lax.ppermute(array, EVERY, pairs)]
    all_to_all x1, blocking collectives: 17.8 us -> 15.7 us  [body(): got = lax.all_to_all(sent, EVERY, 0, 0, tiled=True)]
    ppermute x10, starting transfers between devices: 7.03 us -> 8.57 us  [swap(): return lax.ppermute(array, EVERY, pairs)]
    pallas_call x1, Pallas kernels: 2.01 us -> 3.05 us  [pick(): pl.pallas_call(functools.partial(pick_kernel, width, steps), in_specs=[pl...]
  transfers between devices with their start and end apart: 10 -> 10, of which waited for: 4 -> 5; matrix products, arithmetic and copies ran while one was open for 0% -> 0% of each run, Pallas kernels for 9% -> 10%
where the time goes in v1:
time: 48.9 us; the launch traced here: 48.7 us
  blocking collectives  15.7 us (32%)
  waiting for transfers between devices  12.7 us (26%)
  Pallas kernels  10.9 us (22%)
  starting transfers between devices  8.57 us (18%)
  between operations  0.75 us (2%)
    all_to_all x1, blocking collectives, body(): got = lax.all_to_all(sent, EVERY, 0, 0, tiled=True)  15.7 us
    ppermute x10, waiting for transfers between devices, swap(): return lax.ppermute(array, EVERY, pairs)  12.7 us
    ppermute x10, starting transfers between devices, swap(): return lax.ppermute(array, EVERY, pairs)  8.57 us
    pallas_call x1, Pallas kernels, rest(): pl.pallas_call(rest_kernel, grid=(columns // step,), in_specs=[vmem(), vm...  4.97 us
    pallas_call x1, Pallas kernels, pick(): pl.pallas_call(functools.partial(pick_kernel, width, steps), in_specs=[pl...  3.05 us
    pallas_call x1, Pallas kernels, place(): pl.pallas_call(functools.partial(place_kernel, places, sizes), in_specs=[...  1.57 us
    pallas_call x1, Pallas kernels, add_up(): pl.pallas_call(sum_kernel, in_specs=[vmem(), vmem(), pl.BlockSpec(memory_...  1.36 us
  transfers between devices with their start and end apart: 10, of which 5 were waited for; matrix products, arithmetic and copies ran while one was open for 0% of the time, Pallas kernels for 10%

profile of v1, /device:TPU:0, one launch (start us, length us, event | category | flops | bytes accessed | tf_op | source)
XLA Modules:
  0.0 48.7 jit_solution(10200962237539552679)
XLA Ops:
  0.6 0.0 copy-start.3
  0.7 3.1 %pick_rows.1 = f32[32,4,384]{2,1,0:T(4,128)S(1)} custom-call(bf16[64,192]{1,0:T(8,128)(2,1)} %constant.4.clone.refs_0_.table_ref, s32[4,128]{1,0:T(4,128)} %bitcast.12, s32[1,128]{1,0:T(1,128)} %bitcast.14, s32[8,128]{1,0:T(8,128)} %bitcast.19, f32[1,1,64,8192]{3,2,1,0:T(8,128)} %m_ref.1, f32[1,1,64,8192]{3,2,1,0:T(8,128)} %g_ref.1), custom_call_target="tpu_custom_call" | custom-call | tf_op jit(solution)/shard_map/pick_rows/pallas_call | solution.py:227
  3.7 0.0 copy-start
  3.7 0.0 copy-start.2
  3.7 0.0 copy-start.4
  3.7 0.0 copy-start.5
  3.8 15.7 %all_to_all.5.got_ref = f32[32,4,384]{2,1,0:T(4,128)S(1)} all-to-all(f32[32,4,384]{2,1,0:T(4,128)S(1)} %pick_rows.1), channel_id=1, replica_groups=mesh['row'=4,'col'=8] {'row','col'}, dimensions={0} | all-to-all | bytes 393216 | tf_op jit(solution)/shard_map/all_to_all | solution.py:325
  19.4 1.4 %sum_and_update.1 = f32[64,256]{1,0:T(8,128)S(1)} custom-call(bf16[64,192]{1,0:T(8,128)(2,1)S(1)} %copy-done.3, f32[32,4,384]{2,1,0:T(4,128)S(1)} %all_to_all.5.got_ref, f32[64,8192]{1,0:T(8,128)} %params_ref.1), custom_call_target="tpu_custom_call" | custom-call | tf_op jit(solution)/shard_map/sum_and_update/pallas_call | solution.py:262
  20.8 1.8 %collective-permute-start.2 = (f32[64,256]{1,0:T(8,128)S(1)}, f32[64,256]{1,0:T(8,128)S(1)}, u32[]{:S(2)}, u32[]{:S(2)}) collective-permute-start(f32[64,256]{1,0:T(8,128)S(1)} %sum_and_update.1), channel_id=1, source_target_pairs={{0,6},{1,7},{2,4},{3,5},{4,2},{5,3},{6,0},{7,1},{8,14},{9,15},{10,... | collective-permute-start | bytes 196616 | tf_op jit(solution)/shard_map/ppermute | solution.py:285
  22.6 1.3 %collective-permute-start.1 = (f32[64,256]{1,0:T(8,128)S(1)}, f32[64,256]{1,0:T(8,128)S(1)}, u32[]{:S(2)}, u32[]{:S(2)}) collective-permute-start(f32[64,256]{1,0:T(8,128)S(1)} %sum_and_update.1), channel_id=1, source_target_pairs={{0,4},{1,5},{2,6},{3,7},{4,0},{5,1},{6,2},{7,3},{8,12},{9,13},{10,... | collective-permute-start | bytes 196616 | tf_op jit(solution)/shard_map/ppermute | solution.py:285
  23.9 1.3 %collective-permute-start = (f32[64,256]{1,0:T(8,128)S(1)}, f32[64,256]{1,0:T(8,128)S(1)}, u32[]{:S(2)}, u32[]{:S(2)}) collective-permute-start(f32[64,256]{1,0:T(8,128)S(1)} %sum_and_update.1), channel_id=1, source_target_pairs={{0,2},{1,3},{2,0},{3,1},{4,6},{5,7},{6,4},{7,5},{8,10},{9,11},{10,... | collective-permute-start | bytes 196616 | tf_op jit(solution)/shard_map/ppermute | solution.py:285
  25.2 2.4 %collective-permute-done.2 = f32[64,256]{1,0:T(8,128)S(1)} collective-permute-done((f32[64,256]{1,0:T(8,128)S(1)}, f32[64,256]{1,0:T(8,128)S(1)}, u32[]{:S(2)}, u32[]{:S(2)}) %collective-permute-start.2) | collective-permute-done | bytes 65568 | tf_op jit(solution)/shard_map/ppermute | solution.py:285
  27.6 2.7 %collective-permute-done.1 = f32[64,256]{1,0:T(8,128)S(1)} collective-permute-done((f32[64,256]{1,0:T(8,128)S(1)}, f32[64,256]{1,0:T(8,128)S(1)}, u32[]{:S(2)}, u32[]{:S(2)}) %collective-permute-start.1) | collective-permute-done | bytes 65568 | tf_op jit(solution)/shard_map/ppermute | solution.py:285
  30.3 0.9 %collective-permute-start.4 = (f32[4,64,256]{2,1,0:T(8,128)S(1)}, f32[4,64,256]{2,1,0:T(8,128)S(1)}, u32[]{:S(2)}, u32[]{:S(2)}) collective-permute-start(f32[4,64,256]{2,1,0:T(8,128)S(1)} %pad_maximum_fusion.refs_0_), channel_id=1, source_target_pairs={{0,16},{1,17},{2,18},{3,19},{4,20},{5,21},{6,22},{7,23},{8,24},{9,... | collective-permute-start | bytes 786440 | tf_op jit(solution)/shard_map/ppermute | solution.py:285
  31.2 0.8 %collective-permute-start.3 = (f32[4,64,256]{2,1,0:T(8,128)S(1)}, f32[4,64,256]{2,1,0:T(8,128)S(1)}, u32[]{:S(2)}, u32[]{:S(2)}) collective-permute-start(f32[4,64,256]{2,1,0:T(8,128)S(1)} %pad_maximum_fusion.refs_0_), channel_id=1, source_target_pairs={{0,1},{1,0},{2,3},{3,2},{4,5},{5,4},{6,7},{7,6},{8,9},{9,8},{10,11... | collective-permute-start | bytes 786440 | tf_op jit(solution)/shard_map/ppermute | solution.py:285
  32.0 0.0 collective-permute-start.6
  32.0 1.9 %collective-permute-start.5 = (f32[4,64,256]{2,1,0:T(8,128)S(1)}, f32[4,64,256]{2,1,0:T(8,128)S(1)}, u32[]{:S(2)}, u32[]{:S(2)}) collective-permute-start(f32[4,64,256]{2,1,0:T(8,128)S(1)} %pad_maximum_fusion.refs_0_), channel_id=1, source_target_pairs={{0,17},{1,16},{2,19},{3,18},{4,21},{5,20},{6,23},{7,22},{8,25},{9,... | collective-permute-start | bytes 786440 | tf_op jit(solution)/shard_map/ppermute | solution.py:285
  33.9 4.8 %collective-permute-done.4.refs_2_ = f32[4,64,256]{2,1,0:T(8,128)S(1)} collective-permute-done((f32[4,64,256]{2,1,0:T(8,128)S(1)}, f32[4,64,256]{2,1,0:T(8,128)S(1)}, u32[]{:S(2)}, u32[]{:S(2)}) %collective-permute-start.4) | collective-permute-done | bytes 262176 | tf_op jit(solution)/shard_map/ppermute | solution.py:285
  38.7 0.0 collective-permute-start.8
  38.7 1.7 %collective-permute-done.3.refs_1_ = f32[4,64,256]{2,1,0:T(8,128)S(1)} collective-permute-done((f32[4,64,256]{2,1,0:T(8,128)S(1)}, f32[4,64,256]{2,1,0:T(8,128)S(1)}, u32[]{:S(2)}, u32[]{:S(2)}) %collective-permute-start.3) | collective-permute-done | bytes 262176 | tf_op jit(solution)/shard_map/ppermute | solution.py:285
  40.4 5.0 %residual.1 = f32[1,1,64,8192]{3,2,1,0:T(8,128)} custom-call(bf16[64,192]{1,0:T(8,128)(2,1)S(1)} %copy-done.2, bf16[64,192]{1,0:T(8,128)(2,1)S(1)} %copy-done.3, s32[4,128]{1,0:T(4,128)S(1)} %bitcast.13, s32[1,128]{1,0:T(1,128)S(1)} %bitcast.15, f32[1,1,64,8192]{3,2,1,0:T(8,128)S(1)} %copy-done, f32[1,1,64,8192]{3,2,1,0:T(8,128)S(1)} %copy-done.1), custom_call_target="tpu_custom_call" | custom-call | flops 402653184 | bytes 6291456 | tf_op jit(solution)/shard_map/residual/pallas_call | solution.py:243
  45.4 0.6 %collective-permute-start.9 = (f32[4,64,256]{2,1,0:T(8,128)S(1)}, f32[4,64,256]{2,1,0:T(8,128)S(1)}, u32[]{:S(2)}, u32[]{:S(2)}) collective-permute-start(f32[4,64,256]{2,1,0:T(8,128)S(1)} %collective-permute-done.5.refs_3_), channel_id=1, source_target_pairs={{0,8},{1,9},{2,10},{3,11},{4,12},{5,13},{6,14},{7,15},{8,0},{9,1},... | collective-permute-start | bytes 786440 | tf_op jit(solution)/shard_map/ppermute | solution.py:285
  46.0 1.2 %collective-permute-done.9.refs_7_ = f32[4,64,256]{2,1,0:T(8,128)S(1)} collective-permute-done((f32[4,64,256]{2,1,0:T(8,128)S(1)}, f32[4,64,256]{2,1,0:T(8,128)S(1)}, u32[]{:S(2)}, u32[]{:S(2)}) %collective-permute-start.9) | collective-permute-done | bytes 262176 | tf_op jit(solution)/shard_map/ppermute | solution.py:285
  47.2 1.6 %place_columns.1 = f32[64,8192]{1,0:T(8,128)} custom-call(f32[4,64,256]{2,1,0:T(8,128)S(1)} %pad_maximum_fusion.refs_0_, f32[4,64,256]{2,1,0:T(8,128)S(1)} %collective-permute-done.3.refs_1_, f32[4,64,256]{2,1,0:T(8,128)S(1)} %collective-permute-done.4.refs_2_, f32[4,64,256]{2,1,0:T(8,128)S(1)} %collective-permute-done.5.refs_3_, ...), custom_call_target="tpu_custom_call" | custom-call | tf_op jit(solution)/shard_map/place_columns/pallas_call | solution.py:305
  (14 shorter events, 0.0 us)
Async XLA Ops:
  0.6 18.8 %copy-start.3 = (bf16[64,192]{1,0:T(8,128)(2,1)S(1)}, bf16[64,192]{1,0:T(8,128)(2,1)}, u32[]{:S(2)}) copy-start(bf16[64,192]{1,0:T(8,128)(2,1)} %constant.5.clone.back_ref) | copy-start | bytes 73732
  0.6 39.8 %copy-start.1 = (f32[1,1,64,8192]{3,2,1,0:T(8,128)S(1)}, f32[1,1,64,8192]{3,2,1,0:T(8,128)}, u32[]{:S(2)}) copy-start(f32[1,1,64,8192]{3,2,1,0:T(8,128)} %g_ref.1) | copy-start | bytes 6291460
  3.7 36.7 %copy-start = (f32[1,1,64,8192]{3,2,1,0:T(8,128)S(1)}, f32[1,1,64,8192]{3,2,1,0:T(8,128)}, u32[]{:S(2)}) copy-start(f32[1,1,64,8192]{3,2,1,0:T(8,128)} %m_ref.1) | copy-start | bytes 6291460
  3.7 36.7 %copy-start.2 = (bf16[64,192]{1,0:T(8,128)(2,1)S(1)}, bf16[64,192]{1,0:T(8,128)(2,1)}, u32[]{:S(2)}) copy-start(bf16[64,192]{1,0:T(8,128)(2,1)} %constant.4.clone.refs_0_.table_ref) | copy-start | bytes 73732
  3.7 36.7 %copy-start.4 = (s32[1,1,128,4]{2,3,1,0:T(4,128)S(1)}, s32[1,1,128,4]{2,3,1,0:T(4,128)}, u32[]{:S(2)}) copy-start(s32[1,1,128,4]{2,3,1,0:T(4,128)} %param.11) | copy-start | bytes 6148
  3.7 36.7 %copy-start.5 = (s32[1,1,128]{2,1,0:T(1,128)S(1)}, s32[1,1,128]{2,1,0:T(1,128)}, u32[]{:S(2)}) copy-start(s32[1,1,128]{2,1,0:T(1,128)} %param.12) | copy-start | bytes 1540
  20.8 6.8 %collective-permute-start.2 = (f32[64,256]{1,0:T(8,128)S(1)}, f32[64,256]{1,0:T(8,128)S(1)}, u32[]{:S(2)}, u32[]{:S(2)}) collective-permute-start(f32[64,256]{1,0:T(8,128)S(1)} %sum_and_update.1), channel_id=1, source_target_pairs={{0,6},{1,7},{2,4},{3,5},{4,2},{5,3},{6,0},{7,1},{8,14},{9,15},{10,... | collective-permute-start | bytes 196616 | tf_op jit(solution)/shard_map/ppermute | solution.py:285
  22.6 7.7 %collective-permute-start.1 = (f32[64,256]{1,0:T(8,128)S(1)}, f32[64,256]{1,0:T(8,128)S(1)}, u32[]{:S(2)}, u32[]{:S(2)}) collective-permute-start(f32[64,256]{1,0:T(8,128)S(1)} %sum_and_update.1), channel_id=1, source_target_pairs={{0,4},{1,5},{2,6},{3,7},{4,0},{5,1},{6,2},{7,3},{8,12},{9,13},{10,... | collective-permute-start | bytes 196616 | tf_op jit(solution)/shard_map/ppermute | solution.py:285
  23.9 6.4 %collective-permute-start = (f32[64,256]{1,0:T(8,128)S(1)}, f32[64,256]{1,0:T(8,128)S(1)}, u32[]{:S(2)}, u32[]{:S(2)}) collective-permute-start(f32[64,256]{1,0:T(8,128)S(1)} %sum_and_update.1), channel_id=1, source_target_pairs={{0,2},{1,3},{2,0},{3,1},{4,6},{5,7},{6,4},{7,5},{8,10},{9,11},{10,... | collective-permute-start | bytes 196616 | tf_op jit(solution)/shard_map/ppermute | solution.py:285
  30.3 8.4 %collective-permute-start.4 = (f32[4,64,256]{2,1,0:T(8,128)S(1)}, f32[4,64,256]{2,1,0:T(8,128)S(1)}, u32[]{:S(2)}, u32[]{:S(2)}) collective-permute-start(f32[4,64,256]{2,1,0:T(8,128)S(1)} %pad_maximum_fusion.refs_0_), channel_id=1, source_target_pairs={{0,16},{1,17},{2,18},{3,19},{4,20},{5,21},{6,22},{7,23},{8,24},{9,... | collective-permute-start | bytes 786440 | tf_op jit(solution)/shard_map/ppermute | solution.py:285
  31.2 9.2 %collective-permute-start.3 = (f32[4,64,256]{2,1,0:T(8,128)S(1)}, f32[4,64,256]{2,1,0:T(8,128)S(1)}, u32[]{:S(2)}, u32[]{:S(2)}) collective-permute-start(f32[4,64,256]{2,1,0:T(8,128)S(1)} %pad_maximum_fusion.refs_0_), channel_id=1, source_target_pairs={{0,1},{1,0},{2,3},{3,2},{4,5},{5,4},{6,7},{7,6},{8,9},{9,8},{10,11... | collective-permute-start | bytes 786440 | tf_op jit(solution)/shard_map/ppermute | solution.py:285
  32.0 13.5 %collective-permute-start.6 = (f32[4,64,256]{2,1,0:T(8,128)S(1)}, f32[4,64,256]{2,1,0:T(8,128)S(1)}, u32[]{:S(2)}, u32[]{:S(2)}) collective-permute-start(f32[4,64,256]{2,1,0:T(8,128)S(1)} %pad_maximum_fusion.refs_0_), channel_id=1, source_target_pairs={{0,8},{1,9},{2,10},{3,11},{4,12},{5,13},{6,14},{7,15},{8,0},{9,1},... | collective-permute-start | bytes 786440 | tf_op jit(solution)/shard_map/ppermute | solution.py:285
  32.0 13.5 %collective-permute-start.5 = (f32[4,64,256]{2,1,0:T(8,128)S(1)}, f32[4,64,256]{2,1,0:T(8,128)S(1)}, u32[]{:S(2)}, u32[]{:S(2)}) collective-permute-start(f32[4,64,256]{2,1,0:T(8,128)S(1)} %pad_maximum_fusion.refs_0_), channel_id=1, source_target_pairs={{0,17},{1,16},{2,19},{3,18},{4,21},{5,20},{6,23},{7,22},{8,25},{9,... | collective-permute-start | bytes 786440 | tf_op jit(solution)/shard_map/ppermute | solution.py:285
  38.7 6.7 %collective-permute-start.8 = (f32[4,64,256]{2,1,0:T(8,128)S(1)}, f32[4,64,256]{2,1,0:T(8,128)S(1)}, u32[]{:S(2)}, u32[]{:S(2)}) collective-permute-start(f32[4,64,256]{2,1,0:T(8,128)S(1)} %collective-permute-done.4.refs_2_), channel_id=1, source_target_pairs={{0,8},{1,9},{2,10},{3,11},{4,12},{5,13},{6,14},{7,15},{8,0},{9,1},... | collective-permute-start | bytes 786440 | tf_op jit(solution)/shard_map/ppermute | solution.py:285
  40.4 5.0 %collective-permute-start.7 = (f32[4,64,256]{2,1,0:T(8,128)S(1)}, f32[4,64,256]{2,1,0:T(8,128)S(1)}, u32[]{:S(2)}, u32[]{:S(2)}) collective-permute-start(f32[4,64,256]{2,1,0:T(8,128)S(1)} %collective-permute-done.3.refs_1_), channel_id=1, source_target_pairs={{0,8},{1,9},{2,10},{3,11},{4,12},{5,13},{6,14},{7,15},{8,0},{9,1},... | collective-permute-start | bytes 786440 | tf_op jit(solution)/shard_map/ppermute | solution.py:285
  45.4 1.7 %collective-permute-start.9 = (f32[4,64,256]{2,1,0:T(8,128)S(1)}, f32[4,64,256]{2,1,0:T(8,128)S(1)}, u32[]{:S(2)}, u32[]{:S(2)}) collective-permute-start(f32[4,64,256]{2,1,0:T(8,128)S(1)} %collective-permute-done.5.refs_3_), channel_id=1, source_target_pairs={{0,8},{1,9},{2,10},{3,11},{4,12},{5,13},{6,14},{7,15},{8,0},{9,1},... | collective-permute-start | bytes 786440 | tf_op jit(solution)/shard_map/ppermute | solution.py:285

commit v2 on v1

--- a/solution.py
+++ b/solution.py
@@ -17,6 +17,7 @@
 CORES = 2
 EVERY = ("row", "col")
 VMEM_BYTES = 48 * 1024 * 1024
+LATE = (0, 3)
 
 
 def dct_table(order):
@@ -37,10 +38,6 @@
     low = (field - high.astype(jnp.float32)).astype(jnp.bfloat16)
     stacked = jnp.concatenate([high, high, low], axis=0)
     return jnp.dot(table, stacked, preferred_element_type=jnp.float32)
-
-
-def lane_blocks(order, first):
-    return first + lax.broadcasted_iota(jnp.int32, (SUB, LANES), 1) // order
 
 
 def pick_kernel(width, steps, *refs):
@@ -71,31 +68,30 @@
     inside = chosen == common[0:1]
     for q in range(1, common.shape[0]):
         inside = inside | (chosen == common[q : q + 1])
-    rows = jnp.where(inside & (slot < counts_ref[...]), chosen, -1)
+    live = jnp.where(slot < counts_ref[...], chosen, -1)
+    rows = jnp.where(inside, live, -1)
+    live = jnp.concatenate([live, live], axis=0)
     rows = jnp.concatenate([rows, rows], axis=0)
     share = width // order
     for i in range(steps):
         for copy in copies[4 + 2 * i : 6 + 2 * i]:
             copy.wait()
-        cut = pl.ds(i * step, step)
-        spectrum = product(table_ref[...], decay_rate * m_ref[:, cut] + g_ref[:, cut])
-        for t in range(step // LANES):
-            column = i * step + t * LANES
-            part, at = divmod(column, width)
-            row = block_lanes(rows, order, column // order)
-            tile, within = row >> 3, row & 7
-            picked = jnp.zeros((SUB, LANES), jnp.float32)
-            for r in range(order // SUB):
-                here = spectrum[r * SUB : (r + 1) * SUB, t * LANES : (t + 1) * LANES]
-                picked = jnp.where(
-                    tile == r, jnp.take_along_axis(here, within, axis=0), picked
-                )
-            out_ref[part, :, at : at + LANES] = picked[:slots]
-            if at == 0:
-                lanes = lax.broadcasted_iota(jnp.int32, (SUB, LANES), 1)
-                lanes = column // order + jnp.minimum(lanes, share - 1)
-                numbers = take_blocks(rows, lanes, column // order)
-                out_ref[part, :, width : width + LANES] = numbers[:slots].astype(jnp.float32)
+        for part in range(i * step // width, (i + 1) * step // width):
+            cut = pl.ds(part * width, width)
+            spectrum = product(table_ref[...], decay_rate * m_ref[:, cut] + g_ref[:, cut])
+            for t in range(width // LANES):
+                row = block_lanes(live, order, (part * width + t * LANES) // order)
+                tile, within = row >> 3, row & 7
+                picked = jnp.zeros((SUB, LANES), jnp.float32)
+                for r in range(order // SUB):
+                    here = spectrum[r * SUB : (r + 1) * SUB, t * LANES : (t + 1) * LANES]
+                    here = jnp.take_along_axis(here, within, axis=0)
+                    picked = jnp.where(tile == r, here, picked)
+                out_ref[part, :, t * LANES : (t + 1) * LANES] = picked[:slots]
+            lanes = lax.broadcasted_iota(jnp.int32, (SUB, LANES), 1)
+            lanes = part * share + jnp.minimum(lanes, share - 1)
+            numbers = take_blocks(rows, lanes, part * share)
+            out_ref[part, :, width:] = numbers[:slots].astype(jnp.float32)
 
 
 def take_blocks(rows, lanes, first):
@@ -108,34 +104,43 @@
     return take_blocks(rows, lanes, first)
 
 
-def rest_kernel(table_ref, back_ref, chosen_ref, counts_ref, m_ref, g_ref, out_ref):
-    order, columns = m_ref.shape[-2:]
+def rest_kernel(skipped, start, width, *refs):
+    back_ref, chosen_ref, counts_ref, sent_ref, m_ref, g_ref, out_ref, held, gone = refs[skipped:]
+    order, columns = held.shape
     chosen = chosen_ref[...]
+    slots = chosen.shape[0]
     slot = lax.broadcasted_iota(jnp.int32, chosen.shape, 0)
-    bits = jnp.where(slot < counts_ref[...], jnp.int32(1) << (chosen & 31), 0)
-    words = []
-    for half in range(order // 32):
-        mine = jnp.where((chosen >> 5) == half, bits, 0)
-        word = mine[0:1]
-        for s in range(1, chosen.shape[0]):
-            word = word | mine[s : s + 1]
-        words.append(jnp.broadcast_to(word, (SUB, LANES)))
-    decayed = decay_rate * m_ref[0, 0] + g_ref[0, 0]
-    spectrum = product(table_ref[...], decayed)
-    first = lax.rem(pl.program_id(0) * (columns // order), LANES)
+    live = jnp.where(slot < counts_ref[...], chosen, -1)
+    live = jnp.concatenate([live, live], axis=0)
     sub = lax.broadcasted_iota(jnp.int32, (SUB, LANES), 0)
-    parts = []
-    for t in range(columns // LANES):
-        lanes = lane_blocks(order, first + t * (LANES // order))
-        wide = [jnp.take_along_axis(word, lanes, axis=1) for word in words]
-        tiles = []
-        for r in range(order // SUB):
-            here = spectrum[r * SUB : (r + 1) * SUB, t * LANES : (t + 1) * LANES]
-            bit = jnp.int32(1) << (sub + (r * SUB) % 32)
-            tiles.append(jnp.where((wide[r * SUB // 32] & bit) != 0, here, 0.0))
-        parts.append(jnp.concatenate(tiles, axis=0))
-    sent = jnp.concatenate(parts, axis=1)
-    out_ref[0, 0] = decayed - product(back_ref[...], sent)
+    copies = []
+    for part in range(columns // width):
+        parts = []
+        for t in range(width // LANES):
+            values = sent_ref[start + part, :, t * LANES : (t + 1) * LANES]
+            rows = block_lanes(live, order, ((start + part) * width + t * LANES) // order)
+            wide = [
+                (
+                    jnp.broadcast_to(rows[s : s + 1], (SUB, LANES)) - sub,
+                    jnp.broadcast_to(values[s : s + 1], (SUB, LANES)),
+                )
+                for s in range(slots)
+            ]
+            tiles = []
+            for r in range(order // SUB):
+                tile = jnp.zeros((SUB, LANES), jnp.float32)
+                for row, value in wide:
+                    tile = jnp.where(row == r * SUB, value, tile)
+                tiles.append(tile)
+            parts.append(jnp.concatenate(tiles, axis=0))
+        back = product(back_ref[...], jnp.concatenate(parts, axis=1))
+        cut, here = pl.ds((start + part) * width, width), pl.ds(part * width, width)
+        held[:, here] = decay_rate * m_ref[0, 0, :, cut] + g_ref[0, 0, :, cut] - back
+        copy = pltpu.make_async_copy(held.at[:, here], out_ref.at[0, 0, :, cut], gone.at[part])
+        copy.start()
+        copies.append(copy)
+    for copy in copies:
+        copy.wait()
 
 
 def sum_kernel(back_ref, got_ref, params_ref, out_ref, held, arrived):
@@ -179,17 +184,18 @@
     out_ref[...] = held[...] - step_size * update
 
 
-def place_kernel(places, sizes, *refs):
-    *pieces, out_ref, sems = refs
+def place_kernel(places, sizes, skipped, *refs):
+    *pieces, out_ref, sems = refs[skipped:]
     y_size, z_size, x_size = sizes
     row, col = lax.axis_index("row"), lax.axis_index("col")
     y, core, z, x = row // CORES, row % CORES, col // x_size, col % x_size
     copies = []
-    for piece, (other, dy, dx) in zip(pieces, places, strict=True):
+    for piece, (other, dy, dx, dz) in zip(pieces, places, strict=True):
         owner = 1 - core if other else core
         width = piece.shape[-1]
-        for j in range(z_size):
-            place = ((y ^ dy) * CORES + owner) * (z_size * x_size) + (z ^ j) * x_size + (x ^ dx)
+        for j in range(piece.shape[0]):
+            place = ((y ^ dy) * CORES + owner) * z_size + (z ^ (dz + j))
+            place = place * x_size + (x ^ dx)
             copy = pltpu.make_async_copy(
                 piece.at[j],
                 out_ref.at[:, pl.ds(pl.multiple_of(place * width, LANES), width)],
@@ -220,7 +226,7 @@
 def pick(forward, momentum, gradient, chosen, counts, common, parts):
     order, columns = momentum.shape[-2:]
     width = columns // parts
-    steps = min(8, parts)
+    steps = min(4, parts)
     slots = chosen.shape[0]
     sources = (forward, chosen, counts, common, momentum, gradient)
     held = [pltpu.VMEM(source.shape[-2:], source.dtype) for source in sources]
@@ -235,25 +241,29 @@
     )(*map(in_hbm, sources))
 
 
-def rest(forward, back, momentum, gradient, chosen, counts):
-    order, columns = momentum.shape[-2:]
-    step = columns // 8
-    lists = functools.partial(list_spec, step=step // order)
-    field = pl.BlockSpec((1, 1, order, step), lambda i: (0, 0, 0, i))
+def rest(back, sent, momentum, gradient, chosen, counts, first, parts, before):
+    order = momentum.shape[-2]
+    width = sent.shape[-1] - LANES
+    anywhere = pl.BlockSpec(memory_space=pl.ANY)
+    given = [] if before is None else [before]
     return pl.pallas_call(
-        rest_kernel,
-        grid=(columns // step,),
-        in_specs=[vmem(), vmem(), lists(chosen.shape[0]), lists(1), field, field],
-        out_specs=field,
+        functools.partial(rest_kernel, len(given), first, width),
+        in_specs=[anywhere] * len(given) + [vmem()] * 6,
+        out_specs=anywhere,
         out_shape=jax.ShapeDtypeStruct(momentum.shape, jnp.float32),
+        scratch_shapes=[
+            pltpu.VMEM((order, parts * width), jnp.float32),
+            pltpu.SemaphoreType.DMA((parts,)),
+        ],
+        input_output_aliases={0: 0} if given else {},
         compiler_params=limits(),
         name="residual",
         cost_estimate=pl.CostEstimate(
-            flops=12 * order * order * columns,
-            bytes_accessed=3 * momentum.size * 4,
+            flops=12 * order * order * momentum.shape[-1] * 100,
+            bytes_accessed=3 * momentum.size * 400,
             transcendentals=0,
         ),
-    )(forward, back, chosen, counts, momentum, gradient)
+    )(*given, back, chosen, counts, sent, momentum, gradient)
 
 
 def add_up(back, got, params):
@@ -270,7 +280,7 @@
     )(back, got, in_hbm(params))
 
 
-def spread(mine, residual, sizes):
+def spread(mine, piece, params, sizes):
     y_size, z_size, x_size = sizes
 
     def swap(array, by):
@@ -285,32 +295,51 @@
         return lax.ppermute(array, EVERY, pairs)
 
     line = [mine] + [swap(mine, (0, 0, j, 0)) for j in range(1, z_size)]
-    own = jnp.stack(line)
     far = [(j, i) for j in range(y_size) for i in range(x_size) if j or i]
     far.sort(key=lambda at: sum(map(bool, at)))
-    pieces = [(own, 0, 0)] + [(swap(own, (j, 0, 0, i)), j, i) for j, i in far]
-    others = [(swap(array, (0, 1, 0, 0)), j, i) for array, j, i in pieces[:-1]]
-    array, j, i = pieces.pop()
-    array, residual, early = lax.optimization_barrier((array, residual, [o[0] for o in others]))
-    pieces.append((array, j, i))
-    others = [(a, o[1], o[2]) for a, o in zip(early, others, strict=True)]
-    others.append((swap(array, (0, 1, 0, 0)), j, i))
-    return pieces, others, residual
-
-
-def place(pieces, sizes, params):
+    half = max(1, z_size // 2)
+    groups = z_size // half
+    parts = y_size * CORES * z_size * x_size
+    fill = parts // 8
+    early, late, residual = [], [], None
+    for n in range(groups):
+        held = line[n * half : (n + 1) * half]
+        if n:
+            residual = piece((n - 1) * fill, fill, residual)
+            held, residual = lax.optimization_barrier((held, residual))
+        own = jnp.stack(held)
+        early.append((own, 0, 0, n * half))
+        sent = [(swap(own, (j, 0, 0, i)), j, i, n * half) for j, i in far]
+        kept = len(sent) - LATE[min(n, 1)]
+        early += sent[:kept]
+        late += sent[kept:]
+    residual = piece((groups - 1) * fill, parts - (groups - 1) * fill, residual)
+
+    def both(array, *at):
+        return [(array, 0, *at), (swap(array, (0, 1, 0, 0)), 1, *at)]
+
+    partial = place([made for piece_of in early for made in both(*piece_of)], sizes, params, None)
+    arrays = [piece_of[0] for piece_of in late]
+    arrays, residual, partial = lax.optimization_barrier((arrays, residual, partial))
+    made = [made for array, at in zip(arrays, late, strict=True) for made in both(array, *at[1:])]
+    return place(made, sizes, params, partial), residual
+
+
+def place(pieces, sizes, params, partial):
     arrays = [piece[0] for piece in pieces]
     places = [piece[1:] for piece in pieces]
     anywhere = pl.BlockSpec(memory_space=pl.ANY)
+    given = [] if partial is None else [partial]
     return pl.pallas_call(
-        functools.partial(place_kernel, places, sizes),
-        in_specs=[anywhere] * len(arrays),
+        functools.partial(place_kernel, places, sizes, len(given)),
+        in_specs=[anywhere] * (len(given) + len(arrays)),
         out_specs=anywhere,
         out_shape=jax.ShapeDtypeStruct(params.shape, jnp.float32),
-        scratch_shapes=[pltpu.SemaphoreType.DMA((len(arrays) * sizes[1],))],
+        scratch_shapes=[pltpu.SemaphoreType.DMA((sum(array.shape[0] for array in arrays),))],
+        input_output_aliases={0: 0} if given else {},
         compiler_params=limits(),
         name="place_columns",
-    )(*arrays)
+    )(*given, *arrays)
 
 
 def body(sizes, parts, params, momentum, gradient, chosen_rows, live_counts, common_rows):
@@ -320,14 +349,13 @@
     counts = live_counts[0]
     common = jnp.transpose(common_rows[0])
     sent = pick(forward, momentum, gradient, chosen, counts, common, parts)
-    residual = rest(forward, back, momentum, gradient, chosen, counts)
+    piece = functools.partial(rest, back, sent, momentum, gradient, chosen, counts)
     if sizes is not None:
         got = lax.all_to_all(sent, EVERY, 0, 0, tiled=True)
         mine = add_up(back, got, params)
-        near, others, residual = spread(mine, residual, sizes)
-        pieces = [(a, 0, j, i) for a, j, i in near] + [(a, 1, j, i) for a, j, i in others]
-        new_params = place(pieces, sizes, params)
+        new_params, residual = spread(mine, piece, params, sizes)
     else:
+        residual = piece(0, parts, None)
         new_params = plain_update(back, sent, params)
     return new_params, residual
 

time: 48.9 us -> 45.5 us (0.930)
  waiting for transfers between devices: 12.7 us -> 7.31 us
  starting transfers between devices: 8.57 us -> 12 us
  Pallas kernels: 10.9 us -> 9.55 us
    ppermute x10 -> x17, waiting for transfers between devices: 12.7 us -> 7.31 us  [swap(): return lax.ppermute(array, EVERY, pairs)]
    ppermute x10 -> x17, starting transfers between devices: 8.57 us -> 12 us  [swap(): return lax.ppermute(array, EVERY, pairs)]
    pallas_call x2 -> x4, Pallas kernels: 6.53 us -> 5.45 us  [the longest x2 3.25 us: rest(): pl.pallas_call(functools.partial(rest_kernel, len(given), first, width),...]
  transfers between devices with their start and end apart: 10 -> 17, of which waited for: 5 -> 9; matrix products, arithmetic and copies ran while one was open for 0% -> 0% of each run, Pallas kernels for 10% -> 10%
where the time goes in v2:
time: 45.5 us; the launch traced here: 45.3 us
  blocking collectives  15.7 us (35%)
  starting transfers between devices  12 us (26%)
  Pallas kernels  9.55 us (21%)
  waiting for transfers between devices  7.31 us (16%)
  between operations  0.77 us (2%)
    all_to_all x1, blocking collectives, body(): got = lax.all_to_all(sent, EVERY, 0, 0, tiled=True)  15.7 us
    ppermute x17, starting transfers between devices, swap(): return lax.ppermute(array, EVERY, pairs)  12 us
    ppermute x17, waiting for transfers between devices, swap(): return lax.ppermute(array, EVERY, pairs)  7.31 us
    pallas_call x2, Pallas kernels, rest(): pl.pallas_call(functools.partial(rest_kernel, len(given), first, width),...  3.25 us
    pallas_call x1, Pallas kernels, pick(): pl.pallas_call(functools.partial(pick_kernel, width, steps), in_specs=[pl...  2.74 us
    pallas_call x2, Pallas kernels, place(): pl.pallas_call(functools.partial(place_kernel, places, sizes, len(given))...  2.2 us
    pallas_call x1, Pallas kernels, add_up(): pl.pallas_call(sum_kernel, in_specs=[vmem(), vmem(), pl.BlockSpec(memory_...  1.36 us
  transfers between devices with their start and end apart: 17, of which 9 were waited for; matrix products, arithmetic and copies ran while one was open for 0% of the time, Pallas kernels for 10%

profile of v2, /device:TPU:0, one launch (start us, length us, event | category | flops | bytes accessed | tf_op | source)
XLA Modules:
  0.0 45.3 jit_solution(3394064687850580575)
XLA Ops:
  0.7 2.7 %pick_rows.1.refs_3_.refs_4_ = f32[32,4,384]{2,1,0:T(4,128)S(1)} custom-call(bf16[64,192]{1,0:T(8,128)(2,1)} %constant.4.clone.refs_0_, s32[4,128]{1,0:T(4,128)} %bitcast.12, s32[1,128]{1,0:T(1,128)} %bitcast.15, s32[8,128]{1,0:T(8,128)} %bitcast.21, f32[1,1,64,8192]{3,2,1,0:T(8,128)} %refs_5_.5, f32[1,1,64,8192]{3,2,1,0:T(8,128)} %refs_6_.1), custom_call_target="tpu_custom_call" | custom-call | tf_op jit(solution)/shard_map/pick_rows/pallas_call | solution.py:233
  3.4 15.7 %all_to_all.5.got_ref = f32[32,4,384]{2,1,0:T(4,128)S(1)} all-to-all(f32[32,4,384]{2,1,0:T(4,128)S(1)} %pick_rows.1.refs_3_.refs_4_), channel_id=1, replica_groups=mesh['row'=4,'col'=8] {'row','col'}, dimensions={0} | all-to-all | bytes 393216 | tf_op jit(solution)/shard_map/all_to_all | solution.py:354
  19.1 1.4 %sum_and_update.1 = f32[64,256]{1,0:T(8,128)S(1)} custom-call(bf16[64,192]{1,0:T(8,128)(2,1)S(1)} %copy-done.2, f32[32,4,384]{2,1,0:T(4,128)S(1)} %all_to_all.5.got_ref, f32[64,8192]{1,0:T(8,128)} %params_ref.1), custom_call_target="tpu_custom_call" | custom-call | tf_op jit(solution)/shard_map/sum_and_update/pallas_call | solution.py:272
  20.5 1.7 %collective-permute-start.5 = (f32[64,256]{1,0:T(8,128)S(1)}, f32[64,256]{1,0:T(8,128)S(1)}, u32[]{:S(2)}, u32[]{:S(2)}) collective-permute-start(f32[64,256]{1,0:T(8,128)S(1)} %sum_and_update.1), channel_id=1, source_target_pairs={{0,2},{1,3},{2,0},{3,1},{4,6},{5,7},{6,4},{7,5},{8,10},{9,11},{10,... | collective-permute-start | bytes 196616 | tf_op jit(solution)/shard_map/ppermute | solution.py:295
  22.2 1.4 %collective-permute-start.1 = (f32[64,256]{1,0:T(8,128)S(1)}, f32[64,256]{1,0:T(8,128)S(1)}, u32[]{:S(2)}, u32[]{:S(2)}) collective-permute-start(f32[64,256]{1,0:T(8,128)S(1)} %sum_and_update.1), channel_id=1, source_target_pairs={{0,6},{1,7},{2,4},{3,5},{4,2},{5,3},{6,0},{7,1},{8,14},{9,15},{10,... | collective-permute-start | bytes 196616 | tf_op jit(solution)/shard_map/ppermute | solution.py:295
  23.5 0.5 %collective-permute-start = (f32[64,256]{1,0:T(8,128)S(1)}, f32[64,256]{1,0:T(8,128)S(1)}, u32[]{:S(2)}, u32[]{:S(2)}) collective-permute-start(f32[64,256]{1,0:T(8,128)S(1)} %sum_and_update.1), channel_id=1, source_target_pairs={{0,4},{1,5},{2,6},{3,7},{4,0},{5,1},{6,2},{7,3},{8,12},{9,13},{10,... | collective-permute-start | bytes 196616 | tf_op jit(solution)/shard_map/ppermute | solution.py:295
  24.0 0.8 %collective-permute-done.5 = f32[64,256]{1,0:T(8,128)S(1)} collective-permute-done((f32[64,256]{1,0:T(8,128)S(1)}, f32[64,256]{1,0:T(8,128)S(1)}, u32[]{:S(2)}, u32[]{:S(2)}) %collective-permute-start.5) | collective-permute-done | bytes 65568 | tf_op jit(solution)/shard_map/ppermute | solution.py:295
  24.8 1.8 %collective-permute-start.11 = (f32[2,64,256]{2,1,0:T(8,128)S(1)}, f32[2,64,256]{2,1,0:T(8,128)S(1)}, u32[]{:S(2)}, u32[]{:S(2)}) collective-permute-start(f32[2,64,256]{2,1,0:T(8,128)S(1)} %pad_maximum_fusion.1.refs_0_), channel_id=1, source_target_pairs={{0,17},{1,16},{2,19},{3,18},{4,21},{5,20},{6,23},{7,22},{8,25},{9,... | collective-permute-start | bytes 393224 | tf_op jit(solution)/shard_map/ppermute | solution.py:295
  26.6 1.0 %residual.2.refs_0_ = f32[1,1,64,8192]{3,2,1,0:T(8,128)} custom-call(bf16[64,192]{1,0:T(8,128)(2,1)S(1)} %copy-done.2, s32[4,128]{1,0:T(4,128)S(1)} %bitcast.13, s32[1,128]{1,0:T(1,128)S(1)} %bitcast.16, f32[32,4,384]{2,1,0:T(4,128)S(1)} %pick_rows.1.refs_3_.refs_4_, f32[1,1,64,8192]{3,2,1,0:T(8,128)S(1)} %copy-done, f32[1,1,64,8192]{3,2,1,0:T(8,128)S(1)} %copy-done.1), custom_call_target="tpu_custom_call" | custom-call | flops 40265318400 | bytes 629145600 | tf_op jit(solution)/shard_map/residual/pallas_call | solution.py:249
  27.6 1.5 %collective-permute-start.9 = (f32[2,64,256]{2,1,0:T(8,128)S(1)}, f32[2,64,256]{2,1,0:T(8,128)S(1)}, u32[]{:S(2)}, u32[]{:S(2)}) collective-permute-start(f32[2,64,256]{2,1,0:T(8,128)S(1)} %pad_maximum_fusion.1.refs_0_), channel_id=1, source_target_pairs={{0,16},{1,17},{2,18},{3,19},{4,20},{5,21},{6,22},{7,23},{8,24},{9,... | collective-permute-start | bytes 393224 | tf_op jit(solution)/shard_map/ppermute | solution.py:295
  29.5 1.1 %collective-permute-done = f32[64,256]{1,0:T(8,128)S(1)} collective-permute-done((f32[64,256]{1,0:T(8,128)S(1)}, f32[64,256]{1,0:T(8,128)S(1)}, u32[]{:S(2)}, u32[]{:S(2)}) %collective-permute-start) | collective-permute-done | bytes 65568 | tf_op jit(solution)/shard_map/ppermute | solution.py:295
  30.7 0.4 collective-permute-done.11.refs_6_
  31.2 2.0 %collective-permute-done.9.refs_4_ = f32[2,64,256]{2,1,0:T(8,128)S(1)} collective-permute-done((f32[2,64,256]{2,1,0:T(8,128)S(1)}, f32[2,64,256]{2,1,0:T(8,128)S(1)}, u32[]{:S(2)}, u32[]{:S(2)}) %collective-permute-start.9) | collective-permute-done | bytes 131104 | tf_op jit(solution)/shard_map/ppermute | solution.py:295
  33.2 1.8 %collective-permute-start.4 = (f32[2,64,256]{2,1,0:T(8,128)S(1)}, f32[2,64,256]{2,1,0:T(8,128)S(1)}, u32[]{:S(2)}, u32[]{:S(2)}) collective-permute-start(f32[2,64,256]{2,1,0:T(8,128)S(1)} %pad_maximum_fusion.refs_8_), channel_id=1, source_target_pairs={{0,17},{1,16},{2,19},{3,18},{4,21},{5,20},{6,23},{7,22},{8,25},{9,... | collective-permute-start | bytes 393224 | tf_op jit(solution)/shard_map/ppermute | solution.py:295
  35.0 1.7 %collective-permute-start.3 = (f32[2,64,256]{2,1,0:T(8,128)S(1)}, f32[2,64,256]{2,1,0:T(8,128)S(1)}, u32[]{:S(2)}, u32[]{:S(2)}) collective-permute-start(f32[2,64,256]{2,1,0:T(8,128)S(1)} %pad_maximum_fusion.refs_8_), channel_id=1, source_target_pairs={{0,16},{1,17},{2,18},{3,19},{4,20},{5,21},{6,22},{7,23},{8,24},{9,... | collective-permute-start | bytes 393224 | tf_op jit(solution)/shard_map/ppermute | solution.py:295
  36.8 0.5 %collective-permute-start.8 = (f32[2,64,256]{2,1,0:T(8,128)S(1)}, f32[2,64,256]{2,1,0:T(8,128)S(1)}, u32[]{:S(2)}, u32[]{:S(2)}) collective-permute-start(f32[2,64,256]{2,1,0:T(8,128)S(1)} %collective-permute-done.7.refs_2_), channel_id=1, source_target_pairs={{0,8},{1,9},{2,10},{3,11},{4,12},{5,13},{6,14},{7,15},{8,0},{9,1},... | collective-permute-start | bytes 393224 | tf_op jit(solution)/shard_map/ppermute | solution.py:295
  37.3 2.2 %residual.3 = f32[1,1,64,8192]{3,2,1,0:T(8,128)} custom-call(f32[1,1,64,8192]{3,2,1,0:T(8,128)} %residual.2.refs_0_, bf16[64,192]{1,0:T(8,128)(2,1)S(1)} %copy-done.2, s32[4,128]{1,0:T(4,128)S(1)} %bitcast.14, s32[1,128]{1,0:T(1,128)S(1)} %bitcast.17, f32[32,4,384]{2,1,0:T(4,128)S(1)} %pick_rows.1.refs_3_.refs_4_, ...), custom_call_target="tpu_custom_call", output_to_operand_aliasing={{}: (0, {})} | custom-call | flops 40265318400 | bytes 629145600 | tf_op jit(solution)/shard_map/residual/pallas_call | solution.py:249
  39.6 1.2 %place_columns.2.refs_0_ = f32[64,8192]{1,0:T(8,128)} custom-call(f32[2,64,256]{2,1,0:T(8,128)S(1)} %pad_maximum_fusion.1.refs_0_, f32[2,64,256]{2,1,0:T(8,128)S(1)} %collective-permute-done.6.refs_1_, f32[2,64,256]{2,1,0:T(8,128)S(1)} %collective-permute-done.7.refs_2_, f32[2,64,256]{2,1,0:T(8,128)S(1)} %collective-permute-done.8.refs_3_, ...), custom_call_target="tpu_custom_call" | custom-call | tf_op jit(solution)/shard_map/place_columns/pallas_call | solution.py:333
  40.8 0.7 %collective-permute-done.3.refs_3_ = f32[2,64,256]{2,1,0:T(8,128)S(1)} collective-permute-done((f32[2,64,256]{2,1,0:T(8,128)S(1)}, f32[2,64,256]{2,1,0:T(8,128)S(1)}, u32[]{:S(2)}, u32[]{:S(2)}) %collective-permute-start.3) | collective-permute-done | bytes 131104 | tf_op jit(solution)/shard_map/ppermute | solution.py:295
  41.5 1.0 %collective-permute-done.2.refs_1_ = f32[2,64,256]{2,1,0:T(8,128)S(1)} collective-permute-done((f32[2,64,256]{2,1,0:T(8,128)S(1)}, f32[2,64,256]{2,1,0:T(8,128)S(1)}, u32[]{:S(2)}, u32[]{:S(2)}) %collective-permute-start.2) | collective-permute-done | bytes 131104 | tf_op jit(solution)/shard_map/ppermute | solution.py:295
  42.5 0.5 %collective-permute-start.15 = (f32[2,64,256]{2,1,0:T(8,128)S(1)}, f32[2,64,256]{2,1,0:T(8,128)S(1)}, u32[]{:S(2)}, u32[]{:S(2)}) collective-permute-start(f32[2,64,256]{2,1,0:T(8,128)S(1)} %collective-permute-done.3.refs_3_), channel_id=1, source_target_pairs={{0,8},{1,9},{2,10},{3,11},{4,12},{5,13},{6,14},{7,15},{8,0},{9,1},... | collective-permute-start | bytes 393224 | tf_op jit(solution)/shard_map/ppermute | solution.py:295
  43.0 0.8 %collective-permute-done.14.refs_2_ = f32[2,64,256]{2,1,0:T(8,128)S(1)} collective-permute-done((f32[2,64,256]{2,1,0:T(8,128)S(1)}, f32[2,64,256]{2,1,0:T(8,128)S(1)}, u32[]{:S(2)}, u32[]{:S(2)}) %collective-permute-start.14) | collective-permute-done | bytes 131104 | tf_op jit(solution)/shard_map/ppermute | solution.py:295
  44.0 0.3 collective-permute-done.16.refs_6_
  44.3 1.0 %place_columns.3 = f32[64,8192]{1,0:T(8,128)} custom-call(f32[64,8192]{1,0:T(8,128)} %place_columns.2.refs_0_, f32[2,64,256]{2,1,0:T(8,128)S(1)} %collective-permute-done.2.refs_1_, f32[2,64,256]{2,1,0:T(8,128)S(1)} %collective-permute-done.14.refs_2_, f32[2,64,256]{2,1,0:T(8,128)S(1)} %collective-permute-done.3.refs_3_, ...), custom_call_target="tpu_custom_call", output_to_operand_aliasing={{}: (0, {})} | custom-call | tf_op jit(solution)/shard_map/place_columns/pallas_call | solution.py:333
  (29 shorter events, 0.8 us)
Async XLA Ops:
  0.6 18.5 %copy-start.2 = (bf16[64,192]{1,0:T(8,128)(2,1)S(1)}, bf16[64,192]{1,0:T(8,128)(2,1)}, u32[]{:S(2)}) copy-start(bf16[64,192]{1,0:T(8,128)(2,1)} %constant.5.clone.back_ref.refs_0_.refs_1_) | copy-start | bytes 73732
  0.6 26.0 %copy-start.1 = (f32[1,1,64,8192]{3,2,1,0:T(8,128)S(1)}, f32[1,1,64,8192]{3,2,1,0:T(8,128)}, u32[]{:S(2)}) copy-start(f32[1,1,64,8192]{3,2,1,0:T(8,128)} %refs_6_.1) | copy-start | bytes 6291460
  3.4 23.2 %copy-start = (f32[1,1,64,8192]{3,2,1,0:T(8,128)S(1)}, f32[1,1,64,8192]{3,2,1,0:T(8,128)}, u32[]{:S(2)}) copy-start(f32[1,1,64,8192]{3,2,1,0:T(8,128)} %refs_5_.5) | copy-start | bytes 6291460
  3.4 23.2 %copy-start.3 = (s32[1,1,128,4]{2,3,1,0:T(4,128)S(1)}, s32[1,1,128,4]{2,3,1,0:T(4,128)}, u32[]{:S(2)}) copy-start(s32[1,1,128,4]{2,3,1,0:T(4,128)} %param.11) | copy-start | bytes 6148
  3.4 23.2 %copy-start.4 = (s32[1,1,128]{2,1,0:T(1,128)S(1)}, s32[1,1,128]{2,1,0:T(1,128)}, u32[]{:S(2)}) copy-start(s32[1,1,128]{2,1,0:T(1,128)} %param.12) | copy-start | bytes 1540
  20.5 4.3 %collective-permute-start.5 = (f32[64,256]{1,0:T(8,128)S(1)}, f32[64,256]{1,0:T(8,128)S(1)}, u32[]{:S(2)}, u32[]{:S(2)}) collective-permute-start(f32[64,256]{1,0:T(8,128)S(1)} %sum_and_update.1), channel_id=1, source_target_pairs={{0,2},{1,3},{2,0},{3,1},{4,6},{5,7},{6,4},{7,5},{8,10},{9,11},{10,... | collective-permute-start | bytes 196616 | tf_op jit(solution)/shard_map/ppermute | solution.py:295
  22.2 7.3 %collective-permute-start.1 = (f32[64,256]{1,0:T(8,128)S(1)}, f32[64,256]{1,0:T(8,128)S(1)}, u32[]{:S(2)}, u32[]{:S(2)}) collective-permute-start(f32[64,256]{1,0:T(8,128)S(1)} %sum_and_update.1), channel_id=1, source_target_pairs={{0,6},{1,7},{2,4},{3,5},{4,2},{5,3},{6,0},{7,1},{8,14},{9,15},{10,... | collective-permute-start | bytes 196616 | tf_op jit(solution)/shard_map/ppermute | solution.py:295
  23.5 7.1 %collective-permute-start = (f32[64,256]{1,0:T(8,128)S(1)}, f32[64,256]{1,0:T(8,128)S(1)}, u32[]{:S(2)}, u32[]{:S(2)}) collective-permute-start(f32[64,256]{1,0:T(8,128)S(1)} %sum_and_update.1), channel_id=1, source_target_pairs={{0,4},{1,5},{2,6},{3,7},{4,0},{5,1},{6,2},{7,3},{8,12},{9,13},{10,... | collective-permute-start | bytes 196616 | tf_op jit(solution)/shard_map/ppermute | solution.py:295
  24.8 6.3 %collective-permute-start.11 = (f32[2,64,256]{2,1,0:T(8,128)S(1)}, f32[2,64,256]{2,1,0:T(8,128)S(1)}, u32[]{:S(2)}, u32[]{:S(2)}) collective-permute-start(f32[2,64,256]{2,1,0:T(8,128)S(1)} %pad_maximum_fusion.1.refs_0_), channel_id=1, source_target_pairs={{0,17},{1,16},{2,19},{3,18},{4,21},{5,20},{6,23},{7,22},{8,25},{9,... | collective-permute-start | bytes 393224 | tf_op jit(solution)/shard_map/ppermute | solution.py:295
  27.6 5.6 %collective-permute-start.9 = (f32[2,64,256]{2,1,0:T(8,128)S(1)}, f32[2,64,256]{2,1,0:T(8,128)S(1)}, u32[]{:S(2)}, u32[]{:S(2)}) collective-permute-start(f32[2,64,256]{2,1,0:T(8,128)S(1)} %pad_maximum_fusion.1.refs_0_), channel_id=1, source_target_pairs={{0,16},{1,17},{2,18},{3,19},{4,20},{5,21},{6,22},{7,23},{8,24},{9,... | collective-permute-start | bytes 393224 | tf_op jit(solution)/shard_map/ppermute | solution.py:295
  29.2 5.8 %collective-permute-start.7 = (f32[2,64,256]{2,1,0:T(8,128)S(1)}, f32[2,64,256]{2,1,0:T(8,128)S(1)}, u32[]{:S(2)}, u32[]{:S(2)}) collective-permute-start(f32[2,64,256]{2,1,0:T(8,128)S(1)} %pad_maximum_fusion.1.refs_0_), channel_id=1, source_target_pairs={{0,1},{1,0},{2,3},{3,2},{4,5},{5,4},{6,7},{7,6},{8,9},{9,8},{10,11... | collective-permute-start | bytes 393224 | tf_op jit(solution)/shard_map/ppermute | solution.py:295
  29.5 7.2 %collective-permute-start.6 = (f32[2,64,256]{2,1,0:T(8,128)S(1)}, f32[2,64,256]{2,1,0:T(8,128)S(1)}, u32[]{:S(2)}, u32[]{:S(2)}) collective-permute-start(f32[2,64,256]{2,1,0:T(8,128)S(1)} %pad_maximum_fusion.1.refs_0_), channel_id=1, source_target_pairs={{0,8},{1,9},{2,10},{3,11},{4,12},{5,13},{6,14},{7,15},{8,0},{9,1},... | collective-permute-start | bytes 393224 | tf_op jit(solution)/shard_map/ppermute | solution.py:295
  30.6 6.2 %collective-permute-start.13 = (f32[2,64,256]{2,1,0:T(8,128)S(1)}, f32[2,64,256]{2,1,0:T(8,128)S(1)}, u32[]{:S(2)}, u32[]{:S(2)}) collective-permute-start(f32[2,64,256]{2,1,0:T(8,128)S(1)} %pad_maximum_fusion.refs_8_), channel_id=1, source_target_pairs={{0,8},{1,9},{2,10},{3,11},{4,12},{5,13},{6,14},{7,15},{8,0},{9,1},... | collective-permute-start | bytes 393224 | tf_op jit(solution)/shard_map/ppermute | solution.py:295
  31.1 5.7 %collective-permute-start.12 = (f32[2,64,256]{2,1,0:T(8,128)S(1)}, f32[2,64,256]{2,1,0:T(8,128)S(1)}, u32[]{:S(2)}, u32[]{:S(2)}) collective-permute-start(f32[2,64,256]{2,1,0:T(8,128)S(1)} %collective-permute-done.11.refs_6_), channel_id=1, source_target_pairs={{0,8},{1,9},{2,10},{3,11},{4,12},{5,13},{6,14},{7,15},{8,0},{9,1},... | collective-permute-start | bytes 393224 | tf_op jit(solution)/shard_map/ppermute | solution.py:295
  33.2 7.6 %collective-permute-start.4 = (f32[2,64,256]{2,1,0:T(8,128)S(1)}, f32[2,64,256]{2,1,0:T(8,128)S(1)}, u32[]{:S(2)}, u32[]{:S(2)}) collective-permute-start(f32[2,64,256]{2,1,0:T(8,128)S(1)} %pad_maximum_fusion.refs_8_), channel_id=1, source_target_pairs={{0,17},{1,16},{2,19},{3,18},{4,21},{5,20},{6,23},{7,22},{8,25},{9,... | collective-permute-start | bytes 393224 | tf_op jit(solution)/shard_map/ppermute | solution.py:295
  35.0 6.5 %collective-permute-start.3 = (f32[2,64,256]{2,1,0:T(8,128)S(1)}, f32[2,64,256]{2,1,0:T(8,128)S(1)}, u32[]{:S(2)}, u32[]{:S(2)}) collective-permute-start(f32[2,64,256]{2,1,0:T(8,128)S(1)} %pad_maximum_fusion.refs_8_), channel_id=1, source_target_pairs={{0,16},{1,17},{2,18},{3,19},{4,20},{5,21},{6,22},{7,23},{8,24},{9,... | collective-permute-start | bytes 393224 | tf_op jit(solution)/shard_map/ppermute | solution.py:295
  36.7 5.8 %collective-permute-start.2 = (f32[2,64,256]{2,1,0:T(8,128)S(1)}, f32[2,64,256]{2,1,0:T(8,128)S(1)}, u32[]{:S(2)}, u32[]{:S(2)}) collective-permute-start(f32[2,64,256]{2,1,0:T(8,128)S(1)} %pad_maximum_fusion.refs_8_), channel_id=1, source_target_pairs={{0,1},{1,0},{2,3},{3,2},{4,5},{5,4},{6,7},{7,6},{8,9},{9,8},{10,11... | collective-permute-start | bytes 393224 | tf_op jit(solution)/shard_map/ppermute | solution.py:295
  36.8 2.8 %collective-permute-start.10 = (f32[2,64,256]{2,1,0:T(8,128)S(1)}, f32[2,64,256]{2,1,0:T(8,128)S(1)}, u32[]{:S(2)}, u32[]{:S(2)}) collective-permute-start(f32[2,64,256]{2,1,0:T(8,128)S(1)} %collective-permute-done.9.refs_4_), channel_id=1, source_target_pairs={{0,8},{1,9},{2,10},{3,11},{4,12},{5,13},{6,14},{7,15},{8,0},{9,1},... | collective-permute-start | bytes 393224 | tf_op jit(solution)/shard_map/ppermute | solution.py:295
  36.8 2.8 %collective-permute-start.8 = (f32[2,64,256]{2,1,0:T(8,128)S(1)}, f32[2,64,256]{2,1,0:T(8,128)S(1)}, u32[]{:S(2)}, u32[]{:S(2)}) collective-permute-start(f32[2,64,256]{2,1,0:T(8,128)S(1)} %collective-permute-done.7.refs_2_), channel_id=1, source_target_pairs={{0,8},{1,9},{2,10},{3,11},{4,12},{5,13},{6,14},{7,15},{8,0},{9,1},... | collective-permute-start | bytes 393224 | tf_op jit(solution)/shard_map/ppermute | solution.py:295
  42.5 1.3 %collective-permute-start.14 = (f32[2,64,256]{2,1,0:T(8,128)S(1)}, f32[2,64,256]{2,1,0:T(8,128)S(1)}, u32[]{:S(2)}, u32[]{:S(2)}) collective-permute-start(f32[2,64,256]{2,1,0:T(8,128)S(1)} %collective-permute-done.2.refs_1_), channel_id=1, source_target_pairs={{0,8},{1,9},{2,10},{3,11},{4,12},{5,13},{6,14},{7,15},{8,0},{9,1},... | collective-permute-start | bytes 393224 | tf_op jit(solution)/shard_map/ppermute | solution.py:295
  42.5 1.5 %collective-permute-start.15 = (f32[2,64,256]{2,1,0:T(8,128)S(1)}, f32[2,64,256]{2,1,0:T(8,128)S(1)}, u32[]{:S(2)}, u32[]{:S(2)}) collective-permute-start(f32[2,64,256]{2,1,0:T(8,128)S(1)} %collective-permute-done.3.refs_3_), channel_id=1, source_target_pairs={{0,8},{1,9},{2,10},{3,11},{4,12},{5,13},{6,14},{7,15},{8,0},{9,1},... | collective-permute-start | bytes 393224 | tf_op jit(solution)/shard_map/ppermute | solution.py:295
  43.0 1.3 %collective-permute-start.16 = (f32[2,64,256]{2,1,0:T(8,128)S(1)}, f32[2,64,256]{2,1,0:T(8,128)S(1)}, u32[]{:S(2)}, u32[]{:S(2)}) collective-permute-start(f32[2,64,256]{2,1,0:T(8,128)S(1)} %collective-permute-done.4.refs_5_), channel_id=1, source_target_pairs={{0,8},{1,9},{2,10},{3,11},{4,12},{5,13},{6,14},{7,15},{8,0},{9,1},... | collective-permute-start | bytes 393224 | tf_op jit(solution)/shard_map/ppermute | solution.py:295

commit v3 on v2

v3 whole, which is shorter than its diff:
```python
import functools
import math

import jax
import jax.numpy as jnp
import ml_dtypes
import numpy as np
from jax import lax
from jax.experimental import pallas as pl
from jax.experimental.pallas import tpu as pltpu
from jax.sharding import PartitionSpec as P

decay_rate = 0.9
step_size = 0.1
LANES = 128
SUB = 8
CORES = 2
MESSAGE_ROWS = 2
EVERY = ("row", "col")
VMEM_BYTES = 48 * 1024 * 1024


def dct_table(order):
    freq = np.arange(order, dtype=np.float64)[:, None]
    place = np.arange(order, dtype=np.float64)[None, :]
    matrix = math.sqrt(2.0 / order) * np.cos(math.pi * (2.0 * place + 1.0) * freq / (2.0 * order))
    return np.where(freq == 0.0, matrix * math.sqrt(0.5), matrix)


def split_table(matrix):
    high = matrix.astype(ml_dtypes.bfloat16)
    low = (matrix - high.astype(np.float64)).astype(ml_dtypes.bfloat16)
    return np.concatenate([high, low, high], axis=1)


def product(table, field):
    high = field.astype(jnp.bfloat16)
    low = (field - high.astype(jnp.float32)).astype(jnp.bfloat16)
    stacked = jnp.concatenate([high, high, low], axis=0)
    return jnp.dot(table, stacked, preferred_element_type=jnp.float32)


def pick_kernel(width, steps, slots_of, *refs):
    sources, out_ref, held, arrived = refs[:6], refs[6], refs[7:13], refs[13]
    table_ref, chosen_ref, counts_ref, common_ref, m_ref, g_ref = held
    order, columns = m_ref.shape
    step = columns // steps
    copies = [
        pltpu.make_async_copy(source, target, arrived.at[n])
        for n, (source, target) in enumerate(zip(sources[:4], held[:4], strict=True))
    ]
    for i in range(steps):
        cut = pl.ds(i * step, step)
        for source, target in zip(sources[4:], held[4:], strict=True):
            copies.append(
                pltpu.make_async_copy(
                    source.at[0, 0, :, cut], target.at[:, cut], arrived.at[len(copies)]
                )
            )
    for copy in copies:
        copy.start()
    for copy in copies[:4]:
        copy.wait()
    chosen = chosen_ref[...]
    common = common_ref[...]
    slots = chosen.shape[0]
    slot = lax.broadcasted_iota(jnp.int32, chosen.shape, 0)
    inside = chosen == common[0:1]
    for q in range(1, common.shape[0]):
        inside = inside | (chosen == common[q : q + 1])
    live = jnp.where(slot < counts_ref[...], chosen, -1)
    rows = jnp.where(inside, live, -1)
    live = jnp.concatenate([live, live], axis=0)
    rows = jnp.concatenate([rows, rows], axis=0)
    share = width // order
    for i in range(steps):
        for copy in copies[4 + 2 * i : 6 + 2 * i]:
            copy.wait()
        for part in range(i * step // width, (i + 1) * step // width):
            cut = pl.ds(part * width, width)
            spectrum = product(table_ref[...], decay_rate * m_ref[:, cut] + g_ref[:, cut])
            for t in range(width // LANES):
                row = block_lanes(live, order, (part * width + t * LANES) // order)
                tile, within = row >> 3, row & 7
                picked = jnp.zeros((SUB, LANES), jnp.float32)
                for r in range(order // SUB):
                    here = spectrum[r * SUB : (r + 1) * SUB, t * LANES : (t + 1) * LANES]
                    here = jnp.take_along_axis(here, within, axis=0)
                    picked = jnp.where(tile == r, here, picked)
                for s in range(0, slots, MESSAGE_ROWS):
                    for to in slots_of[part]:
                        out_ref[to, :, columns_of(width, s, t * LANES)] = picked[
                            s : s + MESSAGE_ROWS
                        ]
            lanes = lax.broadcasted_iota(jnp.int32, (SUB, LANES), 1)
            each = LANES * MESSAGE_ROWS // slots
            numbers = jnp.zeros((MESSAGE_ROWS, LANES), jnp.float32)
            for s in range(0, slots, MESSAGE_ROWS):
                from_s = lanes - s // MESSAGE_ROWS * each
                from_s = part * share + jnp.clip(from_s, 0, share - 1)
                from_s = take_blocks(rows, from_s, part * share)[s : s + MESSAGE_ROWS]
                mine = lanes[:MESSAGE_ROWS] // each == s // MESSAGE_ROWS
                numbers = jnp.where(mine, from_s.astype(jnp.float32), numbers)
            for to in slots_of[part]:
                out_ref[to, :, slots // MESSAGE_ROWS * width :] = numbers


def message_shape(slots, width):
    return MESSAGE_ROWS, slots // MESSAGE_ROWS * width + LANES


def columns_of(width, slot, at):
    first = slot // MESSAGE_ROWS * width + at
    return slice(first, first + LANES)


def take_blocks(rows, lanes, first):
    base = first // LANES * LANES
    return jnp.take_along_axis(rows[:, base : base + LANES], lanes - base, axis=1)


def block_lanes(rows, order, first):
    lanes = first + lax.broadcasted_iota(jnp.int32, (SUB, LANES), 1) // order
    return take_blocks(rows, lanes, first)


def rest_kernel(skipped, start, width, slot_of, *refs):
    back_ref, chosen_ref, counts_ref, sent_ref, m_ref, g_ref, out_ref, held, gone = refs[skipped:]
    order, columns = held.shape
    chosen = chosen_ref[...]
    slots = chosen.shape[0]
    slot = lax.broadcasted_iota(jnp.int32, chosen.shape, 0)
    live = jnp.where(slot < counts_ref[...], chosen, -1)
    live = jnp.concatenate([live, live], axis=0)
    sub = lax.broadcasted_iota(jnp.int32, (SUB, LANES), 0)
    copies = []
    for part in range(columns // width):
        parts = []
        for t in range(width // LANES):
            values = [
                sent_ref[
                    slot_of[start + part],
                    s % MESSAGE_ROWS : s % MESSAGE_ROWS + 1,
                    columns_of(width, s, t * LANES),
                ]
                for s in range(slots)
            ]
            rows = block_lanes(live, order, ((start + part) * width + t * LANES) // order)
            wide = [
                (
                    jnp.broadcast_to(rows[s : s + 1], (SUB, LANES)) - sub,
                    jnp.broadcast_to(values[s], (SUB, LANES)),
                )
                for s in range(slots)
            ]
            tiles = []
            for r in range(order // SUB):
                tile = jnp.zeros((SUB, LANES), jnp.float32)
                for row, value in wide:
                    tile = jnp.where(row == r * SUB, value, tile)
                tiles.append(tile)
            parts.append(jnp.concatenate(tiles, axis=0))
        back = product(back_ref[...], jnp.concatenate(parts, axis=1))
        cut, here = pl.ds((start + part) * width, width), pl.ds(part * width, width)
        held[:, here] = decay_rate * m_ref[0, 0, :, cut] + g_ref[0, 0, :, cut] - back
        copy = pltpu.make_async_copy(held.at[:, here], out_ref.at[0, 0, :, cut], gone.at[part])
        copy.start()
        copies.append(copy)
    for copy in copies:
        copy.wait()


def part_index(sizes, row, col, xor=(0, 0, 0), core_xor=0):
    y_size, z_size, x_size, lines = sizes
    y, core = row // CORES, (row % CORES) ^ core_xor
    z, x = (col // x_size) % lines, col % x_size
    return (((y ^ xor[0]) * CORES + core) * lines + (z ^ xor[1])) * x_size + (x ^ xor[2])


def sum_kernel(sizes, back_ref, got_ref, params_ref, out_ref, held, arrived):
    order, width = out_ref.shape
    me = part_index(sizes, lax.axis_index("row"), lax.axis_index("col"))
    copy = pltpu.make_async_copy(
        params_ref.at[:, pl.ds(pl.multiple_of(me * width, LANES), width)], held, arrived
    )
    copy.start()
    lists = got_ref.shape[0]
    chunks = (got_ref.shape[2] - LANES) // width
    each = LANES // chunks
    numbers = jnp.concatenate([got_ref[n, :, chunks * width :] for n in range(lists)], axis=0)
    numbers = jnp.transpose(numbers)
    freq = lax.broadcasted_iota(jnp.int32, (order, numbers.shape[1]), 0).astype(jnp.float32)
    lane = lax.broadcasted_iota(jnp.int32, (order, LANES), 1)
    pair = LANES // order
    totals = []
    for at in range(0, width, LANES):
        table = [
            jnp.concatenate(
                [
                    (numbers[c * each + block : c * each + block + 1] == freq).astype(jnp.float32)
                    for c in range(chunks)
                ],
                axis=1,
            )
            for block in range(at // order, at // order + pair)
        ]
        table = jnp.concatenate(table, axis=0).astype(jnp.bfloat16)
        values = jnp.concatenate(
            [
                got_ref[n, :, c * width + at : c * width + at + LANES]
                for c in range(chunks)
                for n in range(lists)
            ],
            axis=0,
        )
        high = values.astype(jnp.bfloat16)
        low = (values - high.astype(jnp.float32)).astype(jnp.bfloat16)
        total = jnp.dot(table, high, preferred_element_type=jnp.float32)
        total += jnp.dot(table, low, preferred_element_type=jnp.float32)
        mine = total[:order]
        for p in range(1, pair):
            mine = jnp.where(lane // order == p, total[p * order : (p + 1) * order], mine)
        totals.append(mine)
    update = product(back_ref[...], jnp.concatenate(totals, axis=1))
    copy.wait()
    out_ref[...] = held[...] - step_size * update


def place_kernel(places, sizes, skipped, *refs):
    *pieces, out_ref, sems = refs[skipped:]
    row, col = lax.axis_index("row"), lax.axis_index("col")
    copies = []
    for piece, (other, dy, dx, dz) in zip(pieces, places, strict=True):
        width = piece.shape[-1]
        part = part_index(sizes, row, col, (dy, dz, dx), other)
        copy = pltpu.make_async_copy(
            piece,
            out_ref.at[:, pl.ds(pl.multiple_of(part * width, LANES), width)],
            sems.at[len(copies)],
        )
        copy.start()
        copies.append(copy)
    for copy in copies:
        copy.wait()


def in_hbm(array):
    return pltpu.with_memory_space_constraint(array, pltpu.HBM)


def vmem():
    return pl.BlockSpec(memory_space=pltpu.VMEM)


def limits():
    return pltpu.CompilerParams(vmem_limit_bytes=VMEM_BYTES)


def list_spec(rows, step):
    return pl.BlockSpec((rows, LANES), lambda i: (0, i * step // LANES))


def pick(forward, momentum, gradient, chosen, counts, common, part_of):
    order, columns = momentum.shape[-2:]
    parts = max(part_of) + 1
    slots_of = [[to for to, part in enumerate(part_of) if part == p] for p in range(parts)]
    width = columns // parts
    steps = min(4, parts)
    slots = chosen.shape[0]
    sources = (forward, chosen, counts, common, momentum, gradient)
    held = [pltpu.VMEM(source.shape[-2:], source.dtype) for source in sources]
    return pl.pallas_call(
        functools.partial(pick_kernel, width, steps, slots_of),
        in_specs=[pl.BlockSpec(memory_space=pltpu.HBM)] * len(sources),
        out_specs=vmem(),
        out_shape=jax.ShapeDtypeStruct((len(part_of), *message_shape(slots, width)), jnp.float32),
        scratch_shapes=held + [pltpu.SemaphoreType.DMA((4 + 2 * steps,))],
        compiler_params=limits(),
        name="pick_rows",
    )(*map(in_hbm, sources))


def rest(slot_of, back, sent, momentum, gradient, chosen, counts, first, parts, before):
    order = momentum.shape[-2]
    width = momentum.shape[-1] // len(slot_of)
    anywhere = pl.BlockSpec(memory_space=pl.ANY)
    given = [] if before is None else [before]
    return pl.pallas_call(
        functools.partial(rest_kernel, len(given), first, width, slot_of),
        in_specs=[anywhere] * len(given) + [vmem()] * 6,
        out_specs=anywhere,
        out_shape=jax.ShapeDtypeStruct(momentum.shape, jnp.float32),
        scratch_shapes=[
            pltpu.VMEM((order, parts * width), jnp.float32),
            pltpu.SemaphoreType.DMA((parts,)),
        ],
        input_output_aliases={0: 0} if given else {},
        compiler_params=limits(),
        name="residual",
        cost_estimate=pl.CostEstimate(
            flops=12 * order * order * momentum.shape[-1] * (1 if before is None else 100),
            bytes_accessed=3 * momentum.size * 4 * (1 if before is None else 100),
            transcendentals=0,
        ),
    )(*given, back, chosen, counts, sent, momentum, gradient)


def add_up(sizes, parts, back, got, params):
    order = params.shape[0]
    width = params.shape[1] // parts
    return pl.pallas_call(
        functools.partial(sum_kernel, sizes),
        in_specs=[vmem(), vmem(), pl.BlockSpec(memory_space=pltpu.HBM)],
        out_specs=vmem(),
        out_shape=jax.ShapeDtypeStruct((order, width), jnp.float32),
        scratch_shapes=[pltpu.VMEM((order, width), jnp.float32), pltpu.SemaphoreType.DMA],
        compiler_params=limits(),
        name="sum_and_update",
    )(back, got, in_hbm(params))


def spread(mine, piece, params, sizes):
    y_size, z_size, x_size, lines = sizes

    def swap(array, by):
        pairs = []
        for y in range(y_size):
            for core in range(CORES):
                for z in range(z_size):
                    for x in range(x_size):
                        here = ((y * CORES + core) * z_size + z) * x_size + x
                        there = ((y ^ by[0]) * CORES + (core ^ by[1])) * z_size + (z ^ by[2])
                        pairs.append((here, there * x_size + (x ^ by[3])))
        return lax.ppermute(array, EVERY, pairs)

    far = [(j, i) for j in range(y_size) for i in range(x_size) if j or i]
    far.sort(key=lambda at: sum(map(bool, at)))
    parts = y_size * CORES * lines * x_size
    fill = parts * 15 // 16
    line = [mine] + [swap(mine, (0, 0, j, 0)) for j in range(1, lines)]
    early, late, done, residual = [], [], 0, None
    for n, own in enumerate(line):
        if n:
            residual = piece(done, fill, residual)
            own, residual = lax.optimization_barrier((own, residual))
            done += fill
        early.append((own, 0, 0, n))
        sent = [(swap(own, (j, 0, 0, i)), j, i, n) for j, i in far]
        if n == lines - 1:
            late += sent
        else:
            early += sent
    residual = piece(done, parts - done, residual)

    def other(piece_of):
        return (swap(piece_of[0], (0, 1, 0, 0)), 1, *piece_of[1:])

    near = [piece_of for piece_of in early if not (piece_of[1] or piece_of[2])]
    gone = [piece_of for piece_of in early if piece_of[1] or piece_of[2]]
    first = [(array, 0, *at) for array, *at in early] + [other(piece_of) for piece_of in near]
    partial = place(first, sizes, params, None)
    arrays = [piece_of[0] for piece_of in late]
    arrays, residual, partial = lax.optimization_barrier((arrays, residual, partial))
    late = [(array, *at[1:]) for array, at in zip(arrays, late, strict=True)]
    partial = place([(array, 0, *at) for array, *at in late], sizes, params, partial)
    partial = place([other(piece_of) for piece_of in gone + late], sizes, params, partial)
    return partial, residual


def place(pieces, sizes, params, partial):
    arrays = [piece[0] for piece in pieces]
    places = [piece[1:] for piece in pieces]
    anywhere = pl.BlockSpec(memory_space=pl.ANY)
    given = [] if partial is None else [partial]
    return pl.pallas_call(
        functools.partial(place_kernel, places, sizes, len(given)),
        in_specs=[anywhere] * (len(given) + len(arrays)),
        out_specs=anywhere,
        out_shape=jax.ShapeDtypeStruct(params.shape, jnp.float32),
        scratch_shapes=[pltpu.SemaphoreType.DMA((len(arrays),))],
        input_output_aliases={0: 0} if given else {},
        compiler_params=limits(),
        name="place_columns",
    )(*given, *arrays)


def body(sizes, part_of, params, momentum, gradient, chosen_rows, live_counts, common_rows):
    matrix = dct_table(params.shape[0])
    forward, back = jnp.asarray(split_table(matrix)), jnp.asarray(split_table(matrix.T))
    chosen = jnp.transpose(chosen_rows[0, 0])
    counts = live_counts[0]
    common = jnp.transpose(common_rows[0])
    sent = pick(forward, momentum, gradient, chosen, counts, common, part_of)
    parts = max(part_of) + 1
    slot_of = [part_of.index(part) for part in range(parts)]
    piece = functools.partial(rest, slot_of, back, sent, momentum, gradient, chosen, counts)
    if sizes is not None:
        got = lax.all_to_all(sent, EVERY, 0, 0, tiled=True)
        mine = add_up(sizes, parts, back, got, params)
        new_params, residual = spread(mine, piece, params, sizes)
    else:
        residual = piece(0, parts, None)
        new_params = plain_update(back, sent, params)
    return new_params, residual


def plain_update(back, sent, params):
    order, columns = params.shape
    got = lax.all_to_all(sent, "col", 0, 0, tiled=True)
    got = lax.all_gather(got, "row", axis=0, tiled=True)
    width = columns // sent.shape[0]
    chunks = (got.shape[2] - LANES) // width
    values = got[:, :, : chunks * width].reshape(*got.shape[:2], chunks, width)
    numbers = got[:, :, chunks * width :].reshape(*got.shape[:2], chunks, -1)
    row = jnp.repeat(numbers[..., : width // order].astype(jnp.int32), order, axis=3)
    table = row[..., None, :] == jnp.arange(order, dtype=jnp.int32)[:, None]
    total = jnp.sum(jnp.where(table, values[..., None, :], 0.0), axis=(0, 1, 2))
    total = lax.all_gather(total, "col", axis=1, tiled=True)
    return params - step_size * product(back, total)


def plan(rows, cols, columns):
    side = rows // CORES
    depth = cols // max(side, 1)
    whole = rows == side * CORES and cols == side * depth
    if not whole or any(n < 1 or n & (n - 1) for n in (side, depth)):
        return None
    lines = max(depth // 2, 1)
    while lines > 1 and columns % (side * CORES * lines * side * LANES):
        lines //= 2
    if columns % (side * CORES * lines * side * LANES):
        return None
    return side, depth, side, lines


def solution(mesh):
    rows, cols = mesh.shape["row"], mesh.shape["col"]
    placed = (
        P(),
        P("row", "col", None, None),
        P("row", "col", None, None),
        P("row", "col", None, None),
        P("row", "col", None),
        P("col", None, None),
    )

    def step(params, *rest_of):
        sizes = plan(rows, cols, params.shape[1])
        part_of = list(range(cols))
        if sizes is not None:
            part_of = [part_index(sizes, r, c) for r in range(rows) for c in range(cols)]
        return jax.shard_map(
            functools.partial(body, sizes, part_of),
            mesh=mesh,
            in_specs=placed,
            out_specs=(P(), P("row", "col", None, None)),
            check_vma=False,
        )(params, *rest_of)

    return step
```

time: 45.5 us -> 42 us (0.923)
  starting transfers between devices: 12 us -> 7.54 us
  blocking collectives: 15.7 us -> 18.5 us
  waiting for transfers between devices: 7.31 us -> 5.12 us
    ppermute x17 -> x15, starting transfers between devices: 12 us -> 7.54 us  [swap(): return lax.ppermute(array, EVERY, pairs)]
    all_to_all x1, blocking collectives: 15.7 us -> 18.5 us  [body(): got = lax.all_to_all(sent, EVERY, 0, 0, tiled=True)]
    ppermute x17 -> x15, waiting for transfers between devices: 7.31 us -> 5.12 us  [swap(): return lax.ppermute(array, EVERY, pairs)]
    pallas_call x2 -> x3, Pallas kernels: 2.2 us -> 2.66 us  [place(): pl.pallas_call(functools.partial(place_kernel, places, sizes, len(given))...]
  transfers between devices with their start and end apart: 17 -> 15, of which waited for: 9 -> 6; matrix products, arithmetic and copies ran while one was open for 0% -> 0% of each run, Pallas kernels for 10% -> 12%
where the time goes in v3:
time: 42 us; the launch traced here: 41.8 us
  blocking collectives  18.5 us (44%)
  Pallas kernels  9.81 us (23%)
  starting transfers between devices  7.54 us (18%)
  waiting for transfers between devices  5.12 us (12%)
  between operations  0.78 us (2%)
    all_to_all x1, blocking collectives, body(): got = lax.all_to_all(sent, EVERY, 0, 0, tiled=True)  18.5 us
    ppermute x15, starting transfers between devices, swap(): return lax.ppermute(array, EVERY, pairs)  7.54 us
    ppermute x15, waiting for transfers between devices, swap(): return lax.ppermute(array, EVERY, pairs)  5.12 us
    pallas_call x2, Pallas kernels, rest(): pl.pallas_call(functools.partial(rest_kernel, len(given), first, width, s...  3.08 us
    pallas_call x1, Pallas kernels, pick(): pl.pallas_call(functools.partial(pick_kernel, width, steps, slots_of), in...  2.74 us
    pallas_call x3, Pallas kernels, place(): pl.pallas_call(functools.partial(place_kernel, places, sizes, len(given))...  2.66 us
    pallas_call x1, Pallas kernels, add_up(): pl.pallas_call(functools.partial(sum_kernel, sizes), in_specs=[vmem(), vm...  1.33 us
  transfers between devices with their start and end apart: 15, of which 6 were waited for; matrix products, arithmetic and copies ran while one was open for 0% of the time, Pallas kernels for 12%

profile of v3, /device:TPU:0, one launch (start us, length us, event | category | flops | bytes accessed | tf_op | source)
XLA Modules:
  0.0 41.8 jit_solution(2104751683269894719)
XLA Ops:
  0.7 2.7 %pick_rows.1.refs_3_.refs_4_ = f32[32,2,1152]{2,1,0:T(2,128)S(1)} custom-call(bf16[64,192]{1,0:T(8,128)(2,1)} %constant.4.clone.refs_0_, s32[4,128]{1,0:T(4,128)} %bitcast.7, s32[1,128]{1,0:T(1,128)} %bitcast.10, s32[8,128]{1,0:T(8,128)} %bitcast.13, f32[1,1,64,8192]{3,2,1,0:T(8,128)} %refs_5_.5, f32[1,1,64,8192]{3,2,1,0:T(8,128)} %refs_6_.1), custom_call_target="tpu_custom_call" | custom-call | tf_op jit(solution)/shard_map/pick_rows/pallas_call | solution.py:272
  3.4 18.5 %all_to_all.5.got_ref = f32[32,2,1152]{2,1,0:T(2,128)S(1)} all-to-all(f32[32,2,1152]{2,1,0:T(2,128)S(1)} %pick_rows.1.refs_3_.refs_4_), channel_id=1, replica_groups=mesh['row'=4,'col'=8] {'row','col'}, dimensions={0} | all-to-all | bytes 589824 | tf_op jit(solution)/shard_map/all_to_all | solution.py:398
  22.0 1.3 %sum_and_update.1.refs_0_ = f32[64,512]{1,0:T(8,128)S(1)} custom-call(bf16[64,192]{1,0:T(8,128)(2,1)S(1)} %copy-done.2, f32[32,2,1152]{2,1,0:T(2,128)S(1)} %all_to_all.5.got_ref, f32[64,8192]{1,0:T(8,128)} %params_ref.1), custom_call_target="tpu_custom_call" | custom-call | tf_op jit(solution)/shard_map/sum_and_update/pallas_call | solution.py:311
  23.3 0.9 %collective-permute-start = (f32[64,512]{1,0:T(8,128)S(1)}, f32[64,512]{1,0:T(8,128)S(1)}, u32[]{:S(2)}, u32[]{:S(2)}) collective-permute-start(f32[64,512]{1,0:T(8,128)S(1)} %sum_and_update.1.refs_0_), channel_id=1, source_target_pairs={{0,2},{1,3},{2,0},{3,1},{4,6},{5,7},{6,4},{7,5},{8,10},{9,11},{10,... | collective-permute-start | bytes 393224 | tf_op jit(solution)/shard_map/ppermute | solution.py:334
  24.2 0.5 %collective-permute-start.6 = (f32[64,512]{1,0:T(8,128)S(1)}, f32[64,512]{1,0:T(8,128)S(1)}, u32[]{:S(2)}, u32[]{:S(2)}) collective-permute-start(f32[64,512]{1,0:T(8,128)S(1)} %sum_and_update.1.refs_0_), channel_id=1, source_target_pairs={{0,17},{1,16},{2,19},{3,18},{4,21},{5,20},{6,23},{7,22},{8,25},{9,... | collective-permute-start | bytes 393224 | tf_op jit(solution)/shard_map/ppermute | solution.py:334
  24.8 1.2 %collective-permute-start.5 = (f32[64,512]{1,0:T(8,128)S(1)}, f32[64,512]{1,0:T(8,128)S(1)}, u32[]{:S(2)}, u32[]{:S(2)}) collective-permute-start(f32[64,512]{1,0:T(8,128)S(1)} %sum_and_update.1.refs_0_), channel_id=1, source_target_pairs={{0,16},{1,17},{2,18},{3,19},{4,20},{5,21},{6,22},{7,23},{8,24},{9,... | collective-permute-start | bytes 393224 | tf_op jit(solution)/shard_map/ppermute | solution.py:334
  26.0 1.8 %collective-permute-start.4 = (f32[64,512]{1,0:T(8,128)S(1)}, f32[64,512]{1,0:T(8,128)S(1)}, u32[]{:S(2)}, u32[]{:S(2)}) collective-permute-start(f32[64,512]{1,0:T(8,128)S(1)} %sum_and_update.1.refs_0_), channel_id=1, source_target_pairs={{0,1},{1,0},{2,3},{3,2},{4,5},{5,4},{6,7},{7,6},{8,9},{9,8},{10,11... | collective-permute-start | bytes 393224 | tf_op jit(solution)/shard_map/ppermute | solution.py:334
  27.7 2.1 %residual.2.refs_0_ = f32[1,1,64,8192]{3,2,1,0:T(8,128)} custom-call(bf16[64,192]{1,0:T(8,128)(2,1)S(1)} %copy-done.2, s32[4,128]{1,0:T(4,128)S(1)} %bitcast.8, s32[1,128]{1,0:T(1,128)S(1)} %bitcast.11, f32[32,2,1152]{2,1,0:T(2,128)S(1)} %pick_rows.1.refs_3_.refs_4_, f32[1,1,64,8192]{3,2,1,0:T(8,128)S(1)} %copy-done, f32[1,1,64,8192]{3,2,1,0:T(8,128)S(1)} %copy-done.1), custom_call_target="tpu_custom_call" | custom-call | flops 402653184 | bytes 6291456 | tf_op jit(solution)/shard_map/residual/pallas_call | solution.py:288
  29.9 0.1 collective-permute-start.8
  30.0 0.6 %collective-permute-start.3 = (f32[64,512]{1,0:T(8,128)S(1)}, f32[64,512]{1,0:T(8,128)S(1)}, u32[]{:S(2)}, u32[]{:S(2)}) collective-permute-start(f32[64,512]{1,0:T(8,128)S(1)} %collective-permute-done.refs_4_), channel_id=1, source_target_pairs={{0,17},{1,16},{2,19},{3,18},{4,21},{5,20},{6,23},{7,22},{8,25},{9,... | collective-permute-start | bytes 393224 | tf_op jit(solution)/shard_map/ppermute | solution.py:334
  30.6 0.9 %collective-permute-done.6.refs_3_ = f32[64,512]{1,0:T(8,128)S(1)} collective-permute-done((f32[64,512]{1,0:T(8,128)S(1)}, f32[64,512]{1,0:T(8,128)S(1)}, u32[]{:S(2)}, u32[]{:S(2)}) %collective-permute-start.6) | collective-permute-done | bytes 131104 | tf_op jit(solution)/shard_map/ppermute | solution.py:334
  31.5 0.5 %collective-permute-start.2 = (f32[64,512]{1,0:T(8,128)S(1)}, f32[64,512]{1,0:T(8,128)S(1)}, u32[]{:S(2)}, u32[]{:S(2)}) collective-permute-start(f32[64,512]{1,0:T(8,128)S(1)} %collective-permute-done.refs_4_), channel_id=1, source_target_pairs={{0,16},{1,17},{2,18},{3,19},{4,20},{5,21},{6,22},{7,23},{8,24},{9,... | collective-permute-start | bytes 393224 | tf_op jit(solution)/shard_map/ppermute | solution.py:334
  32.0 1.2 %collective-permute-done.5.refs_2_ = f32[64,512]{1,0:T(8,128)S(1)} collective-permute-done((f32[64,512]{1,0:T(8,128)S(1)}, f32[64,512]{1,0:T(8,128)S(1)}, u32[]{:S(2)}, u32[]{:S(2)}) %collective-permute-start.5) | collective-permute-done | bytes 131104 | tf_op jit(solution)/shard_map/ppermute | solution.py:334
  33.2 0.8 %collective-permute-start.1 = (f32[64,512]{1,0:T(8,128)S(1)}, f32[64,512]{1,0:T(8,128)S(1)}, u32[]{:S(2)}, u32[]{:S(2)}) collective-permute-start(f32[64,512]{1,0:T(8,128)S(1)} %collective-permute-done.refs_4_), channel_id=1, source_target_pairs={{0,1},{1,0},{2,3},{3,2},{4,5},{5,4},{6,7},{7,6},{8,9},{9,8},{10,11... | collective-permute-start | bytes 393224 | tf_op jit(solution)/shard_map/ppermute | solution.py:334
  34.1 0.9 %residual.3 = f32[1,1,64,8192]{3,2,1,0:T(8,128)} custom-call(f32[1,1,64,8192]{3,2,1,0:T(8,128)} %residual.2.refs_0_, bf16[64,192]{1,0:T(8,128)(2,1)S(1)} %copy-done.2, s32[4,128]{1,0:T(4,128)S(1)} %bitcast.9, s32[1,128]{1,0:T(1,128)S(1)} %bitcast.12, f32[32,2,1152]{2,1,0:T(2,128)S(1)} %pick_rows.1.refs_3_.refs_4_, ...), custom_call_target="tpu_custom_call", output_to_operand_aliasing={{}: (0, {})} | custom-call | flops 40265318400 | bytes 629145600 | tf_op jit(solution)/shard_map/residual/pallas_call | solution.py:288
  35.0 0.6 %collective-permute-start.10 = (f32[64,512]{1,0:T(8,128)S(1)}, f32[64,512]{1,0:T(8,128)S(1)}, u32[]{:S(2)}, u32[]{:S(2)}) collective-permute-start(f32[64,512]{1,0:T(8,128)S(1)} %collective-permute-done.5.refs_2_), channel_id=1, source_target_pairs={{0,8},{1,9},{2,10},{3,11},{4,12},{5,13},{6,14},{7,15},{8,0},{9,1},... | collective-permute-start | bytes 393224 | tf_op jit(solution)/shard_map/ppermute | solution.py:334
  35.6 1.0 %place_columns.3.refs_0_ = f32[64,8192]{1,0:T(8,128)} custom-call(f32[64,512]{1,0:T(8,128)S(1)} %sum_and_update.1.refs_0_, f32[64,512]{1,0:T(8,128)S(1)} %collective-permute-done.4.refs_1_, f32[64,512]{1,0:T(8,128)S(1)} %collective-permute-done.5.refs_2_, f32[64,512]{1,0:T(8,128)S(1)} %collective-permute-done.6.refs_3_, ...), custom_call_target="tpu_custom_call" | custom-call | tf_op jit(solution)/shard_map/place_columns/pallas_call | solution.py:375
  36.6 0.7 %collective-permute-done.3.refs_3_ = f32[64,512]{1,0:T(8,128)S(1)} collective-permute-done((f32[64,512]{1,0:T(8,128)S(1)}, f32[64,512]{1,0:T(8,128)S(1)}, u32[]{:S(2)}, u32[]{:S(2)}) %collective-permute-start.3) | collective-permute-done | bytes 131104 | tf_op jit(solution)/shard_map/ppermute | solution.py:334
  37.3 1.7 %collective-permute-done.2.refs_2_ = f32[64,512]{1,0:T(8,128)S(1)} collective-permute-done((f32[64,512]{1,0:T(8,128)S(1)}, f32[64,512]{1,0:T(8,128)S(1)}, u32[]{:S(2)}, u32[]{:S(2)}) %collective-permute-start.2) | collective-permute-done | bytes 131104 | tf_op jit(solution)/shard_map/ppermute | solution.py:334
  39.0 0.5 %collective-permute-start.13 = (f32[64,512]{1,0:T(8,128)S(1)}, f32[64,512]{1,0:T(8,128)S(1)}, u32[]{:S(2)}, u32[]{:S(2)}) collective-permute-start(f32[64,512]{1,0:T(8,128)S(1)} %collective-permute-done.2.refs_2_), channel_id=1, source_target_pairs={{0,8},{1,9},{2,10},{3,11},{4,12},{5,13},{6,14},{7,15},{8,0},{9,1},... | collective-permute-start | bytes 393224 | tf_op jit(solution)/shard_map/ppermute | solution.py:334
  39.5 0.8 %place_columns.4.refs_0_ = f32[64,8192]{1,0:T(8,128)} custom-call(f32[64,8192]{1,0:T(8,128)} %place_columns.3.refs_0_, f32[64,512]{1,0:T(8,128)S(1)} %collective-permute-done.1.refs_1_, f32[64,512]{1,0:T(8,128)S(1)} %collective-permute-done.2.refs_2_, f32[64,512]{1,0:T(8,128)S(1)} %collective-permute-done.3.refs_3_), custom_call_target="tpu_custom_call", output_to_operand_aliasing={{}: (0, {})} | custom-call | tf_op jit(solution)/shard_map/place_columns/pallas_call | solution.py:375
  40.4 0.2 collective-permute-done.13.refs_5_
  40.6 0.3 collective-permute-done.14.refs_6_
  40.9 0.9 %place_columns.5 = f32[64,8192]{1,0:T(8,128)} custom-call(f32[64,8192]{1,0:T(8,128)} %place_columns.4.refs_0_, f32[64,512]{1,0:T(8,128)S(1)} %collective-permute-done.9.refs_1_, f32[64,512]{1,0:T(8,128)S(1)} %collective-permute-done.10.refs_2_, f32[64,512]{1,0:T(8,128)S(1)} %collective-permute-done.11.refs_3_, ...), custom_call_target="tpu_custom_call", output_to_operand_aliasing={{}: (0, {})} | custom-call | tf_op jit(solution)/shard_map/place_columns/pallas_call | solution.py:375
  (24 shorter events, 0.1 us)
Async XLA Ops:
  0.6 21.4 %copy-start.2 = (bf16[64,192]{1,0:T(8,128)(2,1)S(1)}, bf16[64,192]{1,0:T(8,128)(2,1)}, u32[]{:S(2)}) copy-start(bf16[64,192]{1,0:T(8,128)(2,1)} %constant.5.clone.back_ref.refs_0_.refs_1_) | copy-start | bytes 73732
  0.6 27.1 %copy-start.1 = (f32[1,1,64,8192]{3,2,1,0:T(8,128)S(1)}, f32[1,1,64,8192]{3,2,1,0:T(8,128)}, u32[]{:S(2)}) copy-start(f32[1,1,64,8192]{3,2,1,0:T(8,128)} %refs_6_.1) | copy-start | bytes 6291460
  3.4 24.3 %copy-start = (f32[1,1,64,8192]{3,2,1,0:T(8,128)S(1)}, f32[1,1,64,8192]{3,2,1,0:T(8,128)}, u32[]{:S(2)}) copy-start(f32[1,1,64,8192]{3,2,1,0:T(8,128)} %refs_5_.5) | copy-start | bytes 6291460
  3.4 24.3 %copy-start.3 = (s32[1,1,128,4]{2,3,1,0:T(4,128)S(1)}, s32[1,1,128,4]{2,3,1,0:T(4,128)}, u32[]{:S(2)}) copy-start(s32[1,1,128,4]{2,3,1,0:T(4,128)} %param.11) | copy-start | bytes 6148
  3.4 24.3 %copy-start.4 = (s32[1,1,128]{2,1,0:T(1,128)S(1)}, s32[1,1,128]{2,1,0:T(1,128)}, u32[]{:S(2)}) copy-start(s32[1,1,128]{2,1,0:T(1,128)} %param.12) | copy-start | bytes 1540
  23.3 6.6 %collective-permute-start = (f32[64,512]{1,0:T(8,128)S(1)}, f32[64,512]{1,0:T(8,128)S(1)}, u32[]{:S(2)}, u32[]{:S(2)}) collective-permute-start(f32[64,512]{1,0:T(8,128)S(1)} %sum_and_update.1.refs_0_), channel_id=1, source_target_pairs={{0,2},{1,3},{2,0},{3,1},{4,6},{5,7},{6,4},{7,5},{8,10},{9,11},{10,... | collective-permute-start | bytes 393224 | tf_op jit(solution)/shard_map/ppermute | solution.py:334
  24.2 5.7 %collective-permute-start.7 = (f32[64,512]{1,0:T(8,128)S(1)}, f32[64,512]{1,0:T(8,128)S(1)}, u32[]{:S(2)}, u32[]{:S(2)}) collective-permute-start(f32[64,512]{1,0:T(8,128)S(1)} %sum_and_update.1.refs_0_), channel_id=1, source_target_pairs={{0,8},{1,9},{2,10},{3,11},{4,12},{5,13},{6,14},{7,15},{8,0},{9,1},... | collective-permute-start | bytes 393224 | tf_op jit(solution)/shard_map/ppermute | solution.py:334
  24.2 7.2 %collective-permute-start.6 = (f32[64,512]{1,0:T(8,128)S(1)}, f32[64,512]{1,0:T(8,128)S(1)}, u32[]{:S(2)}, u32[]{:S(2)}) collective-permute-start(f32[64,512]{1,0:T(8,128)S(1)} %sum_and_update.1.refs_0_), channel_id=1, source_target_pairs={{0,17},{1,16},{2,19},{3,18},{4,21},{5,20},{6,23},{7,22},{8,25},{9,... | collective-permute-start | bytes 393224 | tf_op jit(solution)/shard_map/ppermute | solution.py:334
  24.8 8.4 %collective-permute-start.5 = (f32[64,512]{1,0:T(8,128)S(1)}, f32[64,512]{1,0:T(8,128)S(1)}, u32[]{:S(2)}, u32[]{:S(2)}) collective-permute-start(f32[64,512]{1,0:T(8,128)S(1)} %sum_and_update.1.refs_0_), channel_id=1, source_target_pairs={{0,16},{1,17},{2,18},{3,19},{4,20},{5,21},{6,22},{7,23},{8,24},{9,... | collective-permute-start | bytes 393224 | tf_op jit(solution)/shard_map/ppermute | solution.py:334
  26.0 8.1 %collective-permute-start.4 = (f32[64,512]{1,0:T(8,128)S(1)}, f32[64,512]{1,0:T(8,128)S(1)}, u32[]{:S(2)}, u32[]{:S(2)}) collective-permute-start(f32[64,512]{1,0:T(8,128)S(1)} %sum_and_update.1.refs_0_), channel_id=1, source_target_pairs={{0,1},{1,0},{2,3},{3,2},{4,5},{5,4},{6,7},{7,6},{8,9},{9,8},{10,11... | collective-permute-start | bytes 393224 | tf_op jit(solution)/shard_map/ppermute | solution.py:334
  29.9 5.1 %collective-permute-start.8 = (f32[64,512]{1,0:T(8,128)S(1)}, f32[64,512]{1,0:T(8,128)S(1)}, u32[]{:S(2)}, u32[]{:S(2)}) collective-permute-start(f32[64,512]{1,0:T(8,128)S(1)} %collective-permute-done.refs_4_), channel_id=1, source_target_pairs={{0,8},{1,9},{2,10},{3,11},{4,12},{5,13},{6,14},{7,15},{8,0},{9,1},... | collective-permute-start | bytes 393224 | tf_op jit(solution)/shard_map/ppermute | solution.py:334
  30.0 7.3 %collective-permute-start.3 = (f32[64,512]{1,0:T(8,128)S(1)}, f32[64,512]{1,0:T(8,128)S(1)}, u32[]{:S(2)}, u32[]{:S(2)}) collective-permute-start(f32[64,512]{1,0:T(8,128)S(1)} %collective-permute-done.refs_4_), channel_id=1, source_target_pairs={{0,17},{1,16},{2,19},{3,18},{4,21},{5,20},{6,23},{7,22},{8,25},{9,... | collective-permute-start | bytes 393224 | tf_op jit(solution)/shard_map/ppermute | solution.py:334
  31.5 7.6 %collective-permute-start.2 = (f32[64,512]{1,0:T(8,128)S(1)}, f32[64,512]{1,0:T(8,128)S(1)}, u32[]{:S(2)}, u32[]{:S(2)}) collective-permute-start(f32[64,512]{1,0:T(8,128)S(1)} %collective-permute-done.refs_4_), channel_id=1, source_target_pairs={{0,16},{1,17},{2,18},{3,19},{4,20},{5,21},{6,22},{7,23},{8,24},{9,... | collective-permute-start | bytes 393224 | tf_op jit(solution)/shard_map/ppermute | solution.py:334
  33.2 5.8 %collective-permute-start.1 = (f32[64,512]{1,0:T(8,128)S(1)}, f32[64,512]{1,0:T(8,128)S(1)}, u32[]{:S(2)}, u32[]{:S(2)}) collective-permute-start(f32[64,512]{1,0:T(8,128)S(1)} %collective-permute-done.refs_4_), channel_id=1, source_target_pairs={{0,1},{1,0},{2,3},{3,2},{4,5},{5,4},{6,7},{7,6},{8,9},{9,8},{10,11... | collective-permute-start | bytes 393224 | tf_op jit(solution)/shard_map/ppermute | solution.py:334
  34.1 5.5 %collective-permute-start.11 = (f32[64,512]{1,0:T(8,128)S(1)}, f32[64,512]{1,0:T(8,128)S(1)}, u32[]{:S(2)}, u32[]{:S(2)}) collective-permute-start(f32[64,512]{1,0:T(8,128)S(1)} %collective-permute-done.6.refs_3_), channel_id=1, source_target_pairs={{0,8},{1,9},{2,10},{3,11},{4,12},{5,13},{6,14},{7,15},{8,0},{9,1},... | collective-permute-start | bytes 393224 | tf_op jit(solution)/shard_map/ppermute | solution.py:334
  35.0 5.3 %collective-permute-start.10 = (f32[64,512]{1,0:T(8,128)S(1)}, f32[64,512]{1,0:T(8,128)S(1)}, u32[]{:S(2)}, u32[]{:S(2)}) collective-permute-start(f32[64,512]{1,0:T(8,128)S(1)} %collective-permute-done.5.refs_2_), channel_id=1, source_target_pairs={{0,8},{1,9},{2,10},{3,11},{4,12},{5,13},{6,14},{7,15},{8,0},{9,1},... | collective-permute-start | bytes 393224 | tf_op jit(solution)/shard_map/ppermute | solution.py:334
  37.3 3.0 %collective-permute-start.9 = (f32[64,512]{1,0:T(8,128)S(1)}, f32[64,512]{1,0:T(8,128)S(1)}, u32[]{:S(2)}, u32[]{:S(2)}) collective-permute-start(f32[64,512]{1,0:T(8,128)S(1)} %collective-permute-done.4.refs_1_), channel_id=1, source_target_pairs={{0,8},{1,9},{2,10},{3,11},{4,12},{5,13},{6,14},{7,15},{8,0},{9,1},... | collective-permute-start | bytes 393224 | tf_op jit(solution)/shard_map/ppermute | solution.py:334
  39.0 1.3 %collective-permute-start.12 = (f32[64,512]{1,0:T(8,128)S(1)}, f32[64,512]{1,0:T(8,128)S(1)}, u32[]{:S(2)}, u32[]{:S(2)}) collective-permute-start(f32[64,512]{1,0:T(8,128)S(1)} %collective-permute-done.1.refs_1_), channel_id=1, source_target_pairs={{0,8},{1,9},{2,10},{3,11},{4,12},{5,13},{6,14},{7,15},{8,0},{9,1},... | collective-permute-start | bytes 393224 | tf_op jit(solution)/shard_map/ppermute | solution.py:334
  39.0 1.5 %collective-permute-start.13 = (f32[64,512]{1,0:T(8,128)S(1)}, f32[64,512]{1,0:T(8,128)S(1)}, u32[]{:S(2)}, u32[]{:S(2)}) collective-permute-start(f32[64,512]{1,0:T(8,128)S(1)} %collective-permute-done.2.refs_2_), channel_id=1, source_target_pairs={{0,8},{1,9},{2,10},{3,11},{4,12},{5,13},{6,14},{7,15},{8,0},{9,1},... | collective-permute-start | bytes 393224 | tf_op jit(solution)/shard_map/ppermute | solution.py:334
  39.5 1.3 %collective-permute-start.14 = (f32[64,512]{1,0:T(8,128)S(1)}, f32[64,512]{1,0:T(8,128)S(1)}, u32[]{:S(2)}, u32[]{:S(2)}) collective-permute-start(f32[64,512]{1,0:T(8,128)S(1)} %collective-permute-done.3.refs_3_), channel_id=1, source_target_pairs={{0,8},{1,9},{2,10},{3,11},{4,12},{5,13},{6,14},{7,15},{8,0},{9,1},... | collective-permute-start | bytes 393224 | tf_op jit(solution)/shard_map/ppermute | solution.py:334

commit v4 on v3

--- a/solution.py
+++ b/solution.py
@@ -336,34 +336,40 @@
     far = [(j, i) for j in range(y_size) for i in range(x_size) if j or i]
     far.sort(key=lambda at: sum(map(bool, at)))
     parts = y_size * CORES * lines * x_size
-    fill = parts * 15 // 16
+    fill = parts * 12 // 16
     line = [mine] + [swap(mine, (0, 0, j, 0)) for j in range(1, lines)]
-    early, late, done, residual = [], [], 0, None
-    for n, own in enumerate(line):
-        if n:
-            residual = piece(done, fill, residual)
-            own, residual = lax.optimization_barrier((own, residual))
-            done += fill
-        early.append((own, 0, 0, n))
-        sent = [(swap(own, (j, 0, 0, i)), j, i, n) for j, i in far]
-        if n == lines - 1:
-            late += sent
-        else:
-            early += sent
-    residual = piece(done, parts - done, residual)
-
     def other(piece_of):
         return (swap(piece_of[0], (0, 1, 0, 0)), 1, *piece_of[1:])
 
-    near = [piece_of for piece_of in early if not (piece_of[1] or piece_of[2])]
-    gone = [piece_of for piece_of in early if piece_of[1] or piece_of[2]]
-    first = [(array, 0, *at) for array, *at in early] + [other(piece_of) for piece_of in near]
+    corners = [(j, i) for j, i in far if j and i]
+    sides = [(j, i) for j, i in far if not (j and i)]
+    near = [(own, 0, 0, n) for n, own in enumerate(line)]
+    begun = [(swap(mine, (j, 0, 0, i)), j, i, 0) for j, i in corners]
+    theirs = [other(near[0])]
+    held, theirs_first = lax.optimization_barrier((mine, theirs[0][0]))
+    theirs = [(theirs_first, *theirs[0][1:])]
+    gone = begun + [(swap(held, (j, 0, 0, i)), j, i, 0) for j, i in sides]
+    late, done, residual = [], 0, None
+    for n, own in enumerate(line[1:], 1):
+        residual = piece(done, fill, residual)
+        own, residual = lax.optimization_barrier((own, residual))
+        done += fill
+        near[n] = (own, 0, 0, n)
+        late += [(swap(own, (j, 0, 0, i)), j, i, n) for j, i in sides]
+        late += [(swap(array, (0, 0, n, 0)), j, i, n) for array, j, i, _ in begun]
+    residual = piece(done, parts - done, residual)
+    waiting = near[1:] + gone
+    arrays, residual = lax.optimization_barrier(([piece_of[0] for piece_of in waiting], residual))
+    waiting = [(array, *at[1:]) for array, at in zip(arrays, waiting, strict=True)]
+    first = [(array, 0, *at) for array, *at in near[:1] + waiting] + theirs
     partial = place(first, sizes, params, None)
+    theirs = [other(piece_of) for piece_of in waiting]
     arrays = [piece_of[0] for piece_of in late]
-    arrays, residual, partial = lax.optimization_barrier((arrays, residual, partial))
+    arrays, partial = lax.optimization_barrier((arrays, partial))
     late = [(array, *at[1:]) for array, at in zip(arrays, late, strict=True)]
-    partial = place([(array, 0, *at) for array, *at in late], sizes, params, partial)
-    partial = place([other(piece_of) for piece_of in gone + late], sizes, params, partial)
+    second = [(array, 0, *at) for array, *at in late] + theirs
+    partial = place(second, sizes, params, partial)
+    partial = place([other(piece_of) for piece_of in late], sizes, params, partial)
     return partial, residual
 
 

time: 42 us -> 39.7 us (0.945)
  waiting for transfers between devices: 5.12 us -> 1.67 us
  starting transfers between devices: 7.54 us -> 8.72 us
    ppermute x15, waiting for transfers between devices: 5.12 us -> 1.67 us  [swap(): return lax.ppermute(array, EVERY, pairs)]
    ppermute x15, starting transfers between devices: 7.54 us -> 8.72 us  [swap(): return lax.ppermute(array, EVERY, pairs)]
  transfers between devices with their start and end apart: 15 -> 15, of which waited for: 6 -> 4; matrix products, arithmetic and copies ran while one was open for 0% -> 0% of each run, Pallas kernels for 12% -> 12%
where the time goes in v4:
time: 39.7 us; the launch traced here: 39.5 us
  blocking collectives  18.5 us (47%)
  Pallas kernels  9.81 us (25%)
  starting transfers between devices  8.72 us (22%)
  waiting for transfers between devices  1.67 us (4%)
  between operations  0.78 us (2%)
    all_to_all x1, blocking collectives, body(): got = lax.all_to_all(sent, EVERY, 0, 0, tiled=True)  18.5 us
    ppermute x15, starting transfers between devices, swap(): return lax.ppermute(array, EVERY, pairs)  8.72 us
    pallas_call x2, Pallas kernels, rest(): pl.pallas_call(functools.partial(rest_kernel, len(given), first, width, s...  3.04 us
    pallas_call x1, Pallas kernels, pick(): pl.pallas_call(functools.partial(pick_kernel, width, steps, slots_of), in...  2.74 us
    pallas_call x3, Pallas kernels, place(): pl.pallas_call(functools.partial(place_kernel, places, sizes, len(given))...  2.69 us
    ppermute x15, waiting for transfers between devices, swap(): return lax.ppermute(array, EVERY, pairs)  1.67 us
    pallas_call x1, Pallas kernels, add_up(): pl.pallas_call(functools.partial(sum_kernel, sizes), in_specs=[vmem(), vm...  1.33 us
  transfers between devices with their start and end apart: 15, of which 4 were waited for; matrix products, arithmetic and copies ran while one was open for 0% of the time, Pallas kernels for 12%

profile of v4, /device:TPU:0, one launch (start us, length us, event | category | flops | bytes accessed | tf_op | source)
XLA Modules:
  0.0 39.5 jit_solution(17807470920828833797)
XLA Ops:
  0.7 2.7 %pick_rows.1.refs_3_.refs_4_ = f32[32,2,1152]{2,1,0:T(2,128)S(1)} custom-call(bf16[64,192]{1,0:T(8,128)(2,1)} %constant.4.clone.refs_0_, s32[4,128]{1,0:T(4,128)} %bitcast.7, s32[1,128]{1,0:T(1,128)} %bitcast.10, s32[8,128]{1,0:T(8,128)} %bitcast.13, f32[1,1,64,8192]{3,2,1,0:T(8,128)} %refs_5_.5, f32[1,1,64,8192]{3,2,1,0:T(8,128)} %refs_6_.1), custom_call_target="tpu_custom_call" | custom-call | tf_op jit(solution)/shard_map/pick_rows/pallas_call | solution.py:272
  3.4 18.5 %all_to_all.5.got_ref = f32[32,2,1152]{2,1,0:T(2,128)S(1)} all-to-all(f32[32,2,1152]{2,1,0:T(2,128)S(1)} %pick_rows.1.refs_3_.refs_4_), channel_id=1, replica_groups=mesh['row'=4,'col'=8] {'row','col'}, dimensions={0} | all-to-all | bytes 589824 | tf_op jit(solution)/shard_map/all_to_all | solution.py:404
  22.0 1.3 %sum_and_update.1.refs_0_ = f32[64,512]{1,0:T(8,128)S(1)} custom-call(bf16[64,192]{1,0:T(8,128)(2,1)S(1)} %copy-done.2, f32[32,2,1152]{2,1,0:T(2,128)S(1)} %all_to_all.5.got_ref, f32[64,8192]{1,0:T(8,128)} %params_ref.1), custom_call_target="tpu_custom_call" | custom-call | tf_op jit(solution)/shard_map/sum_and_update/pallas_call | solution.py:311
  23.3 0.1 collective-permute-start.5
  23.4 1.0 %collective-permute-start = (f32[64,512]{1,0:T(8,128)S(1)}, f32[64,512]{1,0:T(8,128)S(1)}, u32[]{:S(2)}, u32[]{:S(2)}) collective-permute-start(f32[64,512]{1,0:T(8,128)S(1)} %sum_and_update.1.refs_0_), channel_id=1, source_target_pairs={{0,2},{1,3},{2,0},{3,1},{4,6},{5,7},{6,4},{7,5},{8,10},{9,11},{10,... | collective-permute-start | bytes 393224 | tf_op jit(solution)/shard_map/ppermute | solution.py:334
  24.4 0.5 %collective-permute-start.3 = (f32[64,512]{1,0:T(8,128)S(1)}, f32[64,512]{1,0:T(8,128)S(1)}, u32[]{:S(2)}, u32[]{:S(2)}) collective-permute-start(f32[64,512]{1,0:T(8,128)S(1)} %sum_and_update.1.refs_0_), channel_id=1, source_target_pairs={{0,17},{1,16},{2,19},{3,18},{4,21},{5,20},{6,23},{7,22},{8,25},{9,... | collective-permute-start | bytes 393224 | tf_op jit(solution)/shard_map/ppermute | solution.py:334
  24.9 1.9 %residual.2.refs_0_ = f32[1,1,64,8192]{3,2,1,0:T(8,128)} custom-call(bf16[64,192]{1,0:T(8,128)(2,1)S(1)} %copy-done.2, s32[4,128]{1,0:T(4,128)S(1)} %bitcast.8, s32[1,128]{1,0:T(1,128)S(1)} %bitcast.11, f32[32,2,1152]{2,1,0:T(2,128)S(1)} %pick_rows.1.refs_3_.refs_4_, f32[1,1,64,8192]{3,2,1,0:T(8,128)S(1)} %copy-done, f32[1,1,64,8192]{3,2,1,0:T(8,128)S(1)} %copy-done.1), custom_call_target="tpu_custom_call" | custom-call | flops 402653184 | bytes 6291456 | tf_op jit(solution)/shard_map/residual/pallas_call | solution.py:288
  26.8 1.1 %collective-permute-start.7 = (f32[64,512]{1,0:T(8,128)S(1)}, f32[64,512]{1,0:T(8,128)S(1)}, u32[]{:S(2)}, u32[]{:S(2)}) collective-permute-start(f32[64,512]{1,0:T(8,128)S(1)} %sum_and_update.1.refs_0_), channel_id=1, source_target_pairs={{0,16},{1,17},{2,18},{3,19},{4,20},{5,21},{6,22},{7,23},{8,24},{9,... | collective-permute-start | bytes 393224 | tf_op jit(solution)/shard_map/ppermute | solution.py:334
  27.9 1.9 %collective-permute-start.6 = (f32[64,512]{1,0:T(8,128)S(1)}, f32[64,512]{1,0:T(8,128)S(1)}, u32[]{:S(2)}, u32[]{:S(2)}) collective-permute-start(f32[64,512]{1,0:T(8,128)S(1)} %sum_and_update.1.refs_0_), channel_id=1, source_target_pairs={{0,1},{1,0},{2,3},{3,2},{4,5},{5,4},{6,7},{7,6},{8,9},{9,8},{10,11... | collective-permute-start | bytes 393224 | tf_op jit(solution)/shard_map/ppermute | solution.py:334
  29.9 0.5 %collective-permute-start.2 = (f32[64,512]{1,0:T(8,128)S(1)}, f32[64,512]{1,0:T(8,128)S(1)}, u32[]{:S(2)}, u32[]{:S(2)}) collective-permute-start(f32[64,512]{1,0:T(8,128)S(1)} %collective-permute-done.refs_1_), channel_id=1, source_target_pairs={{0,16},{1,17},{2,18},{3,19},{4,20},{5,21},{6,22},{7,23},{8,24},{9,... | collective-permute-start | bytes 393224 | tf_op jit(solution)/shard_map/ppermute | solution.py:334
  30.4 0.5 %collective-permute-start.1 = (f32[64,512]{1,0:T(8,128)S(1)}, f32[64,512]{1,0:T(8,128)S(1)}, u32[]{:S(2)}, u32[]{:S(2)}) collective-permute-start(f32[64,512]{1,0:T(8,128)S(1)} %collective-permute-done.refs_1_), channel_id=1, source_target_pairs={{0,1},{1,0},{2,3},{3,2},{4,5},{5,4},{6,7},{7,6},{8,9},{9,8},{10,11... | collective-permute-start | bytes 393224 | tf_op jit(solution)/shard_map/ppermute | solution.py:334
  31.0 1.5 %collective-permute-start.4 = (f32[64,512]{1,0:T(8,128)S(1)}, f32[64,512]{1,0:T(8,128)S(1)}, u32[]{:S(2)}, u32[]{:S(2)}) collective-permute-start(f32[64,512]{1,0:T(8,128)S(1)} %collective-permute-done.3.refs_2_), channel_id=1, source_target_pairs={{0,2},{1,3},{2,0},{3,1},{4,6},{5,7},{6,4},{7,5},{8,10},{9,11},{10,... | collective-permute-start | bytes 393224 | tf_op jit(solution)/shard_map/ppermute | solution.py:334
  32.5 1.2 %residual.3 = f32[1,1,64,8192]{3,2,1,0:T(8,128)} custom-call(f32[1,1,64,8192]{3,2,1,0:T(8,128)} %residual.2.refs_0_, bf16[64,192]{1,0:T(8,128)(2,1)S(1)} %copy-done.2, s32[4,128]{1,0:T(4,128)S(1)} %bitcast.9, s32[1,128]{1,0:T(1,128)S(1)} %bitcast.12, f32[32,2,1152]{2,1,0:T(2,128)S(1)} %pick_rows.1.refs_3_.refs_4_, ...), custom_call_target="tpu_custom_call", output_to_operand_aliasing={{}: (0, {})} | custom-call | flops 40265318400 | bytes 629145600 | tf_op jit(solution)/shard_map/residual/pallas_call | solution.py:288
  33.7 0.6 %collective-permute-done.6.refs_3_ = f32[64,512]{1,0:T(8,128)S(1)} collective-permute-done((f32[64,512]{1,0:T(8,128)S(1)}, f32[64,512]{1,0:T(8,128)S(1)}, u32[]{:S(2)}, u32[]{:S(2)}) %collective-permute-start.6) | collective-permute-done | bytes 131104 | tf_op jit(solution)/shard_map/ppermute | solution.py:334
  34.3 0.5 %collective-permute-start.9 = (f32[64,512]{1,0:T(8,128)S(1)}, f32[64,512]{1,0:T(8,128)S(1)}, u32[]{:S(2)}, u32[]{:S(2)}) collective-permute-start(f32[64,512]{1,0:T(8,128)S(1)} %collective-permute-done.3.refs_2_), channel_id=1, source_target_pairs={{0,8},{1,9},{2,10},{3,11},{4,12},{5,13},{6,14},{7,15},{8,0},{9,1},... | collective-permute-start | bytes 393224 | tf_op jit(solution)/shard_map/ppermute | solution.py:334
  34.8 0.9 %place_columns.3.refs_0_ = f32[64,8192]{1,0:T(8,128)} custom-call(f32[64,512]{1,0:T(8,128)S(1)} %sum_and_update.1.refs_0_, f32[64,512]{1,0:T(8,128)S(1)} %collective-permute-done.refs_1_, f32[64,512]{1,0:T(8,128)S(1)} %collective-permute-done.3.refs_2_, f32[64,512]{1,0:T(8,128)S(1)} %collective-permute-done.6.refs_3_, ...), custom_call_target="tpu_custom_call" | custom-call | tf_op jit(solution)/shard_map/place_columns/pallas_call | solution.py:381
  35.7 0.2 collective-permute-done.4.refs_3_
  35.9 0.5 %collective-permute-done.2.refs_2_ = f32[64,512]{1,0:T(8,128)S(1)} collective-permute-done((f32[64,512]{1,0:T(8,128)S(1)}, f32[64,512]{1,0:T(8,128)S(1)}, u32[]{:S(2)}, u32[]{:S(2)}) %collective-permute-start.2) | collective-permute-done | bytes 131104 | tf_op jit(solution)/shard_map/ppermute | solution.py:334
  36.4 0.5 %collective-permute-start.12 = (f32[64,512]{1,0:T(8,128)S(1)}, f32[64,512]{1,0:T(8,128)S(1)}, u32[]{:S(2)}, u32[]{:S(2)}) collective-permute-start(f32[64,512]{1,0:T(8,128)S(1)} %collective-permute-done.1.refs_1_), channel_id=1, source_target_pairs={{0,8},{1,9},{2,10},{3,11},{4,12},{5,13},{6,14},{7,15},{8,0},{9,1},... | collective-permute-start | bytes 393224 | tf_op jit(solution)/shard_map/ppermute | solution.py:334
  36.9 0.1 collective-permute-start.13
  37.0 0.4 %collective-permute-start.14 = (f32[64,512]{1,0:T(8,128)S(1)}, f32[64,512]{1,0:T(8,128)S(1)}, u32[]{:S(2)}, u32[]{:S(2)}) collective-permute-start(f32[64,512]{1,0:T(8,128)S(1)} %collective-permute-done.4.refs_3_), channel_id=1, source_target_pairs={{0,8},{1,9},{2,10},{3,11},{4,12},{5,13},{6,14},{7,15},{8,0},{9,1},... | collective-permute-start | bytes 393224 | tf_op jit(solution)/shard_map/ppermute | solution.py:334
  37.4 0.3 collective-permute-done.11.refs_7_
  37.7 1.0 %place_columns.4.refs_0_ = f32[64,8192]{1,0:T(8,128)} custom-call(f32[64,8192]{1,0:T(8,128)} %place_columns.3.refs_0_, f32[64,512]{1,0:T(8,128)S(1)} %collective-permute-done.1.refs_1_, f32[64,512]{1,0:T(8,128)S(1)} %collective-permute-done.2.refs_2_, f32[64,512]{1,0:T(8,128)S(1)} %collective-permute-done.4.refs_3_, ...), custom_call_target="tpu_custom_call", output_to_operand_aliasing={{}: (0, {})} | custom-call | tf_op jit(solution)/shard_map/place_columns/pallas_call | solution.py:381
  38.7 0.8 %place_columns.5 = f32[64,8192]{1,0:T(8,128)} custom-call(f32[64,8192]{1,0:T(8,128)} %place_columns.4.refs_0_, f32[64,512]{1,0:T(8,128)S(1)} %collective-permute-done.12.refs_1_, f32[64,512]{1,0:T(8,128)S(1)} %collective-permute-done.13.refs_2_, f32[64,512]{1,0:T(8,128)S(1)} %collective-permute-done.14.refs_3_), custom_call_target="tpu_custom_call", output_to_operand_aliasing={{}: (0, {})} | custom-call | tf_op jit(solution)/shard_map/place_columns/pallas_call | solution.py:381
  (24 shorter events, 0.2 us)
Async XLA Ops:
  0.6 21.4 %copy-start.2 = (bf16[64,192]{1,0:T(8,128)(2,1)S(1)}, bf16[64,192]{1,0:T(8,128)(2,1)}, u32[]{:S(2)}) copy-start(bf16[64,192]{1,0:T(8,128)(2,1)} %constant.5.clone.back_ref.refs_0_.refs_1_) | copy-start | bytes 73732
  0.6 24.2 %copy-start.1 = (f32[1,1,64,8192]{3,2,1,0:T(8,128)S(1)}, f32[1,1,64,8192]{3,2,1,0:T(8,128)}, u32[]{:S(2)}) copy-start(f32[1,1,64,8192]{3,2,1,0:T(8,128)} %refs_6_.1) | copy-start | bytes 6291460
  3.4 21.5 %copy-start = (f32[1,1,64,8192]{3,2,1,0:T(8,128)S(1)}, f32[1,1,64,8192]{3,2,1,0:T(8,128)}, u32[]{:S(2)}) copy-start(f32[1,1,64,8192]{3,2,1,0:T(8,128)} %refs_5_.5) | copy-start | bytes 6291460
  3.4 21.5 %copy-start.3 = (s32[1,1,128,4]{2,3,1,0:T(4,128)S(1)}, s32[1,1,128,4]{2,3,1,0:T(4,128)}, u32[]{:S(2)}) copy-start(s32[1,1,128,4]{2,3,1,0:T(4,128)} %param.11) | copy-start | bytes 6148
  3.4 21.4 %copy-start.4 = (s32[1,1,128]{2,1,0:T(1,128)S(1)}, s32[1,1,128]{2,1,0:T(1,128)}, u32[]{:S(2)}) copy-start(s32[1,1,128]{2,1,0:T(1,128)} %param.12) | copy-start | bytes 1540
  23.3 3.5 %collective-permute-start.5 = (f32[64,512]{1,0:T(8,128)S(1)}, f32[64,512]{1,0:T(8,128)S(1)}, u32[]{:S(2)}, u32[]{:S(2)}) collective-permute-start(f32[64,512]{1,0:T(8,128)S(1)} %sum_and_update.1.refs_0_), channel_id=1, source_target_pairs={{0,8},{1,9},{2,10},{3,11},{4,12},{5,13},{6,14},{7,15},{8,0},{9,1},... | collective-permute-start | bytes 393224 | tf_op jit(solution)/shard_map/ppermute | solution.py:334
  23.4 6.5 %collective-permute-start = (f32[64,512]{1,0:T(8,128)S(1)}, f32[64,512]{1,0:T(8,128)S(1)}, u32[]{:S(2)}, u32[]{:S(2)}) collective-permute-start(f32[64,512]{1,0:T(8,128)S(1)} %sum_and_update.1.refs_0_), channel_id=1, source_target_pairs={{0,2},{1,3},{2,0},{3,1},{4,6},{5,7},{6,4},{7,5},{8,10},{9,11},{10,... | collective-permute-start | bytes 393224 | tf_op jit(solution)/shard_map/ppermute | solution.py:334
  24.4 6.6 %collective-permute-start.3 = (f32[64,512]{1,0:T(8,128)S(1)}, f32[64,512]{1,0:T(8,128)S(1)}, u32[]{:S(2)}, u32[]{:S(2)}) collective-permute-start(f32[64,512]{1,0:T(8,128)S(1)} %sum_and_update.1.refs_0_), channel_id=1, source_target_pairs={{0,17},{1,16},{2,19},{3,18},{4,21},{5,20},{6,23},{7,22},{8,25},{9,... | collective-permute-start | bytes 393224 | tf_op jit(solution)/shard_map/ppermute | solution.py:334
  26.8 6.9 %collective-permute-start.7 = (f32[64,512]{1,0:T(8,128)S(1)}, f32[64,512]{1,0:T(8,128)S(1)}, u32[]{:S(2)}, u32[]{:S(2)}) collective-permute-start(f32[64,512]{1,0:T(8,128)S(1)} %sum_and_update.1.refs_0_), channel_id=1, source_target_pairs={{0,16},{1,17},{2,18},{3,19},{4,20},{5,21},{6,22},{7,23},{8,24},{9,... | collective-permute-start | bytes 393224 | tf_op jit(solution)/shard_map/ppermute | solution.py:334
  27.9 6.3 %collective-permute-start.6 = (f32[64,512]{1,0:T(8,128)S(1)}, f32[64,512]{1,0:T(8,128)S(1)}, u32[]{:S(2)}, u32[]{:S(2)}) collective-permute-start(f32[64,512]{1,0:T(8,128)S(1)} %sum_and_update.1.refs_0_), channel_id=1, source_target_pairs={{0,1},{1,0},{2,3},{3,2},{4,5},{5,4},{6,7},{7,6},{8,9},{9,8},{10,11... | collective-permute-start | bytes 393224 | tf_op jit(solution)/shard_map/ppermute | solution.py:334
  29.9 6.5 %collective-permute-start.2 = (f32[64,512]{1,0:T(8,128)S(1)}, f32[64,512]{1,0:T(8,128)S(1)}, u32[]{:S(2)}, u32[]{:S(2)}) collective-permute-start(f32[64,512]{1,0:T(8,128)S(1)} %collective-permute-done.refs_1_), channel_id=1, source_target_pairs={{0,16},{1,17},{2,18},{3,19},{4,20},{5,21},{6,22},{7,23},{8,24},{9,... | collective-permute-start | bytes 393224 | tf_op jit(solution)/shard_map/ppermute | solution.py:334
  30.4 6.1 %collective-permute-start.1 = (f32[64,512]{1,0:T(8,128)S(1)}, f32[64,512]{1,0:T(8,128)S(1)}, u32[]{:S(2)}, u32[]{:S(2)}) collective-permute-start(f32[64,512]{1,0:T(8,128)S(1)} %collective-permute-done.refs_1_), channel_id=1, source_target_pairs={{0,1},{1,0},{2,3},{3,2},{4,5},{5,4},{6,7},{7,6},{8,9},{9,8},{10,11... | collective-permute-start | bytes 393224 | tf_op jit(solution)/shard_map/ppermute | solution.py:334
  31.0 5.0 %collective-permute-start.4 = (f32[64,512]{1,0:T(8,128)S(1)}, f32[64,512]{1,0:T(8,128)S(1)}, u32[]{:S(2)}, u32[]{:S(2)}) collective-permute-start(f32[64,512]{1,0:T(8,128)S(1)} %collective-permute-done.3.refs_2_), channel_id=1, source_target_pairs={{0,2},{1,3},{2,0},{3,1},{4,6},{5,7},{6,4},{7,5},{8,10},{9,11},{10,... | collective-permute-start | bytes 393224 | tf_op jit(solution)/shard_map/ppermute | solution.py:334
  34.3 2.6 %collective-permute-start.8 = (f32[64,512]{1,0:T(8,128)S(1)}, f32[64,512]{1,0:T(8,128)S(1)}, u32[]{:S(2)}, u32[]{:S(2)}) collective-permute-start(f32[64,512]{1,0:T(8,128)S(1)} %collective-permute-done.refs_1_), channel_id=1, source_target_pairs={{0,8},{1,9},{2,10},{3,11},{4,12},{5,13},{6,14},{7,15},{8,0},{9,1},... | collective-permute-start | bytes 393224 | tf_op jit(solution)/shard_map/ppermute | solution.py:334
  34.3 2.7 %collective-permute-start.9 = (f32[64,512]{1,0:T(8,128)S(1)}, f32[64,512]{1,0:T(8,128)S(1)}, u32[]{:S(2)}, u32[]{:S(2)}) collective-permute-start(f32[64,512]{1,0:T(8,128)S(1)} %collective-permute-done.3.refs_2_), channel_id=1, source_target_pairs={{0,8},{1,9},{2,10},{3,11},{4,12},{5,13},{6,14},{7,15},{8,0},{9,1},... | collective-permute-start | bytes 393224 | tf_op jit(solution)/shard_map/ppermute | solution.py:334
  35.9 1.5 %collective-permute-start.10 = (f32[64,512]{1,0:T(8,128)S(1)}, f32[64,512]{1,0:T(8,128)S(1)}, u32[]{:S(2)}, u32[]{:S(2)}) collective-permute-start(f32[64,512]{1,0:T(8,128)S(1)} %collective-permute-done.6.refs_3_), channel_id=1, source_target_pairs={{0,8},{1,9},{2,10},{3,11},{4,12},{5,13},{6,14},{7,15},{8,0},{9,1},... | collective-permute-start | bytes 393224 | tf_op jit(solution)/shard_map/ppermute | solution.py:334
  36.4 1.3 %collective-permute-start.11 = (f32[64,512]{1,0:T(8,128)S(1)}, f32[64,512]{1,0:T(8,128)S(1)}, u32[]{:S(2)}, u32[]{:S(2)}) collective-permute-start(f32[64,512]{1,0:T(8,128)S(1)} %collective-permute-done.7.refs_4_), channel_id=1, source_target_pairs={{0,8},{1,9},{2,10},{3,11},{4,12},{5,13},{6,14},{7,15},{8,0},{9,1},... | collective-permute-start | bytes 393224 | tf_op jit(solution)/shard_map/ppermute | solution.py:334
  36.4 2.3 %collective-permute-start.12 = (f32[64,512]{1,0:T(8,128)S(1)}, f32[64,512]{1,0:T(8,128)S(1)}, u32[]{:S(2)}, u32[]{:S(2)}) collective-permute-start(f32[64,512]{1,0:T(8,128)S(1)} %collective-permute-done.1.refs_1_), channel_id=1, source_target_pairs={{0,8},{1,9},{2,10},{3,11},{4,12},{5,13},{6,14},{7,15},{8,0},{9,1},... | collective-permute-start | bytes 393224 | tf_op jit(solution)/shard_map/ppermute | solution.py:334
  36.9 1.8 %collective-permute-start.13 = (f32[64,512]{1,0:T(8,128)S(1)}, f32[64,512]{1,0:T(8,128)S(1)}, u32[]{:S(2)}, u32[]{:S(2)}) collective-permute-start(f32[64,512]{1,0:T(8,128)S(1)} %collective-permute-done.2.refs_2_), channel_id=1, source_target_pairs={{0,8},{1,9},{2,10},{3,11},{4,12},{5,13},{6,14},{7,15},{8,0},{9,1},... | collective-permute-start | bytes 393224 | tf_op jit(solution)/shard_map/ppermute | solution.py:334
  37.0 1.8 %collective-permute-start.14 = (f32[64,512]{1,0:T(8,128)S(1)}, f32[64,512]{1,0:T(8,128)S(1)}, u32[]{:S(2)}, u32[]{:S(2)}) collective-permute-start(f32[64,512]{1,0:T(8,128)S(1)} %collective-permute-done.4.refs_3_), channel_id=1, source_target_pairs={{0,8},{1,9},{2,10},{3,11},{4,12},{5,13},{6,14},{7,15},{8,0},{9,1},... | collective-permute-start | bytes 393224 | tf_op jit(solution)/shard_map/ppermute | solution.py:334

commit v5 on v4

--- a/solution.py
+++ b/solution.py
@@ -215,8 +215,11 @@
         )
         high = values.astype(jnp.bfloat16)
         low = (values - high.astype(jnp.float32)).astype(jnp.bfloat16)
-        total = jnp.dot(table, high, preferred_element_type=jnp.float32)
-        total += jnp.dot(table, low, preferred_element_type=jnp.float32)
+        total = jnp.dot(
+            jnp.concatenate([table, table], axis=1),
+            jnp.concatenate([high, low], axis=0),
+            preferred_element_type=jnp.float32,
+        )
         mine = total[:order]
         for p in range(1, pair):
             mine = jnp.where(lane // order == p, total[p * order : (p + 1) * order], mine)
@@ -230,7 +233,12 @@
     *pieces, out_ref, sems = refs[skipped:]
     row, col = lax.axis_index("row"), lax.axis_index("col")
     copies = []
-    for piece, (other, dy, dx, dz) in zip(pieces, places, strict=True):
+    flat = [
+        (piece.at[k] if len(piece.shape) == 3 else piece, place)
+        for piece, among in zip(pieces, places, strict=True)
+        for k, place in enumerate(among)
+    ]
+    for piece, (other, dy, dx, dz) in flat:
         width = piece.shape[-1]
         part = part_index(sizes, row, col, (dy, dz, dx), other)
         copy = pltpu.make_async_copy(
@@ -298,8 +306,8 @@
         compiler_params=limits(),
         name="residual",
         cost_estimate=pl.CostEstimate(
-            flops=12 * order * order * momentum.shape[-1] * (1 if before is None else 100),
-            bytes_accessed=3 * momentum.size * 4 * (1 if before is None else 100),
+            flops=12 * order * order * momentum.shape[-1] * (1 if before is None else 1),
+            bytes_accessed=3 * momentum.size * 4 * (1 if before is None else 1),
             transcendentals=0,
         ),
     )(*given, back, chosen, counts, sent, momentum, gradient)
@@ -336,18 +344,23 @@
     far = [(j, i) for j in range(y_size) for i in range(x_size) if j or i]
     far.sort(key=lambda at: sum(map(bool, at)))
     parts = y_size * CORES * lines * x_size
-    fill = parts * 12 // 16
+    fill = parts * 8 // 16
     line = [mine] + [swap(mine, (0, 0, j, 0)) for j in range(1, lines)]
-    def other(piece_of):
-        return (swap(piece_of[0], (0, 1, 0, 0)), 1, *piece_of[1:])
+    def mine_of(pieces):
+        return [(array, [(0, *at)]) for array, *at in pieces]
+
+    def other(pieces):
+        arrays = [piece_of[0] for piece_of in pieces]
+        array = arrays[0] if len(arrays) == 1 else jnp.stack(arrays)
+        return (swap(array, (0, 1, 0, 0)), [(1, *piece_of[1:]) for piece_of in pieces])
 
     corners = [(j, i) for j, i in far if j and i]
     sides = [(j, i) for j, i in far if not (j and i)]
     near = [(own, 0, 0, n) for n, own in enumerate(line)]
     begun = [(swap(mine, (j, 0, 0, i)), j, i, 0) for j, i in corners]
-    theirs = [other(near[0])]
+    theirs = [other(near[:1])]
     held, theirs_first = lax.optimization_barrier((mine, theirs[0][0]))
-    theirs = [(theirs_first, *theirs[0][1:])]
+    theirs = [(theirs_first, theirs[0][1])]
     gone = begun + [(swap(held, (j, 0, 0, i)), j, i, 0) for j, i in sides]
     late, done, residual = [], 0, None
     for n, own in enumerate(line[1:], 1):
@@ -361,21 +374,21 @@
     waiting = near[1:] + gone
     arrays, residual = lax.optimization_barrier(([piece_of[0] for piece_of in waiting], residual))
     waiting = [(array, *at[1:]) for array, at in zip(arrays, waiting, strict=True)]
-    first = [(array, 0, *at) for array, *at in near[:1] + waiting] + theirs
-    partial = place(first, sizes, params, None)
-    theirs = [other(piece_of) for piece_of in waiting]
+    partial = place(mine_of(near[:1] + waiting) + theirs, sizes, params, None)
+    theirs = [other(waiting[: -len(sides)]), other(waiting[-len(sides) :])]
     arrays = [piece_of[0] for piece_of in late]
     arrays, partial = lax.optimization_barrier((arrays, partial))
     late = [(array, *at[1:]) for array, at in zip(arrays, late, strict=True)]
-    second = [(array, 0, *at) for array, *at in late] + theirs
-    partial = place(second, sizes, params, partial)
-    partial = place([other(piece_of) for piece_of in late], sizes, params, partial)
+    partial = place(mine_of(late) + theirs, sizes, params, partial)
+    straight = [piece_of for piece_of in late if not (piece_of[1] and piece_of[2])]
+    across = [piece_of for piece_of in late if piece_of[1] and piece_of[2]]
+    partial = place([other(group) for group in (straight, across) if group], sizes, params, partial)
     return partial, residual
 
 
 def place(pieces, sizes, params, partial):
     arrays = [piece[0] for piece in pieces]
-    places = [piece[1:] for piece in pieces]
+    places = [piece[1] for piece in pieces]
     anywhere = pl.BlockSpec(memory_space=pl.ANY)
     given = [] if partial is None else [partial]
     return pl.pallas_call(
@@ -383,7 +396,7 @@
         in_specs=[anywhere] * (len(given) + len(arrays)),
         out_specs=anywhere,
         out_shape=jax.ShapeDtypeStruct(params.shape, jnp.float32),
-        scratch_shapes=[pltpu.SemaphoreType.DMA((len(arrays),))],
+        scratch_shapes=[pltpu.SemaphoreType.DMA((sum(map(len, places)),))],
         input_output_aliases={0: 0} if given else {},
         compiler_params=limits(),
         name="place_columns",

time: 39.7 us -> 39.3 us (0.990)
  starting transfers between devices: 8.72 us -> 8.19 us
    ppermute x15 -> x12, starting transfers between devices: 8.72 us -> 8.19 us  [swap(): return lax.ppermute(array, EVERY, pairs)]
    ppermute x15 -> x12, waiting for transfers between devices: 1.67 us -> 1.72 us  [swap(): return lax.ppermute(array, EVERY, pairs)]
  transfers between devices with their start and end apart: 15 -> 12, of which waited for: 4 -> 3; matrix products, arithmetic and copies ran while one was open for 0% -> 0% of each run, Pallas kernels for 12% -> 13%
where the time goes in v5:
time: 39.3 us; the launch traced here: 39.2 us
  blocking collectives  18.5 us (47%)
  Pallas kernels  9.83 us (25%)
  starting transfers between devices  8.19 us (21%)
  waiting for transfers between devices  1.72 us (4%)
  between operations  0.8 us (2%)
    all_to_all x1, blocking collectives, body(): got = lax.all_to_all(sent, EVERY, 0, 0, tiled=True)  18.5 us
    ppermute x12, starting transfers between devices, swap(): return lax.ppermute(array, EVERY, pairs)  8.19 us
    pallas_call x2, Pallas kernels, rest(): pl.pallas_call(functools.partial(rest_kernel, len(given), first, width, s...  3.12 us
    pallas_call x1, Pallas kernels, pick(): pl.pallas_call(functools.partial(pick_kernel, width, steps, slots_of), in...  2.74 us
    pallas_call x3, Pallas kernels, place(): pl.pallas_call(functools.partial(place_kernel, places, sizes, len(given))...  2.66 us
    ppermute x12, waiting for transfers between devices, swap(): return lax.ppermute(array, EVERY, pairs)  1.72 us
    pallas_call x1, Pallas kernels, add_up(): pl.pallas_call(functools.partial(sum_kernel, sizes), in_specs=[vmem(), vm...  1.3 us
  transfers between devices with their start and end apart: 12, of which 3 were waited for; matrix products, arithmetic and copies ran while one was open for 0% of the time, Pallas kernels for 13%

profile of v5, /device:TPU:0, one launch (start us, length us, event | category | flops | bytes accessed | tf_op | source)
XLA Modules:
  0.0 39.2 jit_solution(5209963983815481386)
XLA Ops:
  0.6 0.0 copy-start.2
  0.7 2.7 %pick_rows.1.refs_3_.refs_4_ = f32[32,2,1152]{2,1,0:T(2,128)S(1)} custom-call(bf16[64,192]{1,0:T(8,128)(2,1)} %constant.4.clone.refs_0_, s32[4,128]{1,0:T(4,128)} %bitcast.19, s32[1,128]{1,0:T(1,128)} %bitcast.22, s32[8,128]{1,0:T(8,128)} %bitcast.25, f32[1,1,64,8192]{3,2,1,0:T(8,128)} %refs_5_.5, f32[1,1,64,8192]{3,2,1,0:T(8,128)} %refs_6_.1), custom_call_target="tpu_custom_call" | custom-call | tf_op jit(solution)/shard_map/pick_rows/pallas_call | solution.py:280
  3.4 18.5 %all_to_all.5.got_ref = f32[32,2,1152]{2,1,0:T(2,128)S(1)} all-to-all(f32[32,2,1152]{2,1,0:T(2,128)S(1)} %pick_rows.1.refs_3_.refs_4_), channel_id=1, replica_groups=mesh['row'=4,'col'=8] {'row','col'}, dimensions={0} | all-to-all | bytes 589824 | tf_op jit(solution)/shard_map/all_to_all | solution.py:417
  22.0 1.3 %sum_and_update.1.refs_0_ = f32[64,512]{1,0:T(8,128)S(1)} custom-call(bf16[64,192]{1,0:T(8,128)(2,1)S(1)} %copy-done.2, f32[32,2,1152]{2,1,0:T(2,128)S(1)} %all_to_all.5.got_ref, f32[64,8192]{1,0:T(8,128)} %params_ref.1), custom_call_target="tpu_custom_call" | custom-call | tf_op jit(solution)/shard_map/sum_and_update/pallas_call | solution.py:319
  23.3 0.1 collective-permute-start.5
  23.4 0.9 %collective-permute-start = (f32[64,512]{1,0:T(8,128)S(1)}, f32[64,512]{1,0:T(8,128)S(1)}, u32[]{:S(2)}, u32[]{:S(2)}) collective-permute-start(f32[64,512]{1,0:T(8,128)S(1)} %sum_and_update.1.refs_0_), channel_id=1, source_target_pairs={{0,2},{1,3},{2,0},{3,1},{4,6},{5,7},{6,4},{7,5},{8,10},{9,11},{10,... | collective-permute-start | bytes 393224 | tf_op jit(solution)/shard_map/ppermute | solution.py:342
  24.3 0.5 %collective-permute-start.3 = (f32[64,512]{1,0:T(8,128)S(1)}, f32[64,512]{1,0:T(8,128)S(1)}, u32[]{:S(2)}, u32[]{:S(2)}) collective-permute-start(f32[64,512]{1,0:T(8,128)S(1)} %sum_and_update.1.refs_0_), channel_id=1, source_target_pairs={{0,17},{1,16},{2,19},{3,18},{4,21},{5,20},{6,23},{7,22},{8,25},{9,... | collective-permute-start | bytes 393224 | tf_op jit(solution)/shard_map/ppermute | solution.py:342
  24.8 1.1 %collective-permute-start.7 = (f32[64,512]{1,0:T(8,128)S(1)}, f32[64,512]{1,0:T(8,128)S(1)}, u32[]{:S(2)}, u32[]{:S(2)}) collective-permute-start(f32[64,512]{1,0:T(8,128)S(1)} %sum_and_update.1.refs_0_), channel_id=1, source_target_pairs={{0,16},{1,17},{2,18},{3,19},{4,20},{5,21},{6,22},{7,23},{8,24},{9,... | collective-permute-start | bytes 393224 | tf_op jit(solution)/shard_map/ppermute | solution.py:342
  25.9 1.9 %collective-permute-start.6 = (f32[64,512]{1,0:T(8,128)S(1)}, f32[64,512]{1,0:T(8,128)S(1)}, u32[]{:S(2)}, u32[]{:S(2)}) collective-permute-start(f32[64,512]{1,0:T(8,128)S(1)} %sum_and_update.1.refs_0_), channel_id=1, source_target_pairs={{0,1},{1,0},{2,3},{3,2},{4,5},{5,4},{6,7},{7,6},{8,9},{9,8},{10,11... | collective-permute-start | bytes 393224 | tf_op jit(solution)/shard_map/ppermute | solution.py:342
  27.8 1.6 %residual.2.refs_0_ = f32[1,1,64,8192]{3,2,1,0:T(8,128)} custom-call(bf16[64,192]{1,0:T(8,128)(2,1)S(1)} %copy-done.2, s32[4,128]{1,0:T(4,128)S(1)} %bitcast.20, s32[1,128]{1,0:T(1,128)S(1)} %bitcast.23, f32[32,2,1152]{2,1,0:T(2,128)S(1)} %pick_rows.1.refs_3_.refs_4_, f32[1,1,64,8192]{3,2,1,0:T(8,128)S(1)} %copy-done, f32[1,1,64,8192]{3,2,1,0:T(8,128)S(1)} %copy-done.1), custom_call_target="tpu_custom_call" | custom-call | flops 402653184 | bytes 6291456 | tf_op jit(solution)/shard_map/residual/pallas_call | solution.py:296
  29.4 0.6 %collective-permute-start.2 = (f32[64,512]{1,0:T(8,128)S(1)}, f32[64,512]{1,0:T(8,128)S(1)}, u32[]{:S(2)}, u32[]{:S(2)}) collective-permute-start(f32[64,512]{1,0:T(8,128)S(1)} %collective-permute-done.refs_1_), channel_id=1, source_target_pairs={{0,16},{1,17},{2,18},{3,19},{4,20},{5,21},{6,22},{7,23},{8,24},{9,... | collective-permute-start | bytes 393224 | tf_op jit(solution)/shard_map/ppermute | solution.py:342
  30.0 0.7 %collective-permute-start.1 = (f32[64,512]{1,0:T(8,128)S(1)}, f32[64,512]{1,0:T(8,128)S(1)}, u32[]{:S(2)}, u32[]{:S(2)}) collective-permute-start(f32[64,512]{1,0:T(8,128)S(1)} %collective-permute-done.refs_1_), channel_id=1, source_target_pairs={{0,1},{1,0},{2,3},{3,2},{4,5},{5,4},{6,7},{7,6},{8,9},{9,8},{10,11... | collective-permute-start | bytes 393224 | tf_op jit(solution)/shard_map/ppermute | solution.py:342
  30.8 0.9 %collective-permute-done.3.refs_2_ = f32[64,512]{1,0:T(8,128)S(1)} collective-permute-done((f32[64,512]{1,0:T(8,128)S(1)}, f32[64,512]{1,0:T(8,128)S(1)}, u32[]{:S(2)}, u32[]{:S(2)}) %collective-permute-start.3) | collective-permute-done | bytes 131104 | tf_op jit(solution)/shard_map/ppermute | solution.py:342
  31.6 1.1 %collective-permute-start.4 = (f32[64,512]{1,0:T(8,128)S(1)}, f32[64,512]{1,0:T(8,128)S(1)}, u32[]{:S(2)}, u32[]{:S(2)}) collective-permute-start(f32[64,512]{1,0:T(8,128)S(1)} %collective-permute-done.3.refs_2_), channel_id=1, source_target_pairs={{0,2},{1,3},{2,0},{3,1},{4,6},{5,7},{6,4},{7,5},{8,10},{9,11},{10,... | collective-permute-start | bytes 393224 | tf_op jit(solution)/shard_map/ppermute | solution.py:342
  32.8 1.6 %residual.3 = f32[1,1,64,8192]{3,2,1,0:T(8,128)} custom-call(f32[1,1,64,8192]{3,2,1,0:T(8,128)} %residual.2.refs_0_, bf16[64,192]{1,0:T(8,128)(2,1)S(1)} %copy-done.2, s32[4,128]{1,0:T(4,128)S(1)} %bitcast.21, s32[1,128]{1,0:T(1,128)S(1)} %bitcast.24, f32[32,2,1152]{2,1,0:T(2,128)S(1)} %pick_rows.1.refs_3_.refs_4_, ...), custom_call_target="tpu_custom_call", output_to_operand_aliasing={{}: (0, {})} | custom-call | flops 402653184 | bytes 6291456 | tf_op jit(solution)/shard_map/residual/pallas_call | solution.py:296
  34.4 0.1 collective-permute-start.8
  34.5 0.6 %collective-permute-start.9 = (f32[2,64,512]{2,1,0:T(8,128)S(1)}, f32[2,64,512]{2,1,0:T(8,128)S(1)}, u32[]{:S(2)}, u32[]{:S(2)}) collective-permute-start(f32[2,64,512]{2,1,0:T(8,128)S(1)} %pad_maximum_fusion.1), channel_id=1, source_target_pairs={{0,8},{1,9},{2,10},{3,11},{4,12},{5,13},{6,14},{7,15},{8,0},{9,1},... | collective-permute-start | bytes 786440 | tf_op jit(solution)/shard_map/ppermute | solution.py:342
  35.0 0.9 %place_columns.3.refs_0_ = f32[64,8192]{1,0:T(8,128)} custom-call(f32[64,512]{1,0:T(8,128)S(1)} %sum_and_update.1.refs_0_, f32[64,512]{1,0:T(8,128)S(1)} %collective-permute-done.refs_1_, f32[64,512]{1,0:T(8,128)S(1)} %collective-permute-done.3.refs_2_, f32[64,512]{1,0:T(8,128)S(1)} %collective-permute-done.6.refs_3_, ...), custom_call_target="tpu_custom_call" | custom-call | tf_op jit(solution)/shard_map/place_columns/pallas_call | solution.py:394
  36.0 0.6 %collective-permute-done.4.refs_3_ = f32[64,512]{1,0:T(8,128)S(1)} collective-permute-done((f32[64,512]{1,0:T(8,128)S(1)}, f32[64,512]{1,0:T(8,128)S(1)}, u32[]{:S(2)}, u32[]{:S(2)}) %collective-permute-start.4) | collective-permute-done | bytes 131104 | tf_op jit(solution)/shard_map/ppermute | solution.py:342
  36.6 0.1 collective-permute-start.10
  36.7 0.5 %collective-permute-start.11 = (f32[64,512]{1,0:T(8,128)S(1)}, f32[64,512]{1,0:T(8,128)S(1)}, u32[]{:S(2)}, u32[]{:S(2)}) collective-permute-start(f32[64,512]{1,0:T(8,128)S(1)} %collective-permute-done.4.refs_3_), channel_id=1, source_target_pairs={{0,8},{1,9},{2,10},{3,11},{4,12},{5,13},{6,14},{7,15},{8,0},{9,1},... | collective-permute-start | bytes 393224 | tf_op jit(solution)/shard_map/ppermute | solution.py:342
  37.2 1.0 %place_columns.4.refs_0_ = f32[64,8192]{1,0:T(8,128)} custom-call(f32[64,8192]{1,0:T(8,128)} %place_columns.3.refs_0_, f32[64,512]{1,0:T(8,128)S(1)} %collective-permute-done.1.refs_1_, f32[64,512]{1,0:T(8,128)S(1)} %collective-permute-done.2.refs_2_, f32[64,512]{1,0:T(8,128)S(1)} %collective-permute-done.4.refs_3_, ...), custom_call_target="tpu_custom_call", output_to_operand_aliasing={{}: (0, {})} | custom-call | tf_op jit(solution)/shard_map/place_columns/pallas_call | solution.py:394
  38.2 0.2 collective-permute-done.11.refs_2_
  38.4 0.8 %place_columns.5 = f32[64,8192]{1,0:T(8,128)} custom-call(f32[64,8192]{1,0:T(8,128)} %place_columns.4.refs_0_, f32[2,64,512]{2,1,0:T(8,128)S(1)} %collective-permute-done.10.refs_1_, f32[64,512]{1,0:T(8,128)S(1)} %collective-permute-done.11.refs_2_), custom_call_target="tpu_custom_call", output_to_operand_aliasing={{}: (0, {})} | custom-call | tf_op jit(solution)/shard_map/place_columns/pallas_call | solution.py:394
  (21 shorter events, 0.1 us)
Async XLA Ops:
  0.6 21.4 %copy-start.2 = (bf16[64,192]{1,0:T(8,128)(2,1)S(1)}, bf16[64,192]{1,0:T(8,128)(2,1)}, u32[]{:S(2)}) copy-start(bf16[64,192]{1,0:T(8,128)(2,1)} %constant.5.clone.back_ref.refs_0_.refs_1_) | copy-start | bytes 73732
  0.6 27.2 %copy-start.1 = (f32[1,1,64,8192]{3,2,1,0:T(8,128)S(1)}, f32[1,1,64,8192]{3,2,1,0:T(8,128)}, u32[]{:S(2)}) copy-start(f32[1,1,64,8192]{3,2,1,0:T(8,128)} %refs_6_.1) | copy-start | bytes 6291460
  3.4 24.4 %copy-start = (f32[1,1,64,8192]{3,2,1,0:T(8,128)S(1)}, f32[1,1,64,8192]{3,2,1,0:T(8,128)}, u32[]{:S(2)}) copy-start(f32[1,1,64,8192]{3,2,1,0:T(8,128)} %refs_5_.5) | copy-start | bytes 6291460
  3.4 24.4 %copy-start.3 = (s32[1,1,128,4]{2,3,1,0:T(4,128)S(1)}, s32[1,1,128,4]{2,3,1,0:T(4,128)}, u32[]{:S(2)}) copy-start(s32[1,1,128,4]{2,3,1,0:T(4,128)} %param.11) | copy-start | bytes 6148
  3.4 24.4 %copy-start.4 = (s32[1,1,128]{2,1,0:T(1,128)S(1)}, s32[1,1,128]{2,1,0:T(1,128)}, u32[]{:S(2)}) copy-start(s32[1,1,128]{2,1,0:T(1,128)} %param.12) | copy-start | bytes 1540
  23.3 1.5 %collective-permute-start.5 = (f32[64,512]{1,0:T(8,128)S(1)}, f32[64,512]{1,0:T(8,128)S(1)}, u32[]{:S(2)}, u32[]{:S(2)}) collective-permute-start(f32[64,512]{1,0:T(8,128)S(1)} %sum_and_update.1.refs_0_), channel_id=1, source_target_pairs={{0,8},{1,9},{2,10},{3,11},{4,12},{5,13},{6,14},{7,15},{8,0},{9,1},... | collective-permute-start | bytes 393224 | tf_op jit(solution)/shard_map/ppermute | solution.py:342
  23.4 6.0 %collective-permute-start = (f32[64,512]{1,0:T(8,128)S(1)}, f32[64,512]{1,0:T(8,128)S(1)}, u32[]{:S(2)}, u32[]{:S(2)}) collective-permute-start(f32[64,512]{1,0:T(8,128)S(1)} %sum_and_update.1.refs_0_), channel_id=1, source_target_pairs={{0,2},{1,3},{2,0},{3,1},{4,6},{5,7},{6,4},{7,5},{8,10},{9,11},{10,... | collective-permute-start | bytes 393224 | tf_op jit(solution)/shard_map/ppermute | solution.py:342
  24.3 7.3 %collective-permute-start.3 = (f32[64,512]{1,0:T(8,128)S(1)}, f32[64,512]{1,0:T(8,128)S(1)}, u32[]{:S(2)}, u32[]{:S(2)}) collective-permute-start(f32[64,512]{1,0:T(8,128)S(1)} %sum_and_update.1.refs_0_), channel_id=1, source_target_pairs={{0,17},{1,16},{2,19},{3,18},{4,21},{5,20},{6,23},{7,22},{8,25},{9,... | collective-permute-start | bytes 393224 | tf_op jit(solution)/shard_map/ppermute | solution.py:342
  24.8 9.5 %collective-permute-start.7 = (f32[64,512]{1,0:T(8,128)S(1)}, f32[64,512]{1,0:T(8,128)S(1)}, u32[]{:S(2)}, u32[]{:S(2)}) collective-permute-start(f32[64,512]{1,0:T(8,128)S(1)} %sum_and_update.1.refs_0_), channel_id=1, source_target_pairs={{0,16},{1,17},{2,18},{3,19},{4,20},{5,21},{6,22},{7,23},{8,24},{9,... | collective-permute-start | bytes 393224 | tf_op jit(solution)/shard_map/ppermute | solution.py:342
  25.9 8.4 %collective-permute-start.6 = (f32[64,512]{1,0:T(8,128)S(1)}, f32[64,512]{1,0:T(8,128)S(1)}, u32[]{:S(2)}, u32[]{:S(2)}) collective-permute-start(f32[64,512]{1,0:T(8,128)S(1)} %sum_and_update.1.refs_0_), channel_id=1, source_target_pairs={{0,1},{1,0},{2,3},{3,2},{4,5},{5,4},{6,7},{7,6},{8,9},{9,8},{10,11... | collective-permute-start | bytes 393224 | tf_op jit(solution)/shard_map/ppermute | solution.py:342
  29.4 7.2 %collective-permute-start.2 = (f32[64,512]{1,0:T(8,128)S(1)}, f32[64,512]{1,0:T(8,128)S(1)}, u32[]{:S(2)}, u32[]{:S(2)}) collective-permute-start(f32[64,512]{1,0:T(8,128)S(1)} %collective-permute-done.refs_1_), channel_id=1, source_target_pairs={{0,16},{1,17},{2,18},{3,19},{4,20},{5,21},{6,22},{7,23},{8,24},{9,... | collective-permute-start | bytes 393224 | tf_op jit(solution)/shard_map/ppermute | solution.py:342
  30.0 6.6 %collective-permute-start.1 = (f32[64,512]{1,0:T(8,128)S(1)}, f32[64,512]{1,0:T(8,128)S(1)}, u32[]{:S(2)}, u32[]{:S(2)}) collective-permute-start(f32[64,512]{1,0:T(8,128)S(1)} %collective-permute-done.refs_1_), channel_id=1, source_target_pairs={{0,1},{1,0},{2,3},{3,2},{4,5},{5,4},{6,7},{7,6},{8,9},{9,8},{10,11... | collective-permute-start | bytes 393224 | tf_op jit(solution)/shard_map/ppermute | solution.py:342
  31.6 5.0 %collective-permute-start.4 = (f32[64,512]{1,0:T(8,128)S(1)}, f32[64,512]{1,0:T(8,128)S(1)}, u32[]{:S(2)}, u32[]{:S(2)}) collective-permute-start(f32[64,512]{1,0:T(8,128)S(1)} %collective-permute-done.3.refs_2_), channel_id=1, source_target_pairs={{0,2},{1,3},{2,0},{3,1},{4,6},{5,7},{6,4},{7,5},{8,10},{9,11},{10,... | collective-permute-start | bytes 393224 | tf_op jit(solution)/shard_map/ppermute | solution.py:342
  34.4 2.8 %collective-permute-start.8 = (f32[2,64,512]{2,1,0:T(8,128)S(1)}, f32[2,64,512]{2,1,0:T(8,128)S(1)}, u32[]{:S(2)}, u32[]{:S(2)}) collective-permute-start(f32[2,64,512]{2,1,0:T(8,128)S(1)} %pad_maximum_fusion), channel_id=1, source_target_pairs={{0,8},{1,9},{2,10},{3,11},{4,12},{5,13},{6,14},{7,15},{8,0},{9,1},... | collective-permute-start | bytes 786440 | tf_op jit(solution)/shard_map/ppermute | solution.py:342
  34.5 2.7 %collective-permute-start.9 = (f32[2,64,512]{2,1,0:T(8,128)S(1)}, f32[2,64,512]{2,1,0:T(8,128)S(1)}, u32[]{:S(2)}, u32[]{:S(2)}) collective-permute-start(f32[2,64,512]{2,1,0:T(8,128)S(1)} %pad_maximum_fusion.1), channel_id=1, source_target_pairs={{0,8},{1,9},{2,10},{3,11},{4,12},{5,13},{6,14},{7,15},{8,0},{9,1},... | collective-permute-start | bytes 786440 | tf_op jit(solution)/shard_map/ppermute | solution.py:342
  36.6 1.8 %collective-permute-start.10 = (f32[2,64,512]{2,1,0:T(8,128)S(1)}, f32[2,64,512]{2,1,0:T(8,128)S(1)}, u32[]{:S(2)}, u32[]{:S(2)}) collective-permute-start(f32[2,64,512]{2,1,0:T(8,128)S(1)} %pad_maximum_fusion.2), channel_id=1, source_target_pairs={{0,8},{1,9},{2,10},{3,11},{4,12},{5,13},{6,14},{7,15},{8,0},{9,1},... | collective-permute-start | bytes 786440 | tf_op jit(solution)/shard_map/ppermute | solution.py:342
  36.7 1.7 %collective-permute-start.11 = (f32[64,512]{1,0:T(8,128)S(1)}, f32[64,512]{1,0:T(8,128)S(1)}, u32[]{:S(2)}, u32[]{:S(2)}) collective-permute-start(f32[64,512]{1,0:T(8,128)S(1)} %collective-permute-done.4.refs_3_), channel_id=1, source_target_pairs={{0,8},{1,9},{2,10},{3,11},{4,12},{5,13},{6,14},{7,15},{8,0},{9,1},... | collective-permute-start | bytes 393224 | tf_op jit(solution)/shard_map/ppermute | solution.py:342

commit v6 on v5

--- a/solution.py
+++ b/solution.py
@@ -187,7 +187,7 @@
     lists = got_ref.shape[0]
     chunks = (got_ref.shape[2] - LANES) // width
     each = LANES // chunks
-    numbers = jnp.concatenate([got_ref[n, :, chunks * width :] for n in range(lists)], axis=0)
+    numbers = got_ref[:, :, chunks * width :].reshape(-1, LANES)
     numbers = jnp.transpose(numbers)
     freq = lax.broadcasted_iota(jnp.int32, (order, numbers.shape[1]), 0).astype(jnp.float32)
     lane = lax.broadcasted_iota(jnp.int32, (order, LANES), 1)
@@ -207,9 +207,8 @@
         table = jnp.concatenate(table, axis=0).astype(jnp.bfloat16)
         values = jnp.concatenate(
             [
-                got_ref[n, :, c * width + at : c * width + at + LANES]
+                got_ref[:, :, c * width + at : c * width + at + LANES].reshape(-1, LANES)
                 for c in range(chunks)
-                for n in range(lists)
             ],
             axis=0,
         )

time: 39.3 us -> 39.4 us (level)
  no operation moved by 1% of the time
where the time goes in v6:
time: 39.4 us; the launch traced here: 39.2 us
  blocking collectives  18.5 us (47%)
  Pallas kernels  9.84 us (25%)
  starting transfers between devices  8.23 us (21%)
  waiting for transfers between devices  1.69 us (4%)
  between operations  0.8 us (2%)
    all_to_all x1, blocking collectives, body(): got = lax.all_to_all(sent, EVERY, 0, 0, tiled=True)  18.5 us
    ppermute x12, starting transfers between devices, swap(): return lax.ppermute(array, EVERY, pairs)  8.23 us
    pallas_call x2, Pallas kernels, rest(): pl.pallas_call(functools.partial(rest_kernel, len(given), first, width, s...  3.12 us
    pallas_call x1, Pallas kernels, pick(): pl.pallas_call(functools.partial(pick_kernel, width, steps, slots_of), in...  2.74 us
    pallas_call x3, Pallas kernels, place(): pl.pallas_call(functools.partial(place_kernel, places, sizes, len(given))...  2.66 us
    ppermute x12, waiting for transfers between devices, swap(): return lax.ppermute(array, EVERY, pairs)  1.69 us
    pallas_call x1, Pallas kernels, add_up(): pl.pallas_call(functools.partial(sum_kernel, sizes), in_specs=[vmem(), vm...  1.32 us
  transfers between devices with their start and end apart: 12, of which 3 were waited for; matrix products, arithmetic and copies ran while one was open for 0% of the time, Pallas kernels for 13%

profile of v6, /device:TPU:0, one launch (start us, length us, event | category | flops | bytes accessed | tf_op | source)
XLA Modules:
  0.0 39.2 jit_solution(7853608998252761714)
XLA Ops:
  0.6 0.0 copy-start.2
  0.7 2.7 %pick_rows.1.refs_3_.refs_4_ = f32[32,2,1152]{2,1,0:T(2,128)S(1)} custom-call(bf16[64,192]{1,0:T(8,128)(2,1)} %constant.4.clone.refs_0_, s32[4,128]{1,0:T(4,128)} %bitcast.19, s32[1,128]{1,0:T(1,128)} %bitcast.22, s32[8,128]{1,0:T(8,128)} %bitcast.25, f32[1,1,64,8192]{3,2,1,0:T(8,128)} %refs_5_.5, f32[1,1,64,8192]{3,2,1,0:T(8,128)} %refs_6_.1), custom_call_target="tpu_custom_call" | custom-call | tf_op jit(solution)/shard_map/pick_rows/pallas_call | solution.py:279
  3.4 18.5 %all_to_all.5.got_ref = f32[32,2,1152]{2,1,0:T(2,128)S(1)} all-to-all(f32[32,2,1152]{2,1,0:T(2,128)S(1)} %pick_rows.1.refs_3_.refs_4_), channel_id=1, replica_groups=mesh['row'=4,'col'=8] {'row','col'}, dimensions={0} | all-to-all | bytes 589824 | tf_op jit(solution)/shard_map/all_to_all | solution.py:416
  22.0 1.3 %sum_and_update.1.refs_0_ = f32[64,512]{1,0:T(8,128)S(1)} custom-call(bf16[64,192]{1,0:T(8,128)(2,1)S(1)} %copy-done.2, f32[32,2,1152]{2,1,0:T(2,128)S(1)} %all_to_all.5.got_ref, f32[64,8192]{1,0:T(8,128)} %params_ref.1), custom_call_target="tpu_custom_call" | custom-call | tf_op jit(solution)/shard_map/sum_and_update/pallas_call | solution.py:318
  23.3 0.1 collective-permute-start.5
  23.4 0.9 %collective-permute-start = (f32[64,512]{1,0:T(8,128)S(1)}, f32[64,512]{1,0:T(8,128)S(1)}, u32[]{:S(2)}, u32[]{:S(2)}) collective-permute-start(f32[64,512]{1,0:T(8,128)S(1)} %sum_and_update.1.refs_0_), channel_id=1, source_target_pairs={{0,2},{1,3},{2,0},{3,1},{4,6},{5,7},{6,4},{7,5},{8,10},{9,11},{10,... | collective-permute-start | bytes 393224 | tf_op jit(solution)/shard_map/ppermute | solution.py:341
  24.3 0.5 %collective-permute-start.3 = (f32[64,512]{1,0:T(8,128)S(1)}, f32[64,512]{1,0:T(8,128)S(1)}, u32[]{:S(2)}, u32[]{:S(2)}) collective-permute-start(f32[64,512]{1,0:T(8,128)S(1)} %sum_and_update.1.refs_0_), channel_id=1, source_target_pairs={{0,17},{1,16},{2,19},{3,18},{4,21},{5,20},{6,23},{7,22},{8,25},{9,... | collective-permute-start | bytes 393224 | tf_op jit(solution)/shard_map/ppermute | solution.py:341
  24.9 1.1 %collective-permute-start.7 = (f32[64,512]{1,0:T(8,128)S(1)}, f32[64,512]{1,0:T(8,128)S(1)}, u32[]{:S(2)}, u32[]{:S(2)}) collective-permute-start(f32[64,512]{1,0:T(8,128)S(1)} %sum_and_update.1.refs_0_), channel_id=1, source_target_pairs={{0,16},{1,17},{2,18},{3,19},{4,20},{5,21},{6,22},{7,23},{8,24},{9,... | collective-permute-start | bytes 393224 | tf_op jit(solution)/shard_map/ppermute | solution.py:341
  25.9 1.9 %collective-permute-start.6 = (f32[64,512]{1,0:T(8,128)S(1)}, f32[64,512]{1,0:T(8,128)S(1)}, u32[]{:S(2)}, u32[]{:S(2)}) collective-permute-start(f32[64,512]{1,0:T(8,128)S(1)} %sum_and_update.1.refs_0_), channel_id=1, source_target_pairs={{0,1},{1,0},{2,3},{3,2},{4,5},{5,4},{6,7},{7,6},{8,9},{9,8},{10,11... | collective-permute-start | bytes 393224 | tf_op jit(solution)/shard_map/ppermute | solution.py:341
  27.8 1.6 %residual.2.refs_0_ = f32[1,1,64,8192]{3,2,1,0:T(8,128)} custom-call(bf16[64,192]{1,0:T(8,128)(2,1)S(1)} %copy-done.2, s32[4,128]{1,0:T(4,128)S(1)} %bitcast.20, s32[1,128]{1,0:T(1,128)S(1)} %bitcast.23, f32[32,2,1152]{2,1,0:T(2,128)S(1)} %pick_rows.1.refs_3_.refs_4_, f32[1,1,64,8192]{3,2,1,0:T(8,128)S(1)} %copy-done, f32[1,1,64,8192]{3,2,1,0:T(8,128)S(1)} %copy-done.1), custom_call_target="tpu_custom_call" | custom-call | flops 402653184 | bytes 6291456 | tf_op jit(solution)/shard_map/residual/pallas_call | solution.py:295
  29.4 0.6 %collective-permute-start.2 = (f32[64,512]{1,0:T(8,128)S(1)}, f32[64,512]{1,0:T(8,128)S(1)}, u32[]{:S(2)}, u32[]{:S(2)}) collective-permute-start(f32[64,512]{1,0:T(8,128)S(1)} %collective-permute-done.refs_1_), channel_id=1, source_target_pairs={{0,16},{1,17},{2,18},{3,19},{4,20},{5,21},{6,22},{7,23},{8,24},{9,... | collective-permute-start | bytes 393224 | tf_op jit(solution)/shard_map/ppermute | solution.py:341
  30.1 0.7 %collective-permute-start.1 = (f32[64,512]{1,0:T(8,128)S(1)}, f32[64,512]{1,0:T(8,128)S(1)}, u32[]{:S(2)}, u32[]{:S(2)}) collective-permute-start(f32[64,512]{1,0:T(8,128)S(1)} %collective-permute-done.refs_1_), channel_id=1, source_target_pairs={{0,1},{1,0},{2,3},{3,2},{4,5},{5,4},{6,7},{7,6},{8,9},{9,8},{10,11... | collective-permute-start | bytes 393224 | tf_op jit(solution)/shard_map/ppermute | solution.py:341
  30.8 0.8 %collective-permute-done.3.refs_2_ = f32[64,512]{1,0:T(8,128)S(1)} collective-permute-done((f32[64,512]{1,0:T(8,128)S(1)}, f32[64,512]{1,0:T(8,128)S(1)}, u32[]{:S(2)}, u32[]{:S(2)}) %collective-permute-start.3) | collective-permute-done | bytes 131104 | tf_op jit(solution)/shard_map/ppermute | solution.py:341
  31.6 1.1 %collective-permute-start.4 = (f32[64,512]{1,0:T(8,128)S(1)}, f32[64,512]{1,0:T(8,128)S(1)}, u32[]{:S(2)}, u32[]{:S(2)}) collective-permute-start(f32[64,512]{1,0:T(8,128)S(1)} %collective-permute-done.3.refs_2_), channel_id=1, source_target_pairs={{0,2},{1,3},{2,0},{3,1},{4,6},{5,7},{6,4},{7,5},{8,10},{9,11},{10,... | collective-permute-start | bytes 393224 | tf_op jit(solution)/shard_map/ppermute | solution.py:341
  32.8 1.6 %residual.3 = f32[1,1,64,8192]{3,2,1,0:T(8,128)} custom-call(f32[1,1,64,8192]{3,2,1,0:T(8,128)} %residual.2.refs_0_, bf16[64,192]{1,0:T(8,128)(2,1)S(1)} %copy-done.2, s32[4,128]{1,0:T(4,128)S(1)} %bitcast.21, s32[1,128]{1,0:T(1,128)S(1)} %bitcast.24, f32[32,2,1152]{2,1,0:T(2,128)S(1)} %pick_rows.1.refs_3_.refs_4_, ...), custom_call_target="tpu_custom_call", output_to_operand_aliasing={{}: (0, {})} | custom-call | flops 402653184 | bytes 6291456 | tf_op jit(solution)/shard_map/residual/pallas_call | solution.py:295
  34.4 0.1 collective-permute-start.8
  34.5 0.6 %collective-permute-start.9 = (f32[2,64,512]{2,1,0:T(8,128)S(1)}, f32[2,64,512]{2,1,0:T(8,128)S(1)}, u32[]{:S(2)}, u32[]{:S(2)}) collective-permute-start(f32[2,64,512]{2,1,0:T(8,128)S(1)} %pad_maximum_fusion.1), channel_id=1, source_target_pairs={{0,8},{1,9},{2,10},{3,11},{4,12},{5,13},{6,14},{7,15},{8,0},{9,1},... | collective-permute-start | bytes 786440 | tf_op jit(solution)/shard_map/ppermute | solution.py:341
  35.1 0.9 %place_columns.3.refs_0_ = f32[64,8192]{1,0:T(8,128)} custom-call(f32[64,512]{1,0:T(8,128)S(1)} %sum_and_update.1.refs_0_, f32[64,512]{1,0:T(8,128)S(1)} %collective-permute-done.refs_1_, f32[64,512]{1,0:T(8,128)S(1)} %collective-permute-done.3.refs_2_, f32[64,512]{1,0:T(8,128)S(1)} %collective-permute-done.6.refs_3_, ...), custom_call_target="tpu_custom_call" | custom-call | tf_op jit(solution)/shard_map/place_columns/pallas_call | solution.py:393
  36.0 0.6 %collective-permute-done.4.refs_3_ = f32[64,512]{1,0:T(8,128)S(1)} collective-permute-done((f32[64,512]{1,0:T(8,128)S(1)}, f32[64,512]{1,0:T(8,128)S(1)}, u32[]{:S(2)}, u32[]{:S(2)}) %collective-permute-start.4) | collective-permute-done | bytes 131104 | tf_op jit(solution)/shard_map/ppermute | solution.py:341
  36.6 0.1 collective-permute-start.10
  36.7 0.5 %collective-permute-start.11 = (f32[64,512]{1,0:T(8,128)S(1)}, f32[64,512]{1,0:T(8,128)S(1)}, u32[]{:S(2)}, u32[]{:S(2)}) collective-permute-start(f32[64,512]{1,0:T(8,128)S(1)} %collective-permute-done.4.refs_3_), channel_id=1, source_target_pairs={{0,8},{1,9},{2,10},{3,11},{4,12},{5,13},{6,14},{7,15},{8,0},{9,1},... | collective-permute-start | bytes 393224 | tf_op jit(solution)/shard_map/ppermute | solution.py:341
  37.2 1.0 %place_columns.4.refs_0_ = f32[64,8192]{1,0:T(8,128)} custom-call(f32[64,8192]{1,0:T(8,128)} %place_columns.3.refs_0_, f32[64,512]{1,0:T(8,128)S(1)} %collective-permute-done.1.refs_1_, f32[64,512]{1,0:T(8,128)S(1)} %collective-permute-done.2.refs_2_, f32[64,512]{1,0:T(8,128)S(1)} %collective-permute-done.4.refs_3_, ...), custom_call_target="tpu_custom_call", output_to_operand_aliasing={{}: (0, {})} | custom-call | tf_op jit(solution)/shard_map/place_columns/pallas_call | solution.py:393
  38.2 0.2 collective-permute-done.11.refs_2_
  38.4 0.8 %place_columns.5 = f32[64,8192]{1,0:T(8,128)} custom-call(f32[64,8192]{1,0:T(8,128)} %place_columns.4.refs_0_, f32[2,64,512]{2,1,0:T(8,128)S(1)} %collective-permute-done.10.refs_1_, f32[64,512]{1,0:T(8,128)S(1)} %collective-permute-done.11.refs_2_), custom_call_target="tpu_custom_call", output_to_operand_aliasing={{}: (0, {})} | custom-call | tf_op jit(solution)/shard_map/place_columns/pallas_call | solution.py:393
  (21 shorter events, 0.1 us)
Async XLA Ops:
  0.6 21.4 %copy-start.2 = (bf16[64,192]{1,0:T(8,128)(2,1)S(1)}, bf16[64,192]{1,0:T(8,128)(2,1)}, u32[]{:S(2)}) copy-start(bf16[64,192]{1,0:T(8,128)(2,1)} %constant.5.clone.back_ref.refs_0_.refs_1_) | copy-start | bytes 73732
  0.6 27.2 %copy-start.1 = (f32[1,1,64,8192]{3,2,1,0:T(8,128)S(1)}, f32[1,1,64,8192]{3,2,1,0:T(8,128)}, u32[]{:S(2)}) copy-start(f32[1,1,64,8192]{3,2,1,0:T(8,128)} %refs_6_.1) | copy-start | bytes 6291460
  3.4 24.4 %copy-start = (f32[1,1,64,8192]{3,2,1,0:T(8,128)S(1)}, f32[1,1,64,8192]{3,2,1,0:T(8,128)}, u32[]{:S(2)}) copy-start(f32[1,1,64,8192]{3,2,1,0:T(8,128)} %refs_5_.5) | copy-start | bytes 6291460
  3.4 24.4 %copy-start.3 = (s32[1,1,128,4]{2,3,1,0:T(4,128)S(1)}, s32[1,1,128,4]{2,3,1,0:T(4,128)}, u32[]{:S(2)}) copy-start(s32[1,1,128,4]{2,3,1,0:T(4,128)} %param.11) | copy-start | bytes 6148
  3.4 24.4 %copy-start.4 = (s32[1,1,128]{2,1,0:T(1,128)S(1)}, s32[1,1,128]{2,1,0:T(1,128)}, u32[]{:S(2)}) copy-start(s32[1,1,128]{2,1,0:T(1,128)} %param.12) | copy-start | bytes 1540
  23.3 1.5 %collective-permute-start.5 = (f32[64,512]{1,0:T(8,128)S(1)}, f32[64,512]{1,0:T(8,128)S(1)}, u32[]{:S(2)}, u32[]{:S(2)}) collective-permute-start(f32[64,512]{1,0:T(8,128)S(1)} %sum_and_update.1.refs_0_), channel_id=1, source_target_pairs={{0,8},{1,9},{2,10},{3,11},{4,12},{5,13},{6,14},{7,15},{8,0},{9,1},... | collective-permute-start | bytes 393224 | tf_op jit(solution)/shard_map/ppermute | solution.py:341
  23.4 6.0 %collective-permute-start = (f32[64,512]{1,0:T(8,128)S(1)}, f32[64,512]{1,0:T(8,128)S(1)}, u32[]{:S(2)}, u32[]{:S(2)}) collective-permute-start(f32[64,512]{1,0:T(8,128)S(1)} %sum_and_update.1.refs_0_), channel_id=1, source_target_pairs={{0,2},{1,3},{2,0},{3,1},{4,6},{5,7},{6,4},{7,5},{8,10},{9,11},{10,... | collective-permute-start | bytes 393224 | tf_op jit(solution)/shard_map/ppermute | solution.py:341
  24.3 7.3 %collective-permute-start.3 = (f32[64,512]{1,0:T(8,128)S(1)}, f32[64,512]{1,0:T(8,128)S(1)}, u32[]{:S(2)}, u32[]{:S(2)}) collective-permute-start(f32[64,512]{1,0:T(8,128)S(1)} %sum_and_update.1.refs_0_), channel_id=1, source_target_pairs={{0,17},{1,16},{2,19},{3,18},{4,21},{5,20},{6,23},{7,22},{8,25},{9,... | collective-permute-start | bytes 393224 | tf_op jit(solution)/shard_map/ppermute | solution.py:341
  24.9 9.5 %collective-permute-start.7 = (f32[64,512]{1,0:T(8,128)S(1)}, f32[64,512]{1,0:T(8,128)S(1)}, u32[]{:S(2)}, u32[]{:S(2)}) collective-permute-start(f32[64,512]{1,0:T(8,128)S(1)} %sum_and_update.1.refs_0_), channel_id=1, source_target_pairs={{0,16},{1,17},{2,18},{3,19},{4,20},{5,21},{6,22},{7,23},{8,24},{9,... | collective-permute-start | bytes 393224 | tf_op jit(solution)/shard_map/ppermute | solution.py:341
  25.9 8.4 %collective-permute-start.6 = (f32[64,512]{1,0:T(8,128)S(1)}, f32[64,512]{1,0:T(8,128)S(1)}, u32[]{:S(2)}, u32[]{:S(2)}) collective-permute-start(f32[64,512]{1,0:T(8,128)S(1)} %sum_and_update.1.refs_0_), channel_id=1, source_target_pairs={{0,1},{1,0},{2,3},{3,2},{4,5},{5,4},{6,7},{7,6},{8,9},{9,8},{10,11... | collective-permute-start | bytes 393224 | tf_op jit(solution)/shard_map/ppermute | solution.py:341
  29.4 7.2 %collective-permute-start.2 = (f32[64,512]{1,0:T(8,128)S(1)}, f32[64,512]{1,0:T(8,128)S(1)}, u32[]{:S(2)}, u32[]{:S(2)}) collective-permute-start(f32[64,512]{1,0:T(8,128)S(1)} %collective-permute-done.refs_1_), channel_id=1, source_target_pairs={{0,16},{1,17},{2,18},{3,19},{4,20},{5,21},{6,22},{7,23},{8,24},{9,... | collective-permute-start | bytes 393224 | tf_op jit(solution)/shard_map/ppermute | solution.py:341
  30.1 6.5 %collective-permute-start.1 = (f32[64,512]{1,0:T(8,128)S(1)}, f32[64,512]{1,0:T(8,128)S(1)}, u32[]{:S(2)}, u32[]{:S(2)}) collective-permute-start(f32[64,512]{1,0:T(8,128)S(1)} %collective-permute-done.refs_1_), channel_id=1, source_target_pairs={{0,1},{1,0},{2,3},{3,2},{4,5},{5,4},{6,7},{7,6},{8,9},{9,8},{10,11... | collective-permute-start | bytes 393224 | tf_op jit(solution)/shard_map/ppermute | solution.py:341
  31.6 5.0 %collective-permute-start.4 = (f32[64,512]{1,0:T(8,128)S(1)}, f32[64,512]{1,0:T(8,128)S(1)}, u32[]{:S(2)}, u32[]{:S(2)}) collective-permute-start(f32[64,512]{1,0:T(8,128)S(1)} %collective-permute-done.3.refs_2_), channel_id=1, source_target_pairs={{0,2},{1,3},{2,0},{3,1},{4,6},{5,7},{6,4},{7,5},{8,10},{9,11},{10,... | collective-permute-start | bytes 393224 | tf_op jit(solution)/shard_map/ppermute | solution.py:341
  34.4 2.8 %collective-permute-start.8 = (f32[2,64,512]{2,1,0:T(8,128)S(1)}, f32[2,64,512]{2,1,0:T(8,128)S(1)}, u32[]{:S(2)}, u32[]{:S(2)}) collective-permute-start(f32[2,64,512]{2,1,0:T(8,128)S(1)} %pad_maximum_fusion), channel_id=1, source_target_pairs={{0,8},{1,9},{2,10},{3,11},{4,12},{5,13},{6,14},{7,15},{8,0},{9,1},... | collective-permute-start | bytes 786440 | tf_op jit(solution)/shard_map/ppermute | solution.py:341
  34.5 2.7 %collective-permute-start.9 = (f32[2,64,512]{2,1,0:T(8,128)S(1)}, f32[2,64,512]{2,1,0:T(8,128)S(1)}, u32[]{:S(2)}, u32[]{:S(2)}) collective-permute-start(f32[2,64,512]{2,1,0:T(8,128)S(1)} %pad_maximum_fusion.1), channel_id=1, source_target_pairs={{0,8},{1,9},{2,10},{3,11},{4,12},{5,13},{6,14},{7,15},{8,0},{9,1},... | collective-permute-start | bytes 786440 | tf_op jit(solution)/shard_map/ppermute | solution.py:341
  36.6 1.8 %collective-permute-start.10 = (f32[2,64,512]{2,1,0:T(8,128)S(1)}, f32[2,64,512]{2,1,0:T(8,128)S(1)}, u32[]{:S(2)}, u32[]{:S(2)}) collective-permute-start(f32[2,64,512]{2,1,0:T(8,128)S(1)} %pad_maximum_fusion.2), channel_id=1, source_target_pairs={{0,8},{1,9},{2,10},{3,11},{4,12},{5,13},{6,14},{7,15},{8,0},{9,1},... | collective-permute-start | bytes 786440 | tf_op jit(solution)/shard_map/ppermute | solution.py:341
  36.7 1.7 %collective-permute-start.11 = (f32[64,512]{1,0:T(8,128)S(1)}, f32[64,512]{1,0:T(8,128)S(1)}, u32[]{:S(2)}, u32[]{:S(2)}) collective-permute-start(f32[64,512]{1,0:T(8,128)S(1)} %collective-permute-done.4.refs_3_), channel_id=1, source_target_pairs={{0,8},{1,9},{2,10},{3,11},{4,12},{5,13},{6,14},{7,15},{8,0},{9,1},... | collective-permute-start | bytes 393224 | tf_op jit(solution)/shard_map/ppermute | solution.py:341
